TPU v7x, 32 devices: a whole 2x2x4 slice. The times are simulated.
32 devices in a mesh: dp: 8 (over z, y), vocab: 4 (over x, core).
Axes of the slice: x: 2, y: 2, z: 4, core: 2. Of those that a mesh axis runs over, the one named last changes fastest.
Arguments:
- source_ids: int32 [64, 128], P('dp'), may hold values from 0 to 25599
- target_in: int32 [64, 128], P('dp'), may hold values from 0 to 25599
- target_ids: int32 [64, 128], P('dp'), may hold values from 0 to 25599
- source_length: int32 [64], P('dp'), may hold values from 16 to 128, as said below
- target_length: int32 [64], P('dp'), may hold values from 16 to 128, as said below
- task_ids: int32 [64], P('dp'), may hold values from 0 to 3, as said below
- vocab_table: bfloat16 [25600, 1024], P('vocab')
- positions: bfloat16 [2, 128, 1024], replicated, may hold values from -0.29882812 to 0.29882812
- attention_in: bfloat16 [3, 1024, 3072], P(None, ('dp', 'vocab')), may hold values from -0.1875 to 0.1875
- attention_out: bfloat16 [3, 1024, 1024], P(None, ('dp', 'vocab')), may hold values from -0.375 to 0.375
- widen_weight: bfloat16 [2, 1024, 4096], P(None, ('dp', 'vocab')), may hold values from -0.1875 to 0.1875
- narrow_weight: bfloat16 [2, 4096, 1024], P(None, ('dp', 'vocab')), may hold values from -0.09375 to 0.09375
- adapt_down: float32 [2, 1024, 512], P(None, ('dp', 'vocab')), may hold values from -0.1875 to 0.1875
- adapt_up: float32 [2, 512, 1024], P(None, ('dp', 'vocab')), may hold values from -0.0625 to 0.0625
- norm_params: float32 [14, 1024], P(None, ('dp', 'vocab'))
- down_first: float32 [2, 1024, 512], P(None, ('dp', 'vocab')), may hold values from -2.3841858e-06 to 2.3841858e-06
- down_second: float32 [2, 1024, 512], P(None, ('dp', 'vocab')), may hold values from 1.8943987e-15 to 7.577595e-15
- up_first: float32 [2, 512, 1024], P(None, ('dp', 'vocab')), may hold values from -2.3841858e-06 to 2.3841858e-06
- up_second: float32 [2, 512, 1024], P(None, ('dp', 'vocab')), may hold values from 1.8943987e-15 to 7.577595e-15
- norm_first: float32 [14, 1024], P(None, ('dp', 'vocab')), may hold values from -4.7683716e-06 to 4.7683716e-06
- norm_second: float32 [14, 1024], P(None, ('dp', 'vocab')), may hold values from 7.577595e-15 to 3.031038e-14
Outputs:
- new_down_first: float32 [2, 1024, 512], P(None, ('dp', 'vocab'))
- new_down_second: float32 [2, 1024, 512], P(None, ('dp', 'vocab'))
- new_adapt_down: float32 [2, 1024, 512], P(None, ('dp', 'vocab'))
- new_up_first: float32 [2, 512, 1024], P(None, ('dp', 'vocab'))
- new_up_second: float32 [2, 512, 1024], P(None, ('dp', 'vocab'))
- new_adapt_up: float32 [2, 512, 1024], P(None, ('dp', 'vocab'))
- new_norm_first: float32 [14, 1024], P(None, ('dp', 'vocab'))
- new_norm_second: float32 [14, 1024], P(None, ('dp', 'vocab'))
- new_norm_params: float32 [14, 1024], P(None, ('dp', 'vocab'))
- clip_norm: float32 [], replicated
- task_sums: float32 [4], replicated
- task_counts: float32 [4], replicated
Inputs may be any that keep to these rules, and one draw needn't show every extreme that they name: `source_length`: at least 16; some pair has exactly 128. `target_length`: at least 16; some pair has exactly 128. `task_ids`: every task occurs in some pair.
All inputs are finite; a program needn't handle non-finite values.
Results may differ from a plain program's by a relative error of at most 0.006.
Values may be sent and summed in bfloat16 or wider, within the bound.
A program may use at most 384 MiB of HBM per device.

v0:
```python
import jax
import jax.numpy as jnp
from jax import lax
from jax.sharding import PartitionSpec as P

HEADS = 16
ADAPT = 512
LEN = 128
MICRO = 2
TASKS = 4
STEP = 10


NEGATIVE = -1000000000.0
NORM_EPS = 1e-05
BRANCH_SCALE = 4.0
CLIP_LIMIT = 0.002
BETA_FIRST = 0.9
BETA_SECOND = 0.999
ADAM_EPSILON = 1e-08
WEIGHT_DECAY = 0.01
RATE_ADAPTER = 0.02
RATE_NORMS = 0.2


def as_low(value):
    return value.astype(jnp.bfloat16)


def times_weight(left, right):
    return jnp.dot(left, right, preferred_element_type=jnp.float32)


def times_transpose(left, right):
    return lax.dot_general(
        left, right, (((1,), (1,)), ((), ())), preferred_element_type=jnp.float32
    )


def outer_sum(left, right):
    return lax.dot_general(
        left, right, (((0,), (0,)), ((), ())), preferred_element_type=jnp.float32
    )


def gelu_value(value):
    return jax.nn.gelu(value, approximate=False)


def gelu_slope(value):
    return (
        0.5 * (1.0 + lax.erf(value * 0.7071067811865476))
        + value * jnp.exp(-0.5 * value * value) * 0.3989422804014327
    )


def norm_forward(value, norm_gain, norm_bias):
    centred = value - jnp.mean(value, -1, keepdims=True)
    inv_std = lax.rsqrt(jnp.mean(centred * centred, -1, keepdims=True) + NORM_EPS)
    normed = centred * inv_std
    return (normed * norm_gain + norm_bias, (normed, inv_std))


def norm_backward(grad_out, kept, norm_gain):
    normed, inv_std = kept
    scaled = grad_out * norm_gain
    grad_in = inv_std * (
        scaled
        - jnp.mean(scaled, -1, keepdims=True)
        - normed * jnp.mean(scaled * normed, -1, keepdims=True)
    )
    return (grad_in, jnp.sum(grad_out * normed, 0), jnp.sum(grad_out, 0))


def split_heads(value):
    return value.reshape(value.shape[0], HEADS, -1)


def head_scores(queries, key_rows, key_mask):
    scale = (queries.shape[1] // HEADS) ** (-0.5)
    scores = (
        jnp.einsum(
            "qhd,khd->hqk",
            split_heads(queries),
            split_heads(key_rows),
            preferred_element_type=jnp.float32,
        )
        * scale
    )
    return (jnp.where(key_mask[None], scores, NEGATIVE), scale)


def attend_forward(queries, key_rows, values, key_mask):
    scores, scale = head_scores(queries, key_rows, key_mask)
    top = jnp.max(scores, -1, keepdims=True)
    log_total = top + jnp.log(jnp.sum(jnp.exp(scores - top), -1, keepdims=True))
    probs = as_low(jnp.exp(scores - log_total))
    output = jnp.einsum(
        "hqk,khd->qhd", probs, split_heads(values), preferred_element_type=jnp.float32
    )
    return (output.reshape(queries.shape[0], -1), log_total)


def attend_backward(grad_low, queries, key_rows, values, key_mask, log_total):
    scores, scale = head_scores(queries, key_rows, key_mask)
    probs = jnp.exp(scores - log_total)
    grad_heads = split_heads(grad_low)
    grad_probs = jnp.einsum(
        "qhd,khd->hqk", grad_heads, split_heads(values), preferred_element_type=jnp.float32
    )
    grad_values = jnp.einsum(
        "hqk,qhd->khd", as_low(probs), grad_heads, preferred_element_type=jnp.float32
    )
    grad_scores = as_low(probs * (grad_probs - jnp.sum(probs * grad_probs, -1, keepdims=True)))
    grad_queries = (
        jnp.einsum(
            "hqk,khd->qhd", grad_scores, split_heads(key_rows), preferred_element_type=jnp.float32
        )
        * scale
    )
    grad_keys = (
        jnp.einsum(
            "hqk,qhd->khd", grad_scores, split_heads(queries), preferred_element_type=jnp.float32
        )
        * scale
    )
    rows_q, rows_k = (queries.shape[0], key_rows.shape[0])
    return (
        grad_queries.reshape(rows_q, -1),
        grad_keys.reshape(rows_k, -1),
        grad_values.reshape(rows_k, -1),
    )


def attend_block(inputs, memory, w_in, w_out, norm_gain, norm_bias, key_mask):
    width = inputs.shape[1]
    low_in = as_low(inputs)
    if memory is None:
        packed = as_low(times_weight(low_in, w_in))
        queries, key_rows, values = (
            packed[:, :width],
            packed[:, width : 2 * width],
            packed[:, 2 * width :],
        )
    else:
        queries = as_low(times_weight(low_in, w_in[:, :width]))
        pair = as_low(times_weight(memory, w_in[:, width:]))
        key_rows, values = (pair[:, :width], pair[:, width:])
    attended, log_total = attend_forward(queries, key_rows, values, key_mask)
    low_att = as_low(attended)
    result, norm_kept = norm_forward(inputs + times_weight(low_att, w_out), norm_gain, norm_bias)
    return (result, (queries, key_rows, values, log_total, norm_kept))


def attend_block_back(grad_out, kept, cross, w_in, w_out, norm_gain, key_mask):
    queries, key_rows, values, log_total, norm_kept = kept
    width = queries.shape[1]
    grad_sum, grad_gain, grad_bias = norm_backward(grad_out, norm_kept, norm_gain)
    grad_att = as_low(times_transpose(as_low(grad_sum), w_out))
    grad_q, grad_k, grad_v = attend_backward(
        grad_att, queries, key_rows, values, key_mask, log_total
    )
    if cross:
        grad_in = grad_sum + times_transpose(as_low(grad_q), w_in[:, :width])
        grad_memory = times_transpose(as_low(jnp.concatenate([grad_k, grad_v], 1)), w_in[:, width:])
    else:
        grad_in = grad_sum + times_transpose(
            as_low(jnp.concatenate([grad_q, grad_k, grad_v], 1)), w_in
        )
        grad_memory = None
    return (grad_in, grad_memory, grad_gain, grad_bias)


def feed_block(inputs, widen, narrow, down_part, up_part, norm_gain, norm_bias):
    low_in = as_low(inputs)
    hidden = times_weight(low_in, widen)
    bottle = times_weight(low_in, down_part)
    low_hidden = as_low(gelu_value(hidden))
    low_bottle = as_low(gelu_value(bottle))
    branch = times_weight(low_hidden, narrow) + BRANCH_SCALE * times_weight(low_bottle, up_part)
    result, norm_kept = norm_forward(inputs + branch, norm_gain, norm_bias)
    return (result, (low_in, hidden, bottle, low_bottle, norm_kept))


def feed_block_back(grad_out, kept, widen, narrow, down_part, up_part, norm_gain):
    low_in, hidden, bottle, low_bottle, norm_kept = kept
    grad_sum, grad_gain, grad_bias = norm_backward(grad_out, norm_kept, norm_gain)
    low_grad = as_low(grad_sum)
    grad_hidden = as_low(times_transpose(low_grad, narrow) * gelu_slope(hidden))
    grad_bottle = as_low(BRANCH_SCALE * times_transpose(low_grad, up_part) * gelu_slope(bottle))
    grad_in = (
        grad_sum + times_transpose(grad_hidden, widen) + times_transpose(grad_bottle, down_part)
    )
    grad_up = BRANCH_SCALE * outer_sum(low_bottle, low_grad)
    grad_down = outer_sum(low_in, grad_bottle)
    return (grad_in, grad_down, grad_up, grad_gain, grad_bias)


def layer_forward(inputs, memory, weights, norms, layer, self_mask, cross_mask):
    attention_in, attention_out, widen, narrow, down_all, up_all = weights
    base = 1 + 3 * layer
    final = base + 1 + layer
    hidden, kept_self = attend_block(
        inputs,
        None,
        attention_in[layer],
        attention_out[layer],
        norms[base],
        norms[base + 7],
        self_mask,
    )
    kept_cross = None
    if memory is not None:
        hidden, kept_cross = attend_block(
            hidden, memory, attention_in[2], attention_out[2], norms[5], norms[12], cross_mask
        )
    result, kept_feed = feed_block(
        hidden,
        widen[layer],
        narrow[layer],
        down_all[layer],
        up_all[layer],
        norms[final],
        norms[final + 7],
    )
    return (result, (kept_self, kept_cross, kept_feed))


def layer_backward(grad_out, kept, weights, norms, layer, self_mask, cross_mask, norm_grads):
    attention_in, attention_out, widen, narrow, down_all, up_all = weights
    kept_self, kept_cross, kept_feed = kept
    base = 1 + 3 * layer
    final = base + 1 + layer
    grad_hidden, grad_down, grad_up, grad_gain, grad_bias = feed_block_back(
        grad_out,
        kept_feed,
        widen[layer],
        narrow[layer],
        down_all[layer],
        up_all[layer],
        norms[final],
    )
    norm_grads = norm_grads.at[final].add(grad_gain).at[final + 7].add(grad_bias)
    grad_memory = None
    if kept_cross is not None:
        grad_hidden, grad_memory, grad_gain, grad_bias = attend_block_back(
            grad_hidden, kept_cross, True, attention_in[2], attention_out[2], norms[5], cross_mask
        )
        norm_grads = norm_grads.at[5].add(grad_gain).at[12].add(grad_bias)
    grad_in, _, grad_gain, grad_bias = attend_block_back(
        grad_hidden,
        kept_self,
        False,
        attention_in[layer],
        attention_out[layer],
        norms[base],
        self_mask,
    )
    norm_grads = norm_grads.at[base].add(grad_gain).at[base + 7].add(grad_bias)
    return (grad_in, grad_memory, grad_down, grad_up, norm_grads)


def adam_step(weight, first, second, grad, rate):
    first = BETA_FIRST * first + (1.0 - BETA_FIRST) * grad
    second = BETA_SECOND * second + (1.0 - BETA_SECOND) * grad * grad
    first_hat = first / (1.0 - BETA_FIRST**STEP)
    second_hat = second / (1.0 - BETA_SECOND**STEP)
    weight = weight - rate * (
        first_hat / (jnp.sqrt(second_hat) + ADAM_EPSILON) + WEIGHT_DECAY * weight
    )
    return (first, second, weight)


def local(
    source_ids,
    target_in,
    target_ids,
    source_length,
    target_length,
    task_ids,
    vocab_table,
    positions,
    attention_in,
    attention_out,
    widen_weight,
    narrow_weight,
    adapt_down,
    adapt_up,
    norm_params,
    down_first,
    down_second,
    up_first,
    up_second,
    norm_first,
    norm_second,
):
    groups = lax.axis_size("vocab")
    vocab_rank = lax.axis_index("vocab")
    rows_local = vocab_table.shape[0]
    width = vocab_table.shape[1]
    norms = lax.all_gather(norm_params, ("dp", "vocab"), axis=1, tiled=True)
    joined_ids = (
        jnp.stack([source_ids.reshape(groups, -1), target_in.reshape(groups, -1)], 1).reshape(-1)
        - vocab_rank * rows_local
    )
    inside = (joined_ids >= 0) & (joined_ids < rows_local)
    picked = jnp.where(
        inside[:, None],
        jnp.take(vocab_table, jnp.clip(joined_ids, 0, rows_local - 1), axis=0),
        jnp.zeros((), jnp.bfloat16),
    )
    embedded = lax.psum_scatter(
        picked.astype(jnp.float32).astype(jnp.bfloat16), "vocab", scatter_dimension=0, tiled=True
    ).astype(jnp.float32)
    task_hot = (task_ids[:, None] == jnp.arange(TASKS)[None, :]).astype(jnp.float32)
    task_counts = lax.psum(jnp.sum(task_hot * target_length[:, None].astype(jnp.float32), 0), "dp")
    seq_scale = jnp.sum(task_hot * (1.0 / (TASKS * task_counts))[None, :], 1).reshape(groups, MICRO)
    group_lengths = target_length.reshape(groups, MICRO)
    group_targets = target_ids.reshape(groups, MICRO, LEN)
    positions_wide = positions.astype(jnp.float32)
    key_index = jnp.arange(LEN)
    causal = key_index[:, None] >= key_index[None, :]
    frozen_parts = (
        attention_in,
        attention_out,
        widen_weight,
        narrow_weight,
        as_low(adapt_down),
        as_low(adapt_up),
    )
    weights = (
        lax.all_gather(frozen_parts[0], ("dp", "vocab"), axis=1, tiled=True),
        lax.all_gather(frozen_parts[1], ("dp", "vocab"), axis=1, tiled=True),
        lax.all_gather(frozen_parts[2], ("dp", "vocab"), axis=1, tiled=True),
        lax.all_gather(frozen_parts[3], ("dp", "vocab"), axis=1, tiled=True),
        lax.all_gather(frozen_parts[4], ("dp", "vocab"), axis=1, tiled=True),
        lax.all_gather(frozen_parts[5], ("dp", "vocab"), axis=1, tiled=True),
    )
    grad_down = jnp.zeros((2, width, ADAPT), jnp.float32)
    grad_up = jnp.zeros((2, ADAPT, width), jnp.float32)
    norm_grads = jnp.zeros((14, width), jnp.float32)
    task_local = jnp.zeros((TASKS,), jnp.float32)
    for step in range(MICRO):
        own = vocab_rank * MICRO + step
        source_count = lax.dynamic_index_in_dim(source_length, own, keepdims=False)
        cross_mask = jnp.broadcast_to(key_index[None, :] < source_count, (LEN, LEN))
        source_rows = embedded[step * LEN : (step + 1) * LEN] + positions_wide[0]
        enc_input, kept_enc_norm = norm_forward(source_rows, norms[0], norms[7])
        encoded, kept_enc = layer_forward(
            enc_input, None, weights, norms, 0, cross_mask, cross_mask
        )
        memory = as_low(encoded)
        target_rows = embedded[(MICRO + step) * LEN : (MICRO + step + 1) * LEN] + positions_wide[1]
        dec_input, kept_dec_norm = norm_forward(target_rows, norms[3], norms[10])
        decoded, kept_dec = layer_forward(dec_input, memory, weights, norms, 1, causal, cross_mask)
        head_rows = lax.all_gather(as_low(decoded), "vocab", axis=0, tiled=True)
        logits = times_transpose(head_rows, vocab_table)
        local_target = group_targets[:, step].reshape(-1) - vocab_rank * rows_local
        target_hot = lax.broadcasted_iota(jnp.int32, logits.shape, 1) == local_target[:, None]
        target_logit = jnp.sum(jnp.where(target_hot, logits, 0.0), 1)
        local_max = jnp.max(logits, 1)
        row_max = lax.pmax(local_max, "vocab")
        row_total, row_target = lax.psum(
            (jnp.sum(jnp.exp(logits - row_max[:, None]), 1), target_logit), "vocab"
        )
        log_total = row_max + jnp.log(row_total)
        row_mask = (key_index[None, :] < group_lengths[:, step][:, None]).astype(jnp.float32)
        row_weight = (row_mask * seq_scale[:, step][:, None]).reshape(-1)
        row_loss = (log_total - row_target) * row_mask.reshape(-1)
        own_loss = lax.dynamic_slice_in_dim(row_loss, vocab_rank * LEN, LEN)
        task_local = task_local + lax.dynamic_index_in_dim(task_hot, own, keepdims=False) * jnp.sum(
            own_loss
        )
        grad_logits = as_low(
            row_weight[:, None]
            * (jnp.exp(logits - log_total[:, None]) - target_hot.astype(jnp.float32))
        )
        grad_decoded = lax.psum_scatter(
            times_weight(grad_logits, vocab_table).astype(jnp.bfloat16),
            "vocab",
            scatter_dimension=0,
            tiled=True,
        ).astype(jnp.float32)
        grad_dec_in, grad_memory, down_part, up_part, norm_grads = layer_backward(
            grad_decoded, kept_dec, weights, norms, 1, causal, cross_mask, norm_grads
        )
        grad_down = grad_down.at[1].add(down_part)
        grad_up = grad_up.at[1].add(up_part)
        _, grad_gain, grad_bias = norm_backward(grad_dec_in, kept_dec_norm, norms[3])
        norm_grads = norm_grads.at[3].add(grad_gain).at[10].add(grad_bias)
        grad_enc_in, _, down_part, up_part, norm_grads = layer_backward(
            grad_memory, kept_enc, weights, norms, 0, cross_mask, cross_mask, norm_grads
        )
        grad_down = grad_down.at[0].add(down_part)
        grad_up = grad_up.at[0].add(up_part)
        _, grad_gain, grad_bias = norm_backward(grad_enc_in, kept_enc_norm, norms[0])
        norm_grads = norm_grads.at[0].add(grad_gain).at[7].add(grad_bias)
    full_down, full_up, full_norm, task_sums = lax.psum(
        (grad_down, grad_up, norm_grads, task_local), ("dp", "vocab")
    )
    square_total = (
        jnp.sum(full_down * full_down) + jnp.sum(full_up * full_up) + jnp.sum(full_norm * full_norm)
    )
    member = lax.axis_index(("dp", "vocab"))
    cut = width // lax.axis_size(("dp", "vocab"))
    shard_down = lax.dynamic_slice_in_dim(full_down, member * cut, cut, 1)
    shard_up = lax.dynamic_slice_in_dim(
        full_up,
        member * (ADAPT // lax.axis_size(("dp", "vocab"))),
        ADAPT // lax.axis_size(("dp", "vocab")),
        1,
    )
    shard_norm = lax.dynamic_slice_in_dim(full_norm, member * cut, cut, 1)
    grad_norm = jnp.sqrt(square_total)
    factor = CLIP_LIMIT / jnp.maximum(grad_norm, CLIP_LIMIT)
    down_new = adam_step(adapt_down, down_first, down_second, shard_down * factor, RATE_ADAPTER)
    up_new = adam_step(adapt_up, up_first, up_second, shard_up * factor, RATE_ADAPTER)
    norm_new = adam_step(norm_params, norm_first, norm_second, shard_norm * factor, RATE_NORMS)
    return (
        down_new[0],
        down_new[1],
        down_new[2],
        up_new[0],
        up_new[1],
        up_new[2],
        norm_new[0],
        norm_new[1],
        norm_new[2],
        grad_norm,
        task_sums,
        task_counts,
    )


def solution(mesh):
    return jax.shard_map(
        local,
        mesh=mesh,
        in_specs=(
            P("dp", None),
            P("dp", None),
            P("dp", None),
            P("dp"),
            P("dp"),
            P("dp"),
            P("vocab", None),
            P(),
            P(None, ("dp", "vocab"), None),
            P(None, ("dp", "vocab"), None),
            P(None, ("dp", "vocab"), None),
            P(None, ("dp", "vocab"), None),
            P(None, ("dp", "vocab"), None),
            P(None, ("dp", "vocab"), None),
            P(None, ("dp", "vocab")),
            P(None, ("dp", "vocab"), None),
            P(None, ("dp", "vocab"), None),
            P(None, ("dp", "vocab"), None),
            P(None, ("dp", "vocab"), None),
            P(None, ("dp", "vocab")),
            P(None, ("dp", "vocab")),
        ),
        out_specs=(
            P(None, ("dp", "vocab"), None),
            P(None, ("dp", "vocab"), None),
            P(None, ("dp", "vocab"), None),
            P(None, ("dp", "vocab"), None),
            P(None, ("dp", "vocab"), None),
            P(None, ("dp", "vocab"), None),
            P(None, ("dp", "vocab")),
            P(None, ("dp", "vocab")),
            P(None, ("dp", "vocab")),
            P(),
            P(),
            P(),
        ),
        check_vma=False,
    )
```

profile of v0, /device:TPU:0, one launch (start us, length us, event | category | flops | bytes accessed | tf_op | source)
XLA Modules:
  0.0 1164.7 jit_solution(17696724758123723964)
XLA Ops:
  10.3 17.4 %gather_fusion = bf16[2048,1024]{1,0:T(8,128)(2,1)} fusion(bf16[6400,1024]{1,0:T(8,128)(2,1)} %param.99, s32[2048]{0:T(1024)S(1)} %broadcast_clamp_fusion), kind=kCustom, calls=%fused_computation | custom fusion | bytes 8396800 | tf_op jit(solution)/shard_map/jit(_take)/gather | solution.py:309
  27.7 3.9 select_select_fusion
  36.0 45.2 %all-gather = f32[32,32,14]{1,2,0:T(8,128)S(1)} all-gather(f32[1,32,14]{1,2,0:T(8,128)S(1)} %bitcast.594), channel_id=1, replica_groups=mesh['dp'=8,'vocab'=4] {'dp','vocab'}, dimensions={0}, use_global_device_ids=true | all-gather | bytes 59136 | tf_op jit(solution)/shard_map/all_gather | solution.py:301
  88.5 82.3 %all-gather.10.cloned.1.call-done = bf16[3,1024,3072]{2,1,0:T(8,128)(2,1)} async-done(((bf16[3,32,3072]{2,1,0:T(8,128)(2,1)}), bf16[3,1024,3072]{2,1,0:T(8,128)(2,1)}) %all-gather.10.cloned.1.call-update) | async-done | bytes 18874384 | tf_op jit(solution)/shard_map/all_gather | solution.py:332
  170.8 3.8 fusion.40
  181.8 59.2 %all-gather.12.cloned.1.call-done = bf16[3,1024,1024]{2,1,0:T(8,128)(2,1)} async-done(((bf16[3,32,1024]{2,1,0:T(8,128)(2,1)}), bf16[3,1024,1024]{2,1,0:T(8,128)(2,1)}) %all-gather.12.cloned.1.call-update) | async-done | bytes 6291472 | tf_op jit(solution)/shard_map/all_gather | solution.py:333
  250.7 4.0 fusion.42
  260.6 4.0 fusion.43
  271.7 28.1 %all-gather.18.cloned.1.call-done = bf16[2,1024,512]{2,1,0:T(8,128)(2,1)} async-done(((bf16[2,32,512]{2,1,0:T(8,128)(2,1)}), bf16[2,1024,512]{2,1,0:T(8,128)(2,1)}) %all-gather.18.cloned.1.call-update) | async-done | bytes 2097168 | tf_op jit(solution)/shard_map/all_gather | solution.py:336
  301.4 115.1 %all-gather.14.cloned.1.call-done = bf16[2,1024,4096]{2,1,0:T(8,128)(2,1)} async-done(((bf16[2,32,4096]{2,1,0:T(8,128)(2,1)}), bf16[2,1024,4096]{2,1,0:T(8,128)(2,1)}) %all-gather.14.cloned.1.call-update) | async-done | bytes 16777232 | tf_op jit(solution)/shard_map/all_gather | solution.py:334
  416.5 6.3 fusion.11
  422.8 109.5 %all-gather.16.cloned.1.call-done = bf16[2,4096,1024]{2,1,0:T(8,128)(2,1)} async-done(((bf16[2,128,1024]{2,1,0:T(8,128)(2,1)}), bf16[2,4096,1024]{2,1,0:T(8,128)(2,1)}) %all-gather.16.cloned.1.call-update) | async-done | bytes 16777232 | tf_op jit(solution)/shard_map/all_gather | solution.py:335
  532.3 8.1 fusion.15
  540.4 50.2 %all-gather.20.cloned.1.call-done = bf16[2,512,1024]{2,1,0:T(8,128)(2,1)} async-done(((bf16[2,16,1024]{2,1,0:T(8,128)(2,1)}), bf16[2,512,1024]{2,1,0:T(8,128)(2,1)}) %all-gather.20.cloned.1.call-update) | async-done | bytes 2097168 | tf_op jit(solution)/shard_map/all_gather | solution.py:337
  600.3 3.9 fusion.41
  612.3 4.8 fusion.10
  617.5 8.8 fusion.14
  633.6 4.9 fusion.19
  638.9 9.2 fusion.23
  651.6 8.4 fusion.21
  663.1 20.3 %psum.63 = f32[4]{0:T(128)S(1)} all-reduce(f32[4]{0:T(128)S(1)} %select_reduce_fusion.3), channel_id=1, replica_groups=mesh['dp'=8,'vocab'=4] {'dp'}, use_global_device_ids=true, to_apply=%region_22.23 | all-reduce | flops 4 | bytes 32 | tf_op jit(solution)/shard_map/psum | solution.py:316
  684.8 15.4 %fusion.724 = (f32[512]{0:T(512)S(1)}, f32[512,6400]{1,0:T(8,128)}) fusion(bf16[512,1024]{1,0:T(8,128)(2,1)} %all-gather.22.cloned.1.call-done, bf16[6400,1024]{1,0:T(8,128)(2,1)} %param.99), kind=kOutput, calls=%fused_computation.1059 | convolution fusion | flops 6714162688 | bytes 27265024 | tf_op jit(solution)/shard_map/dot_general | solution.py:35
  700.2 15.0 %fusion.725 = (f32[512]{0:T(512)S(1)}, f32[512,6400]{1,0:T(8,128)}) fusion(bf16[512,1024]{1,0:T(8,128)(2,1)} %all-gather.24.cloned.1.call-done, bf16[6400,1024]{1,0:T(8,128)(2,1)} %param.99), kind=kOutput, calls=%fused_computation.1060 | convolution fusion | flops 6714162688 | bytes 27265024 | tf_op jit(solution)/shard_map/dot_general | solution.py:35
  715.1 5.7 all-reduce.4
  720.9 7.5 select_reduce_fusion
  729.4 4.0 select_reduce_fusion.1
  733.4 6.0 all-reduce.3
  739.6 15.4 %fusion.116 = bf16[512,1024]{1,0:T(8,128)(2,1)} fusion(bf16[6400,1024]{1,0:T(8,128)(2,1)} %param.99, f32[512,6400]{1,0:T(8,128)} %get-tuple-element.631, s32[512]{0:T(512)S(1)} %bitcast.624, f32[512]{0:T(512)S(1)} %get-tuple-element.530, f32[512]{0:T(512)S(1)} %get-tuple-element.592), kind=kOutput, calls=%fused_computation.183 | convolution fusion | flops 6731071488 | bytes 27269120 | tf_op jit(solution)/shard_map/dot_general | solution.py:31
  755.1 15.8 %fusion.117 = bf16[512,1024]{1,0:T(8,128)(2,1)} fusion(bf16[6400,1024]{1,0:T(8,128)(2,1)} %param.99, f32[512,6400]{1,0:T(8,128)} %get-tuple-element.629, s32[512]{0:T(512)S(1)} %bitcast.622, f32[512]{0:T(512)S(1)} %get-tuple-element.528, f32[512]{0:T(512)S(1)} %get-tuple-element.593), kind=kOutput, calls=%fused_computation.184 | convolution fusion | flops 6731071488 | bytes 27269120 | tf_op jit(solution)/shard_map/dot_general | solution.py:31
  774.2 4.5 reduce-scatter.8.cloned.1.call-done
  778.7 27.2 %reduce-scatter.6.cloned.1.call-done = bf16[128,1024]{1,0:T(8,128)(2,1)} async-done(((bf16[512,1024]{1,0:T(8,128)(2,1)}), bf16[128,1024]{1,0:T(8,128)(2,1)}) %reduce-scatter.6.cloned.1.call-update) | async-done | bytes 262160 | tf_op jit(solution)/shard_map/reduce_scatter | solution.py:378
  810.0 10.9 fusion.165
  820.9 10.5 fusion.164
  844.4 3.2 fusion.191
  858.9 3.5 multiply_reduce_fusion.13
  863.2 3.2 fusion.193
  872.1 4.6 multiply_reduce_fusion.11
  876.8 3.3 multiply_reduce_fusion.19
  880.4 9.9 fusion.166
  892.1 12.7 %fusion.167 = f32[128,1024]{1,0:T(8,128)S(1)} fusion(f32[128,1024]{1,0:T(8,128)} %get-tuple-element.581, bf16[2,1024,4096]{2,1,0:T(8,128)(2,1)} %all-gather.14.cloned.1.call-done, bf16[2,4096,1024]{2,1,0:T(8,128)(2,1)} %all-gather.16.cloned.1.call-done, f32[128,4096]{1,0:T(8,128)} %copy-done.293), kind=kOutput, calls=%fused_computation.256 | convolution fusion | flops 2152988672 | bytes 20447232 | tf_op jit(solution)/shard_map/dot_general | solution.py:35
  935.2 5.7 fusion.692
  941.9 5.7 fusion.691
  960.7 3.4 fusion.87
  967.8 6.3 fusion.690
  977.8 5.3 fusion.689
  983.4 41.4 %all-reduce.1 = (f32[14,1024]{1,0:T(8,128)S(1)}, f32[4]{0:T(128)}) all-reduce(f32[14,1024]{1,0:T(8,128)S(1)} %scatter-add.169, f32[4]{0:T(128)S(1)} %copy-done.179), channel_id=1, replica_groups=mesh['dp'=8,'vocab'=4] {'dp','vocab'}, use_global_device_ids=true, to_apply=%region_112.113 | all-reduce | flops 14340 | bytes 114720 | tf_op jit(solution)/shard_map/psum | solution.py:398
  1025.3 118.9 %all-reduce.7.cloned.1.call-done = (f32[2,1024,512]{2,1,0:T(8,128)}, f32[2,512,1024]{2,1,0:T(8,128)}) async-done(((f32[2,1024,512]{2,1,0:T(8,128)}, f32[2,512,1024]{2,1,0:T(8,128)}), (f32[2,1024,512]{2,1,0:T(8,128)}, f32[2,512,1024]{2,1,0:T(8,128)})) %all-reduce.7.cloned.1.call-update) | async-done | bytes 8388624 | tf_op jit(solution)/shard_map/psum | solution.py:398
  1144.2 4.0 multiply_reduce_fusion
  (930 shorter events, 174.6 us)
Async XLA Ops:
  8.0 76.1 %reduce-scatter.4.cloned.1.call-start = ((), (), s32[]{:S(2)}) async-start(), calls=%async_computation.3 | async-start | bytes 5242880 | tf_op jit(solution)/shard_map/reduce_scatter | solution.py:312
  31.7 139.1 %all-gather.10.cloned.1.call-start = ((), (), s32[]{:S(2)}) async-start(), calls=%async_computation.4 | async-start | bytes 19464192 | tf_op jit(solution)/shard_map/all_gather | solution.py:332
  32.3 208.7 %all-gather.12.cloned.1.call-start = ((), (), s32[]{:S(2)}) async-start(), calls=%async_computation.5 | async-start | bytes 6488064 | tf_op jit(solution)/shard_map/all_gather | solution.py:333
  32.9 267.0 %all-gather.18.cloned.1.call-start = ((), (), s32[]{:S(2)}) async-start(), calls=%async_computation.8 | async-start | bytes 2162688 | tf_op jit(solution)/shard_map/all_gather | solution.py:336
  33.6 382.9 %all-gather.14.cloned.1.call-start = ((), (), s32[]{:S(2)}) async-start(), calls=%async_computation.6 | async-start | bytes 17301504 | tf_op jit(solution)/shard_map/all_gather | solution.py:334
  34.4 497.9 %all-gather.16.cloned.1.call-start = ((), (), s32[]{:S(2)}) async-start(), calls=%async_computation.7 | async-start | bytes 17301504 | tf_op jit(solution)/shard_map/all_gather | solution.py:335
  35.1 555.5 %all-gather.20.cloned.1.call-start = ((), (), s32[]{:S(2)}) async-start(), calls=%async_computation.9 | async-start | bytes 2162688 | tf_op jit(solution)/shard_map/all_gather | solution.py:337
  35.8 648.9 %all-gather.22.cloned.1.call-start = ((), (), s32[]{:S(2)}) async-start(), calls=%async_computation.10 | async-start | bytes 1310720 | tf_op jit(solution)/shard_map/all_gather | solution.py:356
  82.1 544.1 %copy-start.144 = (f32[1,1024]{1,0:T(1,128)}, f32[1,1024]{1,0:T(1,128)S(1)}, u32[]{:S(2)}) copy-start(f32[1,1024]{1,0:T(1,128)S(1)} %get-tuple-element.572) | copy-start | bytes 12292
  82.1 545.4 %copy-start.146 = (f32[1,1024]{1,0:T(1,128)}, f32[1,1024]{1,0:T(1,128)S(1)}, u32[]{:S(2)}) copy-start(f32[1,1024]{1,0:T(1,128)S(1)} %get-tuple-element.566) | copy-start | bytes 12292
  85.9 155.1 %copy-start.21 = (f32[128,1024]{1,0:T(8,128)}, f32[128,1024]{1,0:T(8,128)S(1)}, u32[]{:S(2)}) copy-start(f32[128,1024]{1,0:T(8,128)S(1)} %get-tuple-element.542) | copy-start | bytes 1572868
  85.9 172.5 %copy-start.20 = (f32[128,1024]{1,0:T(8,128)}, f32[128,1024]{1,0:T(8,128)S(1)}, u32[]{:S(2)}) copy-start(f32[128,1024]{1,0:T(8,128)S(1)} %get-tuple-element.544) | copy-start | bytes 1572868
  85.9 182.4 %copy-start.16 = (f32[128,1024]{1,0:T(8,128)}, f32[128,1024]{1,0:T(8,128)S(1)}, u32[]{:S(2)}) copy-start(f32[128,1024]{1,0:T(8,128)S(1)} %get-tuple-element.540) | copy-start | bytes 1572868
  85.9 521.6 %copy-start.18 = (f32[128,1024]{1,0:T(8,128)}, f32[128,1024]{1,0:T(8,128)S(1)}, u32[]{:S(2)}) copy-start(f32[128,1024]{1,0:T(8,128)S(1)} %get-tuple-element.532) | copy-start | bytes 1572868
  85.9 182.4 %copy-start.194 = (f32[128]{0:T(128)}, f32[128]{0:T(128)S(1)}, u32[]{:S(2)}) copy-start(f32[128]{0:T(128)S(1)} %broadcast_multiply_fusion.18) | copy-start | bytes 1540
  86.0 155.0 %copy-start.196 = (f32[128]{0:T(128)}, f32[128]{0:T(128)S(1)}, u32[]{:S(2)}) copy-start(f32[128]{0:T(128)S(1)} %broadcast_multiply_fusion.30) | copy-start | bytes 1540
  86.2 154.7 %copy-start.228 = (f32[128]{0:T(128)}, f32[128]{0:T(128)S(1)}, u32[]{:S(2)}) copy-start(f32[128]{0:T(128)S(1)} %add_rsqrt_fusion.10) | copy-start | bytes 1540
  86.3 172.1 %copy-start.198 = (f32[128]{0:T(128)}, f32[128]{0:T(128)S(1)}, u32[]{:S(2)}) copy-start(f32[128]{0:T(128)S(1)} %broadcast_multiply_fusion.33) | copy-start | bytes 1540
  86.5 171.9 %copy-start.226 = (f32[128]{0:T(128)}, f32[128]{0:T(128)S(1)}, u32[]{:S(2)}) copy-start(f32[128]{0:T(128)S(1)} %add_rsqrt_fusion.13) | copy-start | bytes 1540
  86.5 181.8 %copy-start.224 = (f32[128]{0:T(128)}, f32[128]{0:T(128)S(1)}, u32[]{:S(2)}) copy-start(f32[128]{0:T(128)S(1)} %add_rsqrt_fusion.4) | copy-start | bytes 1540
  177.7 65.5 %copy-start.2 = (f32[16,128,128]{1,2,0:T(8,128)}, f32[16,128,128]{1,2,0:T(8,128)S(1)}, u32[]{:S(2)}) copy-start(f32[16,128,128]{1,2,0:T(8,128)S(1)} %get-tuple-element.617) | copy-start | bytes 3145732
  243.3 354.6 %copy-start.200 = (f32[128]{0:T(128)}, f32[128]{0:T(128)S(1)}, u32[]{:S(2)}) copy-start(f32[128]{0:T(128)S(1)} %broadcast_multiply_fusion.29) | copy-start | bytes 1540
  243.5 354.4 %copy-start.230 = (f32[128]{0:T(128)}, f32[128]{0:T(128)S(1)}, u32[]{:S(2)}) copy-start(f32[128]{0:T(128)S(1)} %add_rsqrt_fusion.9) | copy-start | bytes 1540
  250.7 345.6 %copy-start.71 = (bf16[128,1024]{0,1:T(8,128)(2,1)}, bf16[128,1024]{0,1:T(8,128)(2,1)S(1)}, u32[]{:S(2)}) copy-start(bf16[128,1024]{0,1:T(8,128)(2,1)S(1)} %copy.167) | copy-start | bytes 786436
  260.6 330.0 %copy-start.25 = (f32[128,1024]{1,0:T(8,128)}, f32[128,1024]{1,0:T(8,128)S(1)}, u32[]{:S(2)}) copy-start(f32[128,1024]{1,0:T(8,128)S(1)} %get-tuple-element.603) | copy-start | bytes 1572868
  260.6 330.0 %copy-start.184 = (f32[128]{0:T(128)}, f32[128]{0:T(128)S(1)}, u32[]{:S(2)}) copy-start(f32[128]{0:T(128)S(1)} %broadcast_multiply_fusion.32) | copy-start | bytes 1540
  270.5 355.8 %copy-start.22 = (f32[128,1024]{1,0:T(8,128)}, f32[128,1024]{1,0:T(8,128)S(1)}, u32[]{:S(2)}) copy-start(f32[128,1024]{1,0:T(8,128)S(1)} %get-tuple-element.599) | copy-start | bytes 1572868
  270.5 355.8 %copy-start.181 = (f32[128]{0:T(128)}, f32[128]{0:T(128)S(1)}, u32[]{:S(2)}) copy-start(f32[128]{0:T(128)S(1)} %broadcast_multiply_fusion.17) | copy-start | bytes 1540
  270.8 319.8 %copy-start.210 = (f32[128]{0:T(128)}, f32[128]{0:T(128)S(1)}, u32[]{:S(2)}) copy-start(f32[128]{0:T(128)S(1)} %add_rsqrt_fusion.12) | copy-start | bytes 1540
  270.8 355.5 %copy-start.207 = (f32[128]{0:T(128)}, f32[128]{0:T(128)S(1)}, u32[]{:S(2)}) copy-start(f32[128]{0:T(128)S(1)} %add_rsqrt_fusion.3) | copy-start | bytes 1540
  271.7 151.1 %copy-start.90 = (bf16[128,1024]{1,0:T(8,128)(2,1)}, bf16[128,1024]{1,0:T(8,128)(2,1)S(1)}, u32[]{:S(2)}) copy-start(bf16[128,1024]{1,0:T(8,128)(2,1)S(1)} %get-tuple-element.580) | copy-start | bytes 786436
  301.4 289.2 %copy-start.284 = (f32[128,512]{1,0:T(8,128)}, f32[128,512]{1,0:T(8,128)S(1)}, u32[]{:S(2)}) copy-start(f32[128,512]{1,0:T(8,128)S(1)} %fusion.361) | copy-start | bytes 786436
  600.0 236.7 %copy-start.27 = (f32[128,1024]{1,0:T(8,128)}, f32[128,1024]{1,0:T(8,128)S(1)}, u32[]{:S(2)}) copy-start(f32[128,1024]{1,0:T(8,128)S(1)} %get-tuple-element.623) | copy-start | bytes 1572868
  600.0 236.7 %copy-start.189 = (f32[128]{0:T(128)}, f32[128]{0:T(128)S(1)}, u32[]{:S(2)}) copy-start(f32[128]{0:T(128)S(1)} %broadcast_multiply_fusion.28) | copy-start | bytes 1540
  600.3 236.5 %copy-start.215 = (f32[128]{0:T(128)}, f32[128]{0:T(128)S(1)}, u32[]{:S(2)}) copy-start(f32[128]{0:T(128)S(1)} %add_rsqrt_fusion.8) | copy-start | bytes 1540
  632.4 201.5 %copy-start.29 = (f32[128,1024]{1,0:T(8,128)}, f32[128,1024]{1,0:T(8,128)S(1)}, u32[]{:S(2)}) copy-start(f32[128,1024]{1,0:T(8,128)S(1)} %get-tuple-element.613) | copy-start | bytes 1572868
  632.4 201.5 %copy-start.191 = (f32[128]{0:T(128)}, f32[128]{0:T(128)S(1)}, u32[]{:S(2)}) copy-start(f32[128]{0:T(128)S(1)} %broadcast_multiply_fusion.15) | copy-start | bytes 1540
  632.6 201.3 %copy-start.217 = (f32[128]{0:T(128)}, f32[128]{0:T(128)S(1)}, u32[]{:S(2)}) copy-start(f32[128]{0:T(128)S(1)} %add_rsqrt_fusion.1) | copy-start | bytes 1540
  638.8 192.6 %copy-start.287 = (f32[128,512]{1,0:T(8,128)}, f32[128,512]{1,0:T(8,128)S(1)}, u32[]{:S(2)}) copy-start(f32[128,512]{1,0:T(8,128)S(1)} %fusion.363) | copy-start | bytes 786436
  649.7 181.8 %copy-start.155 = (f32[128]{0:T(128)}, f32[128]{0:T(128)S(1)}, u32[]{:S(2)}) copy-start(f32[128]{0:T(128)S(1)} %broadcast_multiply_fusion.27) | copy-start | bytes 1540
  649.9 181.6 %copy-start.175 = (f32[128]{0:T(128)}, f32[128]{0:T(128)S(1)}, u32[]{:S(2)}) copy-start(f32[128]{0:T(128)S(1)} %add_rsqrt_fusion.7) | copy-start | bytes 1540
  651.6 156.6 %copy-start.288 = (f32[128,512]{1,0:T(8,128)}, f32[128,512]{1,0:T(8,128)S(1)}, u32[]{:S(2)}) copy-start(f32[128,512]{1,0:T(8,128)S(1)} %fusion.362) | copy-start | bytes 786436
  661.6 148.3 %copy-start.157 = (f32[128]{0:T(128)}, f32[128]{0:T(128)S(1)}, u32[]{:S(2)}) copy-start(f32[128]{0:T(128)S(1)} %broadcast_multiply_fusion.14) | copy-start | bytes 1540
  661.9 148.1 %copy-start.177 = (f32[128]{0:T(128)}, f32[128]{0:T(128)S(1)}, u32[]{:S(2)}) copy-start(f32[128]{0:T(128)S(1)} %add_rsqrt_fusion) | copy-start | bytes 1540
  663.0 37.2 %all-gather.24.cloned.1.call-start = ((), (), s32[]{:S(2)}) async-start(), calls=%async_computation.12 | async-start | bytes 1310720 | tf_op jit(solution)/shard_map/all_gather | solution.py:356
  684.2 94.5 %reduce-scatter.8.cloned.1.call-start = ((), (), s32[]{:S(2)}) async-start(), calls=%async_computation.13 | async-start | bytes 1310720 | tf_op jit(solution)/shard_map/reduce_scatter | solution.py:378
  755.0 51.0 %reduce-scatter.6.cloned.1.call-start = ((), (), s32[]{:S(2)}) async-start(), calls=%async_computation.11 | async-start | bytes 1310720 | tf_op jit(solution)/shard_map/reduce_scatter | solution.py:378
  770.9 373.3 %all-reduce.7.cloned.1.call-start = ((), (), s32[]{:S(2)}) async-start(), calls=%async_computation.14 | async-start | bytes 16777216 | tf_op jit(solution)/shard_map/psum | solution.py:398
  (270 other events, 1321.1 us)
Sparse Core Ops, SparseCore 0:
  31.8 48.8 reduce-scatter.3
  663.1 15.6 all-gather.21
  684.4 13.0 all-gather.23
  755.1 23.5 reduce-scatter.7
  781.1 24.8 reduce-scatter.5
Sparse Core Ops, SparseCore 1:
  35.0 135.7 all-gather.9
  173.6 67.4 all-gather.11
  244.3 55.4 all-gather.17
  302.8 113.6 all-gather.13
  419.4 112.8 all-gather.15
  535.8 54.7 all-gather.19
  964.1 180.0 all-reduce.6
where the time goes:
time: 1170 us; the launch traced here: 1160 us
  waiting for transfers between devices  598 us (51%)
  matrix products  312 us (27%)
  blocking collectives  119 us (10%)
  local copies, waits for them, and re-layouts  59.4 us (5%)
  other arithmetic  52.6 us (4%)
  between operations  23.8 us (2%)
    dot_general x28, matrix products, times_transpose(): lax.dot_general(left, right, (((1,), (1,)), ((), ())), preferred_element_...  143 us
    dot_general x32, matrix products, times_weight(): return jnp.dot(left, right, preferred_element_type=jnp.float32)  127 us
    psum x1, waiting for transfers between devices, local(): lax.psum((grad_down, grad_up, norm_grads, task_local), ('dp', 'vocab'))  119 us
    all_gather x1, waiting for transfers between devices, local(): lax.all_gather(frozen_parts[2], ('dp', 'vocab'), axis=1, tiled=True)  115 us
    all_gather x1, waiting for transfers between devices, local(): lax.all_gather(frozen_parts[3], ('dp', 'vocab'), axis=1, tiled=True)  109 us
    all_gather x1, waiting for transfers between devices, local(): lax.all_gather(frozen_parts[0], ('dp', 'vocab'), axis=1, tiled=True)  82.3 us
    all_gather x1, waiting for transfers between devices, local(): lax.all_gather(frozen_parts[1], ('dp', 'vocab'), axis=1, tiled=True)  59.2 us
    all_gather x1, waiting for transfers between devices, local(): lax.all_gather(frozen_parts[5], ('dp', 'vocab'), axis=1, tiled=True)  50.2 us
  transfers between devices with their start and end apart: 12, of which 9 were waited for; matrix products, arithmetic and copies ran while one was open for 10% of the time, Pallas kernels for 0%

commit v1 on v0

--- a/solution.py
+++ b/solution.py
@@ -1,6 +1,10 @@
+import functools
+
 import jax
 import jax.numpy as jnp
 from jax import lax
+from jax.experimental import pallas as pl
+from jax.experimental.pallas import tpu as pltpu
 from jax.sharding import PartitionSpec as P
 
 HEADS = 16
@@ -73,21 +77,21 @@
 
 
 def split_heads(value):
-    return value.reshape(value.shape[0], HEADS, -1)
+    return value.reshape(-1, LEN, HEADS, value.shape[1] // HEADS)
 
 
 def head_scores(queries, key_rows, key_mask):
     scale = (queries.shape[1] // HEADS) ** (-0.5)
     scores = (
         jnp.einsum(
-            "qhd,khd->hqk",
+            "bqhd,bkhd->bhqk",
             split_heads(queries),
             split_heads(key_rows),
             preferred_element_type=jnp.float32,
         )
         * scale
     )
-    return (jnp.where(key_mask[None], scores, NEGATIVE), scale)
+    return (jnp.where(key_mask[:, None], scores, NEGATIVE), scale)
 
 
 def attend_forward(queries, key_rows, values, key_mask):
@@ -96,7 +100,7 @@
     log_total = top + jnp.log(jnp.sum(jnp.exp(scores - top), -1, keepdims=True))
     probs = as_low(jnp.exp(scores - log_total))
     output = jnp.einsum(
-        "hqk,khd->qhd", probs, split_heads(values), preferred_element_type=jnp.float32
+        "bhqk,bkhd->bqhd", probs, split_heads(values), preferred_element_type=jnp.float32
     )
     return (output.reshape(queries.shape[0], -1), log_total)
 
@@ -106,21 +110,21 @@
     probs = jnp.exp(scores - log_total)
     grad_heads = split_heads(grad_low)
     grad_probs = jnp.einsum(
-        "qhd,khd->hqk", grad_heads, split_heads(values), preferred_element_type=jnp.float32
+        "bqhd,bkhd->bhqk", grad_heads, split_heads(values), preferred_element_type=jnp.float32
     )
     grad_values = jnp.einsum(
-        "hqk,qhd->khd", as_low(probs), grad_heads, preferred_element_type=jnp.float32
+        "bhqk,bqhd->bkhd", as_low(probs), grad_heads, preferred_element_type=jnp.float32
     )
     grad_scores = as_low(probs * (grad_probs - jnp.sum(probs * grad_probs, -1, keepdims=True)))
     grad_queries = (
         jnp.einsum(
-            "hqk,khd->qhd", grad_scores, split_heads(key_rows), preferred_element_type=jnp.float32
+            "bhqk,bkhd->bqhd", grad_scores, split_heads(key_rows), preferred_element_type=jnp.float32
         )
         * scale
     )
     grad_keys = (
         jnp.einsum(
-            "hqk,qhd->khd", grad_scores, split_heads(queries), preferred_element_type=jnp.float32
+            "bhqk,bqhd->bkhd", grad_scores, split_heads(queries), preferred_element_type=jnp.float32
         )
         * scale
     )
@@ -269,6 +273,214 @@
         first_hat / (jnp.sqrt(second_hat) + ADAM_EPSILON) + WEIGHT_DECAY * weight
     )
     return (first, second, weight)
+
+
+MESH_ID = pl.DeviceIdType.MESH
+ORDERS = ("xzy", "yzx", "zyx", "xzy", "yzx", "zxy")
+
+
+def grid_of(dp, vocab):
+    cores = 2
+    wide = vocab // cores
+    high = wide
+    return {"z": dp // high, "y": high, "x": wide, "c": cores}
+
+
+def hops_of(order, sizes):
+    return [(axis, hop) for axis in order for hop in range(1, sizes[axis])]
+
+
+def plan_units(shapes, col_step, sequence):
+    units = []
+    for name, layer in sequence:
+        rows, cols = shapes[name]
+        row_step = min(rows, 32)
+        if name == "norms":
+            units.append((name, None, None, None))
+            continue
+        for top in range(0, rows, row_step):
+            for left in range(0, cols, col_step):
+                units.append((name, layer, (top, min(row_step, rows - top)), (left, min(col_step, cols - left))))
+    return units
+
+
+def gather_kernel(sizes, units, names, lags, *refs):
+    count = len(names)
+    ins = dict(zip(names, refs[:count]))
+    outs = dict(zip(names, refs[count : 2 * count]))
+    send_sem, recv_sem, local_sem, sib_send, sib_recv = refs[2 * count :]
+    dp, vocab = lax.axis_index("dp"), lax.axis_index("vocab")
+    here = {
+        "z": dp // sizes["y"],
+        "y": dp % sizes["y"],
+        "x": vocab // sizes["c"],
+        "c": vocab % sizes["c"],
+    }
+
+    def device(**moved):
+        at = dict(here)
+        at.update(moved)
+        return (at["z"] * sizes["y"] + at["y"], at["x"] * sizes["c"] + at["c"])
+
+    def ends(axis):
+        return here[axis] > 0, here[axis] < sizes[axis] - 1
+
+    barrier = pltpu.get_barrier_semaphore()
+    axes = [axis for axis in "zyx" if sizes[axis] > 1]
+    pl.semaphore_signal(barrier, inc=1, device_id=device(c=1 - here["c"]), device_id_type=MESH_ID)
+    peers = jnp.int32(1)
+    for axis in axes:
+        low, high = ends(axis)
+        peers = peers + low.astype(jnp.int32) + high.astype(jnp.int32)
+        for ok, step in ((low, -1), (high, 1)):
+            @pl.when(ok)
+            def _(axis=axis, step=step):
+                pl.semaphore_signal(
+                    barrier, inc=1, device_id=device(**{axis: here[axis] + step}), device_id_type=MESH_ID
+                )
+    pl.semaphore_wait(barrier, peers)
+
+    def own_source(unit):
+        name, layer, rows, cols = unit
+        if name == "norms":
+            return ins[name]
+        return ins[name].at[layer, pl.ds(*rows), pl.ds(*cols)]
+
+    def piece(unit, z, y, x, c):
+        name, layer, rows, cols = unit
+        index = (z, y, x, c)
+        if name == "norms":
+            return outs[name].at[index]
+        return outs[name].at[(layer,) + index + (pl.ds(*rows), pl.ds(*cols))]
+
+    everything = slice(None)
+
+    def view(unit, order, axis, coordinate):
+        at = {"c": here["c"]}
+        place = order.index(axis)
+        for other in "zyx":
+            position = order.index(other)
+            at[other] = everything if position < place else here[other]
+        at[axis] = coordinate
+        return piece(unit, at["z"], at["y"], at["x"], at["c"])
+
+    def sends(number, stage):
+        unit, order = units[number], ORDERS[number % len(ORDERS)]
+        axis, hop = hops_of(order, sizes)[stage]
+        size, mine = sizes[axis], here[axis]
+        first = order.index(axis) == 0
+        found = []
+        for way, (step, sem) in enumerate(((1, 0), (-1, 1))):
+            origin = mine - step * (hop - 1)
+            ok = (origin >= 0) & (origin < size) & (mine + step >= 0) & (mine + step < size)
+            def build(step=step, sem=sem, origin=origin):
+                src = own_source(unit) if first and hop == 1 else view(unit, order, axis, origin)
+                return pltpu.make_async_remote_copy(
+                    src_ref=src,
+                    dst_ref=view(unit, order, axis, origin),
+                    send_sem=send_sem.at[number, stage * 2 + sem],
+                    recv_sem=recv_sem.at[number, stage * 2 + sem],
+                    device_id=device(**{axis: mine + step}),
+                    device_id_type=MESH_ID,
+                )
+            origin_r = mine - step * hop
+            ok_r = (origin_r >= 0) & (origin_r < size)
+            def build_r(step=step, sem=sem, origin=origin_r):
+                return pltpu.make_async_remote_copy(
+                    src_ref=view(unit, order, axis, origin),
+                    dst_ref=view(unit, order, axis, origin),
+                    send_sem=send_sem.at[number, stage * 2 + sem],
+                    recv_sem=recv_sem.at[number, stage * 2 + sem],
+                    device_id=device(**{axis: mine + step}),
+                    device_id_type=MESH_ID,
+                )
+            found.append((ok, build, ok_r, build_r))
+        return found
+
+    def local_copy(number):
+        unit = units[number]
+        return pltpu.make_async_copy(
+            own_source(unit), piece(unit, here["z"], here["y"], here["x"], here["c"]), local_sem.at[number]
+        )
+
+    def sibling(number):
+        unit = units[number]
+        everywhere = piece(unit, everything, everything, everything, here["c"])
+        return pltpu.make_async_remote_copy(
+            src_ref=everywhere, dst_ref=everywhere,
+            send_sem=sib_send.at[number], recv_sem=sib_recv.at[number],
+            device_id=device(c=1 - here["c"]), device_id_type=MESH_ID,
+        )
+
+    depth = sum(sizes[axis] - 1 for axis in "zyx")
+    stages = depth + 2
+    events = sorted(
+        (number + lags[stage], -stage, number, stage) for number in range(len(units)) for stage in range(stages)
+    )
+    for _, _, number, stage in events:
+        if stage == 0:
+            local_copy(number).start()
+        if 1 <= stage <= depth:
+            for _, _, ok_r, build_r in sends(number, stage - 1):
+                @pl.when(ok_r)
+                def _(build_r=build_r):
+                    build_r().wait_recv()
+        order = ORDERS[number % len(ORDERS)]
+        if stage == sizes[order[0]] - 1:
+            local_copy(number).wait()
+        if stage < depth:
+            for ok, build, _, _ in sends(number, stage):
+                @pl.when(ok)
+                def _(build=build):
+                    build().start()
+        if stage == depth:
+            sibling(number).start()
+        if stage == depth + 1:
+            sibling(number).wait_recv()
+    for number in range(len(units)):
+        sibling(number).wait_send()
+        for stage in range(depth):
+            for ok, build, _, _ in sends(number, stage):
+                @pl.when(ok)
+                def _(build=build):
+                    build().wait_send()
+
+
+def gather_all(arrays, dp, vocab, sequence, col_step=512, lags=None):
+    sizes = grid_of(dp, vocab)
+    names = list(arrays)
+    shapes = {name: arrays[name].shape[-2:] for name in names}
+    units = plan_units(shapes, col_step, sequence)
+    depth = sum(sizes[axis] - 1 for axis in "zyx")
+    if lags is None:
+        lags = [2 * stage for stage in range(depth + 2)]
+    grid = tuple(sizes[axis] for axis in "zyxc")
+    out_shape = []
+    for name in names:
+        value = arrays[name]
+        lead = value.shape[:-2]
+        out_shape.append(jax.ShapeDtypeStruct(lead + grid + value.shape[-2:], value.dtype))
+    anywhere = pl.BlockSpec(memory_space=pl.ANY)
+    n = len(units)
+    out = pl.pallas_call(
+        functools.partial(gather_kernel, sizes, units, names, lags),
+        out_shape=out_shape,
+        in_specs=[anywhere] * len(names),
+        out_specs=[anywhere] * len(names),
+        scratch_shapes=[
+            pltpu.SemaphoreType.DMA((n, 2 * depth)),
+            pltpu.SemaphoreType.DMA((n, 2 * depth)),
+            pltpu.SemaphoreType.DMA((n,)),
+            pltpu.SemaphoreType.DMA((n,)),
+            pltpu.SemaphoreType.DMA((n,)),
+        ],
+        compiler_params=pltpu.CompilerParams(collective_id=0, has_side_effects=True),
+    )(*[arrays[name] for name in names])
+    return dict(zip(names, out))
+
+
+SEQUENCE = [("norms", None), ("attn_in", 0), ("attn_out", 0), ("down", 0), ("widen", 0), ("up", 0), ("narrow", 0),
+            ("attn_in", 1), ("attn_out", 1), ("attn_in", 2), ("attn_out", 2), ("down", 1), ("widen", 1), ("up", 1), ("narrow", 1)]
 
 
 def local(
@@ -298,7 +510,6 @@
     vocab_rank = lax.axis_index("vocab")
     rows_local = vocab_table.shape[0]
     width = vocab_table.shape[1]
-    norms = lax.all_gather(norm_params, ("dp", "vocab"), axis=1, tiled=True)
     joined_ids = (
         jnp.stack([source_ids.reshape(groups, -1), target_in.reshape(groups, -1)], 1).reshape(-1)
         - vocab_rank * rows_local
@@ -314,102 +525,91 @@
     ).astype(jnp.float32)
     task_hot = (task_ids[:, None] == jnp.arange(TASKS)[None, :]).astype(jnp.float32)
     task_counts = lax.psum(jnp.sum(task_hot * target_length[:, None].astype(jnp.float32), 0), "dp")
-    seq_scale = jnp.sum(task_hot * (1.0 / (TASKS * task_counts))[None, :], 1).reshape(groups, MICRO)
-    group_lengths = target_length.reshape(groups, MICRO)
-    group_targets = target_ids.reshape(groups, MICRO, LEN)
+    seq_scale = jnp.sum(task_hot * (1.0 / (TASKS * task_counts))[None, :], 1)
     positions_wide = positions.astype(jnp.float32)
     key_index = jnp.arange(LEN)
     causal = key_index[:, None] >= key_index[None, :]
-    frozen_parts = (
-        attention_in,
-        attention_out,
-        widen_weight,
-        narrow_weight,
-        as_low(adapt_down),
-        as_low(adapt_up),
-    )
-    weights = (
-        lax.all_gather(frozen_parts[0], ("dp", "vocab"), axis=1, tiled=True),
-        lax.all_gather(frozen_parts[1], ("dp", "vocab"), axis=1, tiled=True),
-        lax.all_gather(frozen_parts[2], ("dp", "vocab"), axis=1, tiled=True),
-        lax.all_gather(frozen_parts[3], ("dp", "vocab"), axis=1, tiled=True),
-        lax.all_gather(frozen_parts[4], ("dp", "vocab"), axis=1, tiled=True),
-        lax.all_gather(frozen_parts[5], ("dp", "vocab"), axis=1, tiled=True),
-    )
-    grad_down = jnp.zeros((2, width, ADAPT), jnp.float32)
-    grad_up = jnp.zeros((2, ADAPT, width), jnp.float32)
+    parts = {
+        "norms": norm_params,
+        "attn_in": attention_in,
+        "attn_out": attention_out,
+        "widen": widen_weight,
+        "narrow": narrow_weight,
+        "down": as_low(adapt_down),
+        "up": as_low(adapt_up),
+    }
+    held = gather_all(parts, lax.axis_size("dp"), groups, SEQUENCE)
+    norms = held["norms"].reshape(-1, 14, norm_params.shape[1]).transpose(1, 0, 2).reshape(14, width)
+    weights = tuple(
+        held[name].reshape(held[name].shape[0], -1, held[name].shape[-1])
+        for name in ("attn_in", "attn_out", "widen", "narrow", "down", "up")
+    )
     norm_grads = jnp.zeros((14, width), jnp.float32)
-    task_local = jnp.zeros((TASKS,), jnp.float32)
-    for step in range(MICRO):
-        own = vocab_rank * MICRO + step
-        source_count = lax.dynamic_index_in_dim(source_length, own, keepdims=False)
-        cross_mask = jnp.broadcast_to(key_index[None, :] < source_count, (LEN, LEN))
-        source_rows = embedded[step * LEN : (step + 1) * LEN] + positions_wide[0]
-        enc_input, kept_enc_norm = norm_forward(source_rows, norms[0], norms[7])
-        encoded, kept_enc = layer_forward(
-            enc_input, None, weights, norms, 0, cross_mask, cross_mask
-        )
-        memory = as_low(encoded)
-        target_rows = embedded[(MICRO + step) * LEN : (MICRO + step + 1) * LEN] + positions_wide[1]
-        dec_input, kept_dec_norm = norm_forward(target_rows, norms[3], norms[10])
-        decoded, kept_dec = layer_forward(dec_input, memory, weights, norms, 1, causal, cross_mask)
-        head_rows = lax.all_gather(as_low(decoded), "vocab", axis=0, tiled=True)
-        logits = times_transpose(head_rows, vocab_table)
-        local_target = group_targets[:, step].reshape(-1) - vocab_rank * rows_local
-        target_hot = lax.broadcasted_iota(jnp.int32, logits.shape, 1) == local_target[:, None]
-        target_logit = jnp.sum(jnp.where(target_hot, logits, 0.0), 1)
-        local_max = jnp.max(logits, 1)
-        row_max = lax.pmax(local_max, "vocab")
-        row_total, row_target = lax.psum(
-            (jnp.sum(jnp.exp(logits - row_max[:, None]), 1), target_logit), "vocab"
-        )
-        log_total = row_max + jnp.log(row_total)
-        row_mask = (key_index[None, :] < group_lengths[:, step][:, None]).astype(jnp.float32)
-        row_weight = (row_mask * seq_scale[:, step][:, None]).reshape(-1)
-        row_loss = (log_total - row_target) * row_mask.reshape(-1)
-        own_loss = lax.dynamic_slice_in_dim(row_loss, vocab_rank * LEN, LEN)
-        task_local = task_local + lax.dynamic_index_in_dim(task_hot, own, keepdims=False) * jnp.sum(
-            own_loss
-        )
-        grad_logits = as_low(
-            row_weight[:, None]
-            * (jnp.exp(logits - log_total[:, None]) - target_hot.astype(jnp.float32))
-        )
-        grad_decoded = lax.psum_scatter(
-            times_weight(grad_logits, vocab_table).astype(jnp.bfloat16),
-            "vocab",
-            scatter_dimension=0,
-            tiled=True,
-        ).astype(jnp.float32)
-        grad_dec_in, grad_memory, down_part, up_part, norm_grads = layer_backward(
-            grad_decoded, kept_dec, weights, norms, 1, causal, cross_mask, norm_grads
-        )
-        grad_down = grad_down.at[1].add(down_part)
-        grad_up = grad_up.at[1].add(up_part)
-        _, grad_gain, grad_bias = norm_backward(grad_dec_in, kept_dec_norm, norms[3])
-        norm_grads = norm_grads.at[3].add(grad_gain).at[10].add(grad_bias)
-        grad_enc_in, _, down_part, up_part, norm_grads = layer_backward(
-            grad_memory, kept_enc, weights, norms, 0, cross_mask, cross_mask, norm_grads
-        )
-        grad_down = grad_down.at[0].add(down_part)
-        grad_up = grad_up.at[0].add(up_part)
-        _, grad_gain, grad_bias = norm_backward(grad_enc_in, kept_enc_norm, norms[0])
-        norm_grads = norm_grads.at[0].add(grad_gain).at[7].add(grad_bias)
-    full_down, full_up, full_norm, task_sums = lax.psum(
-        (grad_down, grad_up, norm_grads, task_local), ("dp", "vocab")
-    )
-    square_total = (
-        jnp.sum(full_down * full_down) + jnp.sum(full_up * full_up) + jnp.sum(full_norm * full_norm)
-    )
-    member = lax.axis_index(("dp", "vocab"))
-    cut = width // lax.axis_size(("dp", "vocab"))
-    shard_down = lax.dynamic_slice_in_dim(full_down, member * cut, cut, 1)
-    shard_up = lax.dynamic_slice_in_dim(
-        full_up,
-        member * (ADAPT // lax.axis_size(("dp", "vocab"))),
-        ADAPT // lax.axis_size(("dp", "vocab")),
-        1,
-    )
+    own = vocab_rank * MICRO
+    rows = MICRO * LEN
+    source_count = lax.dynamic_slice_in_dim(source_length, own, MICRO)
+    cross_mask = jnp.broadcast_to(
+        key_index[None, None, :] < source_count[:, None, None], (MICRO, LEN, LEN)
+    )
+    causal = jnp.broadcast_to(causal[None], (MICRO, LEN, LEN))
+    source_rows = embedded[:rows] + jnp.tile(positions_wide[0], (MICRO, 1))
+    enc_input, kept_enc_norm = norm_forward(source_rows, norms[0], norms[7])
+    encoded, kept_enc = layer_forward(enc_input, None, weights, norms, 0, cross_mask, cross_mask)
+    memory = as_low(encoded)
+    target_rows = embedded[rows:] + jnp.tile(positions_wide[1], (MICRO, 1))
+    dec_input, kept_dec_norm = norm_forward(target_rows, norms[3], norms[10])
+    decoded, kept_dec = layer_forward(dec_input, memory, weights, norms, 1, causal, cross_mask)
+    head_rows = lax.all_gather(as_low(decoded), "vocab", axis=0, tiled=True)
+    logits = times_transpose(head_rows, vocab_table)
+    local_target = target_ids.reshape(-1) - vocab_rank * rows_local
+    target_hot = lax.broadcasted_iota(jnp.int32, logits.shape, 1) == local_target[:, None]
+    target_logit = jnp.sum(jnp.where(target_hot, logits, 0.0), 1)
+    local_max = jnp.max(logits, 1)
+    row_max = lax.pmax(local_max, "vocab")
+    row_total, row_target = lax.psum(
+        (jnp.sum(jnp.exp(logits - row_max[:, None]), 1), target_logit), "vocab"
+    )
+    log_total = row_max + jnp.log(row_total)
+    row_mask = (key_index[None, :] < target_length[:, None]).astype(jnp.float32)
+    row_weight = (row_mask * seq_scale[:, None]).reshape(-1)
+    row_loss = (log_total - row_target).reshape(-1, LEN) * row_mask
+    own_loss = lax.dynamic_slice_in_dim(row_loss, own, MICRO)
+    task_local = jnp.sum(
+        lax.dynamic_slice_in_dim(task_hot, own, MICRO) * jnp.sum(own_loss, 1)[:, None], 0
+    )
+    grad_logits = as_low(
+        row_weight[:, None]
+        * (jnp.exp(logits - log_total[:, None]) - target_hot.astype(jnp.float32))
+    )
+    grad_decoded = lax.psum_scatter(
+        times_weight(grad_logits, vocab_table).astype(jnp.bfloat16),
+        "vocab",
+        scatter_dimension=0,
+        tiled=True,
+    ).astype(jnp.float32)
+    grad_dec_in, grad_memory, down_part, up_part, norm_grads = layer_backward(
+        grad_decoded, kept_dec, weights, norms, 1, causal, cross_mask, norm_grads
+    )
+    _, grad_gain, grad_bias = norm_backward(grad_dec_in, kept_dec_norm, norms[3])
+    norm_grads = norm_grads.at[3].add(grad_gain).at[10].add(grad_bias)
+    everyone = ("dp", "vocab")
+    dec_down = lax.psum_scatter(down_part, everyone, scatter_dimension=0, tiled=True)
+    dec_up = lax.psum_scatter(up_part, everyone, scatter_dimension=0, tiled=True)
+    grad_enc_in, _, down_part, up_part, norm_grads = layer_backward(
+        grad_memory, kept_enc, weights, norms, 0, cross_mask, cross_mask, norm_grads
+    )
+    _, grad_gain, grad_bias = norm_backward(grad_enc_in, kept_enc_norm, norms[0])
+    norm_grads = norm_grads.at[0].add(grad_gain).at[7].add(grad_bias)
+    enc_down = lax.psum_scatter(down_part, everyone, scatter_dimension=0, tiled=True)
+    enc_up = lax.psum_scatter(up_part, everyone, scatter_dimension=0, tiled=True)
+    full_norm, task_sums = lax.psum((norm_grads, task_local), everyone)
+    shard_down = jnp.stack([enc_down, dec_down])
+    shard_up = jnp.stack([enc_up, dec_up])
+    square_total = jnp.sum(full_norm * full_norm) + lax.psum(
+        jnp.sum(shard_down * shard_down) + jnp.sum(shard_up * shard_up), everyone
+    )
+    member = lax.axis_index(everyone)
+    cut = width // lax.axis_size(everyone)
     shard_norm = lax.dynamic_slice_in_dim(full_norm, member * cut, cut, 1)
     grad_norm = jnp.sqrt(square_total)
     factor = CLIP_LIMIT / jnp.maximum(grad_norm, CLIP_LIMIT)

time: 1170 us -> 1280 us (1.094)
  Pallas kernels: 0 us -> 323 us
  matrix products: 312 us -> 190 us
  waiting for transfers between devices: 598 us -> 494 us
  local copies, waits for them, and re-layouts: 59.4 us -> 138 us
  blocking collectives: 119 us -> 67.2 us
  other arithmetic: 52.6 us -> 39 us
    reduce_scatter x0 -> x4, waiting for transfers between devices: none -> 459 us  [the longest x2 268 us: local(): lax.psum_scatter(down_part, everyone, scatter_dimension=0, tiled=True)]
    all_gather x6 -> x0, waiting for transfers between devices: 444 us -> none  [the longest x1 115 us: local(): lax.all_gather(frozen_parts[2], ('dp', 'vocab'), axis=1, tiled=True)]
    pallas_call x0 -> x1, Pallas kernels: none -> 323 us  [gather_all(): pl.pallas_call(functools.partial(gather_kernel, sizes, units, names, lags...]
    psum x1 -> x0, waiting for transfers between devices: 119 us -> none  [local(): lax.psum((grad_down, grad_up, norm_grads, task_local), ('dp', 'vocab'))]
    dot_general x28 -> x14, matrix products: 143 us -> 78.9 us  [times_transpose(): lax.dot_general(left, right, (((1,), (1,)), ((), ())), preferred_element_...]
    dot_general x32 -> x16, matrix products: 127 us -> 77.9 us  [times_weight(): return jnp.dot(left, right, preferred_element_type=jnp.float32)]
    reshape x2 -> x24, local copies, waits for them, and re-layouts: 0.17 us -> 48.7 us  [split_heads(): return value.reshape(-1, LEN, HEADS, value.shape[1] // HEADS)]
    all_gather x1 -> x0, blocking collectives: 45.2 us -> none  [local(): norms = lax.all_gather(norm_params, ('dp', 'vocab'), axis=1, tiled=True)]
  transfers between devices with their start and end apart: 12 -> 7, of which waited for: 9 -> 6; matrix products, arithmetic and copies ran while one was open for 10% -> 10% of each run, Pallas kernels for 0% -> 25%
where the time goes in v1:
time: 1280 us; the launch traced here: 1270 us
  waiting for transfers between devices  494 us (39%)
  Pallas kernels  323 us (25%)
  matrix products  190 us (15%)
  local copies, waits for them, and re-layouts  138 us (11%)
  blocking collectives  67.2 us (5%)
  other arithmetic  39 us (3%)
  between operations  20.5 us (2%)
    pallas_call x1, Pallas kernels, gather_all(): pl.pallas_call(functools.partial(gather_kernel, sizes, units, names, lags...  323 us
    reduce_scatter x2, waiting for transfers between devices, local(): lax.psum_scatter(down_part, everyone, scatter_dimension=0, tiled=True)  268 us
    reduce_scatter x2, waiting for transfers between devices, local(): lax.psum_scatter(up_part, everyone, scatter_dimension=0, tiled=True)  191 us
    dot_general x14, matrix products, times_transpose(): lax.dot_general(left, right, (((1,), (1,)), ((), ())), preferred_element_...  78.9 us
    dot_general x16, matrix products, times_weight(): return jnp.dot(left, right, preferred_element_type=jnp.float32)  77.9 us
    reshape x24, local copies, waits for them, and re-layouts, split_heads(): return value.reshape(-1, LEN, HEADS, value.shape[1] // HEADS)  48.7 us
    psum x1, blocking collectives, local(): full_norm, task_sums = lax.psum((norm_grads, task_local), everyone)  37.6 us
    reduce_scatter x1, waiting for transfers between devices, local(): lax.psum_scatter(times_weight(grad_logits, vocab_table).astype(jnp.bfloat...  32.9 us
  transfers between devices with their start and end apart: 7, of which 6 were waited for; matrix products, arithmetic and copies ran while one was open for 10% of the time, Pallas kernels for 25%

profile of v1, /device:TPU:0, one launch (start us, length us, event | category | flops | bytes accessed | tf_op | source)
XLA Modules:
  0.0 1271.9 jit_solution(8057929858467422771)
XLA Ops:
  9.5 17.4 %gather_fusion = bf16[2048,1024]{1,0:T(8,128)(2,1)} fusion(bf16[6400,1024]{1,0:T(8,128)(2,1)} %param.55, s32[2048]{0:T(1024)S(1)} %broadcast_clamp_fusion), kind=kCustom, calls=%fused_computation | custom fusion | bytes 8396800 | tf_op jit(solution)/shard_map/jit(_take)/gather | solution.py:520
  26.9 3.9 select_select_fusion
  33.2 323.0 %shard_map.292 = (f32[4,2,2,2,14,32]{5,4,3,2,1,0:T(8,128)}, bf16[3,4,2,2,2,32,3072]{6,5,4,3,2,1,0:T(8,128)(2,1)}, bf16[3,4,2,2,2,32,1024]{6,5,4,3,2,1,0:T(8,128)...) custom-call(f32[14,32]{1,0:T(8,128)} %refs_0_.1, ...), custom_call_target="tpu_custom_call" | custom-call | tf_op jit(solution)/shard_map/pallas_call | solution.py:465
  356.3 2.7 slice_reduce_fusion.1
  361.5 2.9 fusion.348
  366.0 7.0 fusion.347
  374.5 7.2 fusion.344
  381.7 11.9 fusion.346
  393.6 11.7 fusion.345
  420.8 2.7 reshape.844
  423.5 2.8 copy.146
  430.3 3.2 fusion.147
  437.3 4.7 convolution_convert_fusion.1
  449.8 2.9 reshape.841
  452.7 2.8 copy.138
  459.6 6.3 fusion.362
  466.0 10.8 fusion.43
  483.8 3.1 reshape.849
  493.9 6.7 fusion.364
  500.7 10.7 fusion.41
  514.7 18.0 %psum.42 = f32[4]{0:T(128)S(1)} all-reduce(f32[4]{0:T(128)S(1)} %select_reduce_fusion.2), channel_id=1, replica_groups=mesh['dp'=8,'vocab'=4] {'dp'}, use_global_device_ids=true, to_apply=%region_22.23 | all-reduce | flops 4 | bytes 32 | tf_op jit(solution)/shard_map/psum | solution.py:527
  534.7 22.7 %fusion.361 = (f32[1024]{0:T(1024)S(1)}, f32[1024,6400]{1,0:T(8,128)}) fusion(bf16[1024,1024]{1,0:T(8,128)(2,1)} %all-gather.2.cloned.1.call-done, bf16[6400,1024]{1,0:T(8,128)(2,1)} %param.55), kind=kOutput, calls=%fused_computation.558 | convolution fusion | flops 13428325376 | bytes 41422848 | tf_op jit(solution)/shard_map/dot_general | solution.py:39
  557.4 5.9 pmax.7
  563.3 10.5 select_reduce_fusion
  573.7 5.8 all-reduce.2
  579.6 24.2 %fusion.105 = bf16[1024,1024]{1,0:T(8,128)(2,1)} fusion(bf16[6400,1024]{1,0:T(8,128)(2,1)} %param.55, f32[1024,6400]{1,0:T(8,128)} %get-tuple-element.300, s32[1024]{0:T(1024)S(1)} %subtract_bitcast_fusion, f32[1024]{0:T(1024)S(1)} %get-tuple-element.251, f32[1024]{0:T(1024)S(1)} %get-tuple-element.282), kind=kOutput, calls=%fused_computation.146 | convolution fusion | flops 13462142976 | bytes 41431040 | tf_op jit(solution)/shard_map/dot_general | solution.py:35
  603.9 32.9 %reduce-scatter.9.cloned.1.call-done = bf16[256,1024]{1,0:T(8,128)(2,1)} async-done(((bf16[1024,1024]{1,0:T(8,128)(2,1)}), bf16[256,1024]{1,0:T(8,128)(2,1)}) %reduce-scatter.9.cloned.1.call-update) | async-done | bytes 524304 | tf_op jit(solution)/shard_map/reduce_scatter | solution.py:584
  640.3 14.6 %convolution_add_fusion.6 = f32[256,1024]{1,0:T(8,128)} fusion(bf16[1024,4096]{1,0:T(8,128)(2,1)} %bitcast.269, bf16[4096,1024]{1,0:T(8,128)(2,1)} %bitcast.264, f32[256,4096]{1,0:T(8,128)} %copy-done.108, f32[256]{0:T(256)S(1)} %broadcast_multiply_fusion.8, f32[256,1024]{1,0:T(8,128)S(1)} %get-tuple-element.298, f32[256]{0:T(256)S(1)} %broadcast_multiply_fusion.10, ...), kind=kOutput, calls=%fused_computation.195 | convolution fusion | flops 4310171648 | bytes 23601152 | tf_op jit(solution)/shard_map/dot_general | solution.py:39
  659.7 2.9 reshape.850
  673.3 2.8 convolution_multiply_fusion.3
  676.2 4.5 convolution_multiply_fusion.2
  681.0 2.3 fusion.164
  683.3 11.2 convolution_add_fusion.5
  699.5 2.6 reshape.852
  702.2 2.8 copy.184
  705.0 2.9 fusion.366
  707.9 3.1 multiply_reduce_fusion
  711.1 2.2 multiply_convert_fusion.2
  720.8 3.2 multiply_reduce_fusion.8
  726.7 2.7 reshape.851
  729.4 2.8 copy.172
  743.6 6.0 fusion.338
  750.6 5.8 fusion.337
  756.7 56.3 %reduce-scatter.15.cloned.1.call-done = f32[16,1024]{1,0:T(8,128)} async-done(((f32[512,1024]{1,0:T(8,128)}), f32[16,1024]{1,0:T(8,128)}) %reduce-scatter.15.cloned.1.call-update) | async-done | bytes 65552 | tf_op jit(solution)/shard_map/reduce_scatter | solution.py:604
  813.0 134.8 %reduce-scatter.17.cloned.1.call-done = f32[16,1024]{1,0:T(8,128)} async-done(((f32[512,1024]{1,0:T(8,128)}), f32[16,1024]{1,0:T(8,128)}) %reduce-scatter.17.cloned.1.call-update) | async-done | bytes 65552 | tf_op jit(solution)/shard_map/reduce_scatter | solution.py:597
  949.3 133.3 %reduce-scatter.11.cloned.1.call-done = f32[32,512]{1,0:T(8,128)} async-done(((f32[1024,512]{1,0:T(8,128)}), f32[32,512]{1,0:T(8,128)}) %reduce-scatter.11.cloned.1.call-update) | async-done | bytes 65552 | tf_op jit(solution)/shard_map/reduce_scatter | solution.py:603
  1082.6 134.7 %reduce-scatter.13.cloned.1.call-done = f32[32,512]{1,0:T(8,128)} async-done(((f32[1024,512]{1,0:T(8,128)}), f32[32,512]{1,0:T(8,128)}) %reduce-scatter.13.cloned.1.call-update) | async-done | bytes 65552 | tf_op jit(solution)/shard_map/reduce_scatter | solution.py:596
  1220.0 37.6 %all-reduce.1 = (f32[14,1024]{1,0:T(8,128)S(1)}, f32[]{:T(128)}, f32[4]{0:T(128)}) all-reduce(f32[14,1024]{1,0:T(8,128)S(1)} %scatter-add.69, f32[]{:T(128)S(6)} %add.498, f32[4]{0:T(128)S(1)} %multiply_reduce_fusion.27), channel_id=1, replica_groups=mesh['dp'=8,'vocab'=4] {'dp','vocab'}, use_global_device_ids=true, to_apply=%region_58.59 | all-reduce | flops 14341 | bytes 114728 | tf_op jit(solution)/shard_map/psum | solution.py:605
  (446 shorter events, 118.0 us)
Async XLA Ops:
  7.2 398.1 %reduce-scatter.7.cloned.1.call-start = ((), (), s32[]{:S(2)}) async-start(), calls=%async_computation.6 | async-start | bytes 5242880 | tf_op jit(solution)/shard_map/reduce_scatter | solution.py:523
  30.8 330.4 %copy-start.104 = (s32[8]{0:T(128)S(1)}, s32[8]{0:T(128)}, u32[]{:S(2)}) copy-start(s32[8]{0:T(128)} %param.52) | copy-start | bytes 100
  30.8 503.8 %all-gather.2.cloned.1.call-start = ((), (), s32[]{:S(2)}) async-start(), calls=%async_computation.7 | async-start | bytes 2621440 | tf_op jit(solution)/shard_map/all_gather | solution.py:562
  359.2 130.8 %copy-start.74 = (f32[1024]{0:T(1024)}, f32[1024]{0:T(1024)S(1)}, u32[]{:S(2)}) copy-start(f32[1024]{0:T(1024)S(1)} %mul.726) | copy-start | bytes 12292
  359.5 117.3 %copy-start.77 = (f32[1024]{0:T(1024)}, f32[1024]{0:T(1024)S(1)}, u32[]{:S(2)}) copy-start(f32[1024]{0:T(1024)S(1)} %mul.704) | copy-start | bytes 12292
  359.7 119.1 %copy-start.88 = (f32[1024]{0:T(1024)}, f32[1024]{0:T(1024)S(1)}, u32[]{:S(2)}) copy-start(f32[1024]{0:T(1024)S(1)} %mul.730) | copy-start | bytes 12292
  361.5 13.0 %copy-start.6 = (bf16[3,4,2,2,2,32,3072]{6,5,4,3,2,1,0:T(8,128)(2,1)S(1)}, bf16[3,4,2,2,2,32,3072]{6,5,4,3,2,1,0:T(8,128)(2,1)}, u32[]{:S(2)}) copy-start(bf16[3,4,2,2,2,32,3072]{6,5,4,3,2,1,0:T(8,128)(2,1)} %get-tuple-element.188) | copy-start | bytes 56623108
  364.4 94.7 %copy-start.13 = (bf16[1,4,2,2,2,32,512]{6,5,4,3,2,1,0:T(8,128)(2,1)}, bf16[1,4,2,2,2,32,512]{6,5,4,3,2,1,0:T(8,128)(2,1)S(1)}, u32[]{:S(2)}) copy-start(bf16[1,4,2,2,2,32,512]{6,5,4,3,2,1,0:T(8,128)(2,1)S(1)} %get-tuple-element.267) | copy-start | bytes 3145732
  408.6 19.9 %copy-start.84 = (f32[256]{0:T(256)}, f32[256]{0:T(256)S(1)}, u32[]{:S(2)}) copy-start(f32[256]{0:T(256)S(1)} %add_rsqrt_fusion.3) | copy-start | bytes 3076
  429.4 60.6 %copy-start.79 = (f32[256]{0:T(256)}, f32[256]{0:T(256)S(1)}, u32[]{:S(2)}) copy-start(f32[256]{0:T(256)S(1)} %broadcast_multiply_fusion.12) | copy-start | bytes 3076
  429.7 60.4 %copy-start.86 = (f32[256]{0:T(256)}, f32[256]{0:T(256)S(1)}, u32[]{:S(2)}) copy-start(f32[256]{0:T(256)S(1)} %add_rsqrt_fusion.2) | copy-start | bytes 3076
  437.3 20.3 %copy-start.82 = (f32[256]{0:T(256)}, f32[256]{0:T(256)S(1)}, u32[]{:S(2)}) copy-start(f32[256]{0:T(256)S(1)} %add_rsqrt_fusion.6) | copy-start | bytes 3076
  449.7 8.7 copy-start.66
  458.5 18.3 %copy-start.7 = (f32[256,1024]{1,0:T(8,128)}, f32[256,1024]{1,0:T(8,128)S(1)}, u32[]{:S(2)}) copy-start(f32[256,1024]{1,0:T(8,128)S(1)} %get-tuple-element.288) | copy-start | bytes 3145732
  458.5 18.3 %copy-start.91 = (f32[256]{0:T(256)}, f32[256]{0:T(256)S(1)}, u32[]{:S(2)}) copy-start(f32[256]{0:T(256)S(1)} %broadcast_multiply_fusion.15) | copy-start | bytes 3076
  458.8 18.0 %copy-start.93 = (f32[256]{0:T(256)}, f32[256]{0:T(256)S(1)}, u32[]{:S(2)}) copy-start(f32[256]{0:T(256)S(1)} %add_rsqrt_fusion.5) | copy-start | bytes 3076
  459.5 17.3 %copy-start.61 = (f32[256,512]{1,0:T(8,128)}, f32[256,512]{1,0:T(8,128)S(1)}, u32[]{:S(2)}) copy-start(f32[256,512]{1,0:T(8,128)S(1)} %fusion.363) | copy-start | bytes 1572868
  459.5 19.3 %slice-start.6 = ((s8[6291456]{0:T(1024)(128)(4,1)}), s8[4194304]{0:T(1024)(128)(4,1)S(1)}, s32[]{:S(2)}) async-start(s8[6291456]{0:T(1024)(128)(4,1)} %bitcast.280), calls=%async_computation.19 | async-start | bytes 8388608
  465.9 10.9 copy-start.107
  466.0 10.9 copy-start.53
  466.0 12.8 %slice-start.7 = ((s8[6291456]{0:T(1024)(128)(4,1)}), s8[2097152]{0:T(1024)(128)(4,1)S(1)}, s32[]{:S(2)}) async-start(s8[6291456]{0:T(1024)(128)(4,1)} %bitcast.280), calls=%async_computation.20 | async-start | bytes 4194304
  492.8 164.2 %copy-start.9 = (f32[256,1024]{1,0:T(8,128)}, f32[256,1024]{1,0:T(8,128)S(1)}, u32[]{:S(2)}) copy-start(f32[256,1024]{1,0:T(8,128)S(1)} %get-tuple-element.296) | copy-start | bytes 3145732
  493.9 17.6 %copy-start.63 = (f32[256,512]{1,0:T(8,128)}, f32[256,512]{1,0:T(8,128)S(1)}, u32[]{:S(2)}) copy-start(f32[256,512]{1,0:T(8,128)S(1)} %fusion.365) | copy-start | bytes 1572868
  500.6 10.8 copy-start.108
  500.6 10.8 copy-start.55
  511.5 21.4 %copy-start.101 = (s32[8,128]{1,0:T(8,128)S(1)}, s32[8,128]{1,0:T(8,128)}, u32[]{:S(2)}) copy-start(s32[8,128]{1,0:T(8,128)} %param.51) | copy-start | bytes 12292
  513.1 127.1 %copy-start.17 = (f32[256,1024]{1,0:T(8,128)}, f32[256,1024]{1,0:T(8,128)S(1)}, u32[]{:S(2)}) copy-start(f32[256,1024]{1,0:T(8,128)S(1)} %get-tuple-element.298) | copy-start | bytes 3145732
  514.5 122.3 %reduce-scatter.9.cloned.1.call-start = ((), (), s32[]{:S(2)}) async-start(), calls=%async_computation.8 | async-start | bytes 2621440 | tf_op jit(solution)/shard_map/reduce_scatter | solution.py:584
  532.7 24.7 %copy-start.105 = (f32[4]{0:T(128)}, f32[4]{0:T(128)S(1)}, u32[]{:S(2)}) copy-start(f32[4]{0:T(128)S(1)} %psum.42) | copy-start | bytes 52
  603.8 209.2 %reduce-scatter.15.cloned.1.call-start = ((), (), s32[]{:S(2)}) async-start(), calls=%async_computation.11 | async-start | bytes 2162688 | tf_op jit(solution)/shard_map/reduce_scatter | solution.py:604
  640.3 14.6 %copy-start.16 = (bf16[1,4,2,2,2,32,512]{6,5,4,3,2,1,0:T(8,128)(2,1)S(1)}, bf16[1,4,2,2,2,32,512]{6,5,4,3,2,1,0:T(8,128)(2,1)}, u32[]{:S(2)}) copy-start(bf16[1,4,2,2,2,32,512]{6,5,4,3,2,1,0:T(8,128)(2,1)} %get-tuple-element.266) | copy-start | bytes 3145732
  676.1 271.7 %reduce-scatter.17.cloned.1.call-start = ((), (), s32[]{:S(2)}) async-start(), calls=%async_computation.12 | async-start | bytes 2162688 | tf_op jit(solution)/shard_map/reduce_scatter | solution.py:597
  680.7 401.9 %reduce-scatter.11.cloned.1.call-start = ((), (), s32[]{:S(2)}) async-start(), calls=%async_computation.9 | async-start | bytes 2162688 | tf_op jit(solution)/shard_map/reduce_scatter | solution.py:603
  683.3 11.2 copy-start.8
  683.3 11.2 copy-start.14
  683.3 11.2 copy-start.78
  683.3 11.2 copy-start.92
  683.3 11.2 copy-start.94
  711.0 506.2 %reduce-scatter.13.cloned.1.call-start = ((), (), s32[]{:S(2)}) async-start(), calls=%async_computation.10 | async-start | bytes 2162688 | tf_op jit(solution)/shard_map/reduce_scatter | solution.py:596
  750.5 509.1 %copy-start.58 = (f32[2,16,1024]{2,1,0:T(8,128)S(1)}, f32[2,16,1024]{2,1,0:T(8,128)}, u32[]{:S(2)}) copy-start(f32[2,16,1024]{2,1,0:T(8,128)} %param.62) | copy-start | bytes 393220
  750.5 509.1 %copy-start.70 = (f32[2,16,1024]{2,1,0:T(8,128)S(1)}, f32[2,16,1024]{2,1,0:T(8,128)}, u32[]{:S(2)}) copy-start(f32[2,16,1024]{2,1,0:T(8,128)} %param.67) | copy-start | bytes 393220
  750.5 509.1 %copy-start.71 = (f32[2,16,1024]{2,1,0:T(8,128)S(1)}, f32[2,16,1024]{2,1,0:T(8,128)}, u32[]{:S(2)}) copy-start(f32[2,16,1024]{2,1,0:T(8,128)} %param.66) | copy-start | bytes 393220
  750.5 510.8 %copy-start.60 = (f32[2,32,512]{2,1,0:T(8,128)S(1)}, f32[2,32,512]{2,1,0:T(8,128)}, u32[]{:S(2)}) copy-start(f32[2,32,512]{2,1,0:T(8,128)} %param.61) | copy-start | bytes 393220
  750.5 510.8 %copy-start.72 = (f32[2,32,512]{2,1,0:T(8,128)S(1)}, f32[2,32,512]{2,1,0:T(8,128)}, u32[]{:S(2)}) copy-start(f32[2,32,512]{2,1,0:T(8,128)} %param.65) | copy-start | bytes 393220
  750.6 510.8 %copy-start.73 = (f32[2,32,512]{2,1,0:T(8,128)S(1)}, f32[2,32,512]{2,1,0:T(8,128)}, u32[]{:S(2)}) copy-start(f32[2,32,512]{2,1,0:T(8,128)} %param.64) | copy-start | bytes 393220
  750.6 512.4 %copy-start.81 = (f32[14,32]{1,0:T(8,128)S(1)}, f32[14,32]{1,0:T(8,128)}, u32[]{:S(2)}) copy-start(f32[14,32]{1,0:T(8,128)} %refs_0_.1) | copy-start | bytes 5380
  750.6 512.4 %copy-start.97 = (f32[14,32]{1,0:T(8,128)S(1)}, f32[14,32]{1,0:T(8,128)}, u32[]{:S(2)}) copy-start(f32[14,32]{1,0:T(8,128)} %param.69) | copy-start | bytes 5380
  750.6 512.4 %copy-start.98 = (f32[14,32]{1,0:T(8,128)S(1)}, f32[14,32]{1,0:T(8,128)}, u32[]{:S(2)}) copy-start(f32[14,32]{1,0:T(8,128)} %param.68) | copy-start | bytes 5380
  (78 other events, 301.5 us)
Sparse Core Ops, SparseCore 0:
  31.0 68.3 reduce-scatter.6
  514.6 19.9 all-gather.1
  603.9 32.7 reduce-scatter.8
  676.2 136.7 reduce-scatter.14
  815.2 132.5 reduce-scatter.16
  949.9 132.6 reduce-scatter.10
  1084.9 132.2 reduce-scatter.12

commit v2 on v1

--- a/solution.py
+++ b/solution.py
@@ -483,6 +483,202 @@
             ("attn_in", 1), ("attn_out", 1), ("attn_in", 2), ("attn_out", 2), ("down", 1), ("widen", 1), ("up", 1), ("narrow", 1)]
 
 
+def position(sizes):
+    dp, vocab = lax.axis_index("dp"), lax.axis_index("vocab")
+    return {
+        "z": dp // sizes["y"],
+        "y": dp % sizes["y"],
+        "x": vocab // sizes["c"],
+        "c": vocab % sizes["c"],
+    }
+
+
+def device_at(here, sizes, **moved):
+    at = dict(here)
+    at.update(moved)
+    return (at["z"] * sizes["y"] + at["y"], at["x"] * sizes["c"] + at["c"])
+
+
+def lines_barrier(here, sizes):
+    barrier = pltpu.get_barrier_semaphore()
+    peers = 0
+    for axis in "zyxc":
+        for step in range(1, sizes[axis]):
+            other = (here[axis] + step) % sizes[axis]
+            pl.semaphore_signal(
+                barrier, inc=1, device_id=device_at(here, sizes, **{axis: other}), device_id_type=MESH_ID
+            )
+            peers += 1
+    pl.semaphore_wait(barrier, peers)
+
+
+def reduce_kernel(sizes, *refs):
+    grads = refs[0:4]
+    small = refs[4]
+    shards = refs[5:9]
+    small_out, square_out = refs[9:11]
+    sums, core_send, core_recv = refs[11:15], refs[15:19], refs[19:23]
+    wide_send, wide_recv, mid_send, mid_recv, last_send, last_recv = (
+        refs[23:27], refs[27:31], refs[31:35], refs[35:39], refs[39:43], refs[43:47]
+    )
+    small_slots, square_slots = refs[47:51], refs[51:55]
+    send_sem, recv_sem = refs[55:57]
+    here = position(sizes)
+    lines_barrier(here, sizes)
+    used = [0]
+    started = []
+
+    def copy_to(src, dst, **moved):
+        number = used[0]
+        used[0] += 1
+        copy = pltpu.make_async_remote_copy(
+            src_ref=src,
+            dst_ref=dst,
+            send_sem=send_sem.at[number],
+            recv_sem=recv_sem.at[number],
+            device_id=device_at(here, sizes, **moved),
+            device_id_type=MESH_ID,
+        )
+        copy.start()
+        started.append(copy)
+        return copy
+
+    def low(value):
+        return value.astype(jnp.bfloat16)
+
+    mine = here["c"]
+
+    def share(slots, value, axis):
+        slots[here[axis]] = value
+        return [
+            copy_to(slots.at[here[axis]], slots.at[here[axis]], **{axis: (here[axis] + step) % sizes[axis]})
+            for step in range(1, sizes[axis])
+        ]
+
+    def total(slots, axis, copies):
+        for copy in copies:
+            copy.wait_recv()
+        value = slots[0]
+        for index in range(1, sizes[axis]):
+            value = value + slots[index]
+        return value
+
+    first = []
+    for part in range(4):
+        core_send[part][...] = low(grads[part][:, :, :, 1 - mine])
+        first.append(copy_to(core_send[part], core_recv[part], c=1 - mine))
+    copies = share(small_slots[0], small[...], "c")
+    plans = (("x", "y"), ("x", "y"), ("y", "x"), ("y", "x"))
+
+    second = []
+    for part in range(4):
+        first[part].wait_recv()
+        sums[part][...] = grads[part][:, :, :, mine] + core_recv[part][...].astype(jnp.float32)
+        axis = plans[part][0]
+        found = []
+        for step in range(1, sizes[axis]):
+            other = (here[axis] + step) % sizes[axis]
+            piece = sums[part][:, :, other] if axis == "x" else sums[part][:, other]
+            wide_send[part][step - 1] = low(piece)
+            found.append(copy_to(wide_send[part].at[step - 1], wide_recv[part].at[step - 1], **{axis: other}))
+        second.append(found)
+    copies = share(small_slots[1], total(small_slots[0], "c", copies), "x")
+    third = []
+    for part in range(4):
+        axis, later = plans[part]
+        held = sums[part].at[:, :, here["x"]] if axis == "x" else sums[part].at[:, here["y"]]
+        value = held[...]
+        for step, copy in enumerate(second[part]):
+            copy.wait_recv()
+            value = value + wide_recv[part][step].astype(jnp.float32)
+        held[...] = value
+        found = []
+        for step in range(1, sizes[later]):
+            other = (here[later] + step) % sizes[later]
+            mid_send[part][step - 1] = low(held[:, other])
+            found.append(copy_to(mid_send[part].at[step - 1], mid_recv[part].at[step - 1], **{later: other}))
+        third.append(found)
+    copies = share(small_slots[2], total(small_slots[1], "x", copies), "y")
+    fourth = []
+    for part in range(4):
+        axis, later = plans[part]
+        held = sums[part].at[:, here["y"], here["x"]]
+        value = held[...]
+        for step, copy in enumerate(third[part]):
+            copy.wait_recv()
+            value = value + mid_recv[part][step].astype(jnp.float32)
+        held[...] = value
+        found = []
+        for step in range(1, sizes["z"]):
+            other = (here["z"] + step) % sizes["z"]
+            last_send[part][step - 1] = low(held[other])
+            found.append(copy_to(last_send[part].at[step - 1], last_recv[part].at[step - 1], z=other))
+        fourth.append(found)
+    copies = share(small_slots[3], total(small_slots[2], "y", copies), "z")
+    square = jnp.zeros((1, 1), jnp.float32)
+    for part in range(4):
+        value = sums[part][here["z"], here["y"], here["x"]]
+        for step, copy in enumerate(fourth[part]):
+            copy.wait_recv()
+            value = value + last_recv[part][step].astype(jnp.float32)
+        shards[part][...] = value
+        square = square + jnp.sum(value * value, keepdims=True)
+    square = jnp.broadcast_to(square, (8, 128))
+    for place, axis in enumerate("cxyz"):
+        parts = share(square_slots[place], square, axis)
+        if place == 0:
+            whole = total(small_slots[3], "z", copies)
+            small_out[...] = whole
+            norm_square = jnp.sum(whole[:14] * whole[:14], keepdims=True)
+        square = total(square_slots[place], axis, parts)
+    square_out[...] = square + norm_square
+    for copy in started:
+        copy.wait_send()
+
+
+def reduce_gradients(down_enc, up_enc, down_dec, up_dec, small, dp, vocab):
+    sizes = grid_of(dp, vocab)
+    grid = tuple(sizes[axis] for axis in "zyxc")
+    whole = dp * vocab
+    grads = [
+        value.reshape(grid + (value.shape[0] // whole, value.shape[1]))
+        for value in (down_enc, up_enc, down_dec, up_dec)
+    ]
+    z, y, x, c = grid
+    tails = [value.shape[4:] for value in grads]
+    vmem = pl.BlockSpec(memory_space=pltpu.VMEM)
+    scratch = [pltpu.VMEM((z, y, x) + tail, jnp.float32) for tail in tails]
+    for _ in range(2):
+        scratch += [pltpu.VMEM((z, y, x) + tail, jnp.bfloat16) for tail in tails]
+    for _ in range(2):
+        scratch += [
+            pltpu.VMEM(((x - 1, z, y) if place < 2 else (y - 1, z, x)) + tail, jnp.bfloat16)
+            for place, tail in enumerate(tails)
+        ]
+    for _ in range(2):
+        scratch += [
+            pltpu.VMEM(((y - 1, z) if place < 2 else (x - 1, z)) + tail, jnp.bfloat16)
+            for place, tail in enumerate(tails)
+        ]
+    for _ in range(2):
+        scratch += [pltpu.VMEM((z - 1,) + tail, jnp.bfloat16) for tail in tails]
+    scratch += [pltpu.VMEM((sizes[axis],) + small.shape, jnp.float32) for axis in "cxyz"]
+    scratch += [pltpu.VMEM((sizes[axis], 8, 128), jnp.float32) for axis in "cxyz"]
+    links = 6 * (x + y + z + c)
+    scratch += [pltpu.SemaphoreType.DMA((links,)), pltpu.SemaphoreType.DMA((links,))]
+    return pl.pallas_call(
+        functools.partial(reduce_kernel, sizes),
+        out_shape=[jax.ShapeDtypeStruct(tail, jnp.float32) for tail in tails]
+        + [jax.ShapeDtypeStruct(small.shape, jnp.float32), jax.ShapeDtypeStruct((8, 128), jnp.float32)],
+        in_specs=[vmem] * 5,
+        out_specs=[vmem] * 6,
+        scratch_shapes=scratch,
+        compiler_params=pltpu.CompilerParams(
+            collective_id=1, has_side_effects=True, vmem_limit_bytes=48 * 2**20
+        ),
+    )(*grads, small)
+
+
 def local(
     source_ids,
     target_in,
@@ -592,22 +788,22 @@
     )
     _, grad_gain, grad_bias = norm_backward(grad_dec_in, kept_dec_norm, norms[3])
     norm_grads = norm_grads.at[3].add(grad_gain).at[10].add(grad_bias)
-    everyone = ("dp", "vocab")
-    dec_down = lax.psum_scatter(down_part, everyone, scatter_dimension=0, tiled=True)
-    dec_up = lax.psum_scatter(up_part, everyone, scatter_dimension=0, tiled=True)
-    grad_enc_in, _, down_part, up_part, norm_grads = layer_backward(
+    grad_enc_in, _, down_first_part, up_first_part, norm_grads = layer_backward(
         grad_memory, kept_enc, weights, norms, 0, cross_mask, cross_mask, norm_grads
     )
     _, grad_gain, grad_bias = norm_backward(grad_enc_in, kept_enc_norm, norms[0])
     norm_grads = norm_grads.at[0].add(grad_gain).at[7].add(grad_bias)
-    enc_down = lax.psum_scatter(down_part, everyone, scatter_dimension=0, tiled=True)
-    enc_up = lax.psum_scatter(up_part, everyone, scatter_dimension=0, tiled=True)
-    full_norm, task_sums = lax.psum((norm_grads, task_local), everyone)
+    small = jnp.concatenate(
+        [norm_grads, jnp.zeros((1, width), jnp.float32).at[0, :TASKS].set(task_local), jnp.zeros((1, width), jnp.float32)], 0
+    )
+    enc_down, enc_up, dec_down, dec_up, small, square = reduce_gradients(
+        down_first_part, up_first_part, down_part, up_part, small, lax.axis_size("dp"), groups
+    )
     shard_down = jnp.stack([enc_down, dec_down])
     shard_up = jnp.stack([enc_up, dec_up])
-    square_total = jnp.sum(full_norm * full_norm) + lax.psum(
-        jnp.sum(shard_down * shard_down) + jnp.sum(shard_up * shard_up), everyone
-    )
+    full_norm, task_sums = small[:14], small[14, :TASKS]
+    square_total = square[0, 0]
+    everyone = ("dp", "vocab")
     member = lax.axis_index(everyone)
     cut = width // lax.axis_size(everyone)
     shard_norm = lax.dynamic_slice_in_dim(full_norm, member * cut, cut, 1)

time: 1280 us -> 824 us (0.64)
  waiting for transfers between devices: 494 us -> 32.6 us
  Pallas kernels: 323 us -> 377 us
  blocking collectives: 67.2 us -> 29.6 us
    reduce_scatter x4 -> x0, waiting for transfers between devices: 459 us -> none  [the longest x2 268 us: local(): lax.psum_scatter(down_part, everyone, scatter_dimension=0, tiled=True)]
    pallas_call x0 -> x1, Pallas kernels: none -> 53.9 us  [reduce_gradients(): pl.pallas_call(functools.partial(reduce_kernel, sizes), out_shape=[jax.Sh...]
    psum x1 -> x0, blocking collectives: 37.6 us -> none  [local(): full_norm, task_sums = lax.psum((norm_grads, task_local), everyone)]
  transfers between devices with their start and end apart: 7 -> 3, of which waited for: 6 -> 2; matrix products, arithmetic and copies ran while one was open for 10% -> 6% of each run, Pallas kernels for 25% -> 39%
where the time goes in v2:
time: 824 us; the launch traced here: 820 us
  Pallas kernels  377 us (46%)
  matrix products  189 us (23%)
  local copies, waits for them, and re-layouts  140 us (17%)
  other arithmetic  33.4 us (4%)
  waiting for transfers between devices  32.6 us (4%)
  blocking collectives  29.6 us (4%)
  between operations  18.2 us (2%)
    pallas_call x1, Pallas kernels, gather_all(): pl.pallas_call(functools.partial(gather_kernel, sizes, units, names, lags...  323 us
    dot_general x14, matrix products, times_transpose(): lax.dot_general(left, right, (((1,), (1,)), ((), ())), preferred_element_...  78.9 us
    dot_general x16, matrix products, times_weight(): return jnp.dot(left, right, preferred_element_type=jnp.float32)  78.1 us
    pallas_call x1, Pallas kernels, reduce_gradients(): pl.pallas_call(functools.partial(reduce_kernel, sizes), out_shape=[jax.Sh...  53.9 us
    reshape x24, local copies, waits for them, and re-layouts, split_heads(): return value.reshape(-1, LEN, HEADS, value.shape[1] // HEADS)  48.6 us
    reduce_scatter x1, waiting for transfers between devices, local(): lax.psum_scatter(times_weight(grad_logits, vocab_table).astype(jnp.bfloat...  31.2 us
    psum x1, blocking collectives, local(): lax.psum(jnp.sum(task_hot * target_length[:, None].astype(jnp.float32), 0...  18 us
    gather x1, local copies, waits for them, and re-layouts, local(): jnp.take(vocab_table, jnp.clip(joined_ids, 0, rows_local - 1), axis=0)  17.4 us
  transfers between devices with their start and end apart: 3, of which 2 were waited for; matrix products, arithmetic and copies ran while one was open for 6% of the time, Pallas kernels for 39%

profile of v2, /device:TPU:0, one launch (start us, length us, event | category | flops | bytes accessed | tf_op | source)
XLA Modules:
  0.0 820.0 jit_solution(710149998638765523)
XLA Ops:
  9.5 17.4 %gather_fusion = bf16[2048,1024]{1,0:T(8,128)(2,1)} fusion(bf16[6400,1024]{1,0:T(8,128)(2,1)} %param.57, s32[2048]{0:T(1024)S(1)} %broadcast_clamp_fusion), kind=kCustom, calls=%fused_computation | custom fusion | bytes 8396800 | tf_op jit(solution)/shard_map/jit(_take)/gather | solution.py:716
  26.9 3.9 select_select_fusion
  33.2 323.0 %shard_map.292 = (f32[4,2,2,2,14,32]{5,4,3,2,1,0:T(8,128)}, bf16[3,4,2,2,2,32,3072]{6,5,4,3,2,1,0:T(8,128)(2,1)}, bf16[3,4,2,2,2,32,1024]{6,5,4,3,2,1,0:T(8,128)...) custom-call(f32[14,32]{1,0:T(8,128)} %refs_0_.1, ...), custom_call_target="tpu_custom_call" | custom-call | tf_op jit(solution)/shard_map/pallas_call | solution.py:465
  356.3 2.7 slice_reduce_fusion.1
  361.5 2.9 fusion.351
  366.1 7.0 fusion.350
  374.5 7.2 fusion.347
  381.7 11.9 %fusion.349 = (bf16[1,4,2,2,2,128,1024]{6,5,4,3,2,1,0:T(8,128)(2,1)}, bf16[1,4,2,2,2,128,1024]{6,5,4,3,2,1,0:T(8,128)(2,1)}) fusion(bf16[2,4,2,2,2,128,1024]{6,5,4,3,2,1,0:T(8,128)(2,1)} %get-tuple-element.209), kind=kLoop, calls=%fused_computation.549 | loop fusion | bytes 33554432 | tf_op jit(solution)/shard_map/slice | solution.py:224
  393.6 11.7 %fusion.348 = (bf16[1,4,2,2,2,32,4096]{6,5,4,3,2,1,0:T(8,128)(2,1)}, bf16[1,4,2,2,2,32,4096]{6,5,4,3,2,1,0:T(8,128)(2,1)}) fusion(bf16[2,4,2,2,2,32,4096]{6,5,4,3,2,1,0:T(8,128)(2,1)} %get-tuple-element.208), kind=kLoop, calls=%fused_computation.548 | loop fusion | bytes 33554432 | tf_op jit(solution)/shard_map/slice | solution.py:223
  420.7 2.8 reshape.898
  423.5 2.8 copy.146
  430.3 3.2 fusion.147
  433.5 2.1 reshape.901
  437.3 4.7 convolution_convert_fusion.1
  449.7 2.9 reshape.895
  452.7 2.7 copy.138
  459.1 6.6 fusion.365
  466.2 10.8 %fusion.43 = f32[256,1024]{1,0:T(8,128)S(1)} fusion(bf16[4096,1024]{1,0:T(8,128)(2,1)S(1)} %bitcast.280, f32[256,4096]{1,0:T(8,128)S(1)} %fusion.365), kind=kOutput, calls=%fused_computation.70 | convolution fusion | flops 2215641088 | bytes 13631488 | tf_op jit(solution)/shard_map/dot_general | solution.py:35
  484.0 3.1 reshape.903
  487.2 2.0 copy.154
  491.0 2.1 fusion.362
  494.1 6.7 fusion.367
  500.9 10.8 %fusion.41 = f32[256,1024]{1,0:T(8,128)S(1)} fusion(bf16[4096,1024]{1,0:T(8,128)(2,1)S(1)} %bitcast.286, f32[256,4096]{1,0:T(8,128)S(1)} %fusion.367), kind=kOutput, calls=%fused_computation.69 | convolution fusion | flops 2215641088 | bytes 13631488 | tf_op jit(solution)/shard_map/dot_general | solution.py:35
  514.9 18.0 %psum.21 = f32[4]{0:T(128)S(1)} all-reduce(f32[4]{0:T(128)S(1)} %select_reduce_fusion.2), channel_id=1, replica_groups=mesh['dp'=8,'vocab'=4] {'dp'}, use_global_device_ids=true, to_apply=%region_22.23 | all-reduce | flops 4 | bytes 32 | tf_op jit(solution)/shard_map/psum | solution.py:723
  534.9 22.7 %fusion.364 = (f32[1024]{0:T(1024)S(1)}, f32[1024,6400]{1,0:T(8,128)}) fusion(bf16[1024,1024]{1,0:T(8,128)(2,1)} %all-gather.2.cloned.1.call-done, bf16[6400,1024]{1,0:T(8,128)(2,1)} %param.57), kind=kOutput, calls=%fused_computation.564 | convolution fusion | flops 13428325376 | bytes 41422848 | tf_op jit(solution)/shard_map/dot_general | solution.py:39
  557.7 5.9 pmax.7
  563.5 10.5 %select_reduce_fusion = (f32[1024]{0:T(1024)S(1)}, f32[1024]{0:T(1024)S(1)}) fusion(f32[1024,6400]{1,0:T(8,128)} %get-tuple-element.321, s32[1024]{0:T(1024)S(1)} %subtract_bitcast_fusion, f32[1024]{0:T(1024)S(1)} %pmax.7), kind=kLoop, calls=%fused_computation.1 | loop fusion | flops 32765952 | bytes 26230784 | tf_op jit(solution)/shard_map/reduce_sum | solution.py:762
  574.0 5.8 all-reduce.2
  579.9 24.2 %fusion.105 = bf16[1024,1024]{1,0:T(8,128)(2,1)} fusion(bf16[6400,1024]{1,0:T(8,128)(2,1)} %param.57, f32[1024,6400]{1,0:T(8,128)} %get-tuple-element.321, s32[1024]{0:T(1024)S(1)} %subtract_bitcast_fusion, f32[1024]{0:T(1024)S(1)} %get-tuple-element.272, f32[1024]{0:T(1024)S(1)} %get-tuple-element.303), kind=kOutput, calls=%fused_computation.146 | convolution fusion | flops 13462142976 | bytes 41431040 | tf_op jit(solution)/shard_map/dot_general | solution.py:35
  605.8 31.2 %reduce-scatter.5.cloned.1.call-done = bf16[256,1024]{1,0:T(8,128)(2,1)} async-done(((bf16[1024,1024]{1,0:T(8,128)(2,1)}), bf16[256,1024]{1,0:T(8,128)(2,1)}) %reduce-scatter.5.cloned.1.call-update) | async-done | bytes 524304 | tf_op jit(solution)/shard_map/reduce_scatter | solution.py:780
  640.5 14.6 %convolution_add_fusion.6 = f32[256,1024]{1,0:T(8,128)} fusion(bf16[1024,4096]{1,0:T(8,128)(2,1)} %bitcast.288, bf16[4096,1024]{1,0:T(8,128)(2,1)} %bitcast.283, f32[256,4096]{1,0:T(8,128)} %copy-done.113, f32[256]{0:T(256)S(1)} %broadcast_multiply_fusion.8, f32[256,1024]{1,0:T(8,128)S(1)} %get-tuple-element.319, f32[256]{0:T(256)S(1)} %broadcast_multiply_fusion.10, ...), kind=kOutput, calls=%fused_computation.195 | convolution fusion | flops 4310171648 | bytes 23601152 | tf_op jit(solution)/shard_map/dot_general | solution.py:39
  655.1 2.1 multiply_reduce_fusion.10
  659.9 2.8 reshape.904
  662.8 2.0 copy.160
  673.3 11.2 %convolution_add_fusion.5 = f32[256,1024]{1,0:T(8,128)} fusion(f32[256,1024]{1,0:T(8,128)S(1)} %subtract_multiply_fusion.2, bf16[1024,4096]{1,0:T(8,128)(2,1)} %bitcast.282, bf16[4096,1024]{1,0:T(8,128)(2,1)} %bitcast.277, f32[256,4096]{1,0:T(8,128)} %copy-done.112), kind=kOutput, calls=%fused_computation.194 | convolution fusion | flops 4305977344 | bytes 23068672 | tf_op jit(solution)/shard_map/dot_general | solution.py:39
  684.5 2.1 fusion.164
  686.6 2.1 multiply_reduce_fusion.4
  691.5 2.6 reshape.906
  694.1 2.8 copy.184
  705.0 3.2 multiply_reduce_fusion.8
  710.9 2.7 reshape.905
  713.6 2.8 copy.172
  716.4 1.9 multiply_reduce_fusion.1
  722.9 2.8 convolution_multiply_fusion.3
  735.5 6.2 fusion.341
  742.8 6.0 fusion.340
  749.2 4.9 convolution_multiply_fusion.2
  754.1 53.9 %shard_map.293 = (f32[32,512]{1,0:T(8,128)S(1)}, f32[16,1024]{1,0:T(8,128)S(1)}, f32[32,512]{1,0:T(8,128)S(1)}, f32[16,1024]{1,0:T(8,128)S(1)}, f32[16,1024]{1,0:T(8,128)S(1)}, /*index=5*/f32[8,128]{1,0:T(8,128)S(1)}) custom-call(f32[4,2,2,2,32,512]{5,4,3,2,1,0:T(8,128)S(1)} %bitcast.261, f32[4,2,2,2,16,1024]{5,4,3,2,1,0:T(8,128)S(1)} %bitcast.262, ...), custom_call_target="tpu_custom_call" | custom-call | tf_op jit(solution)/shard_map/pallas_call | solution.py:669
  (447 shorter events, 105.9 us)
Async XLA Ops:
  7.2 398.1 %reduce-scatter.3.cloned.1.call-start = ((), (), s32[]{:S(2)}) async-start(), calls=%async_computation.2 | async-start | bytes 5242880 | tf_op jit(solution)/shard_map/reduce_scatter | solution.py:719
  30.8 330.4 %copy-start.109 = (s32[8]{0:T(128)S(1)}, s32[8]{0:T(128)}, u32[]{:S(2)}) copy-start(s32[8]{0:T(128)} %param.54) | copy-start | bytes 100
  30.8 504.1 %all-gather.2.cloned.1.call-start = ((), (), s32[]{:S(2)}) async-start(), calls=%async_computation.3 | async-start | bytes 2621440 | tf_op jit(solution)/shard_map/all_gather | solution.py:758
  359.2 131.0 %copy-start.80 = (f32[1024]{0:T(1024)}, f32[1024]{0:T(1024)S(1)}, u32[]{:S(2)}) copy-start(f32[1024]{0:T(1024)S(1)} %mul.717) | copy-start | bytes 12292
  359.5 117.5 %copy-start.82 = (f32[1024]{0:T(1024)}, f32[1024]{0:T(1024)S(1)}, u32[]{:S(2)}) copy-start(f32[1024]{0:T(1024)S(1)} %mul.695) | copy-start | bytes 12292
  359.7 119.3 %copy-start.93 = (f32[1024]{0:T(1024)}, f32[1024]{0:T(1024)S(1)}, u32[]{:S(2)}) copy-start(f32[1024]{0:T(1024)S(1)} %mul.721) | copy-start | bytes 12292
  361.5 13.0 %copy-start.7 = (bf16[3,4,2,2,2,32,3072]{6,5,4,3,2,1,0:T(8,128)(2,1)S(1)}, bf16[3,4,2,2,2,32,3072]{6,5,4,3,2,1,0:T(8,128)(2,1)}, u32[]{:S(2)}) copy-start(bf16[3,4,2,2,2,32,3072]{6,5,4,3,2,1,0:T(8,128)(2,1)} %get-tuple-element.206) | copy-start | bytes 56623108
  364.4 101.2 %copy-start.15 = (bf16[1,4,2,2,2,32,512]{6,5,4,3,2,1,0:T(8,128)(2,1)}, bf16[1,4,2,2,2,32,512]{6,5,4,3,2,1,0:T(8,128)(2,1)S(1)}, u32[]{:S(2)}) copy-start(bf16[1,4,2,2,2,32,512]{6,5,4,3,2,1,0:T(8,128)(2,1)S(1)} %get-tuple-element.288) | copy-start | bytes 3145732
  408.6 19.9 %copy-start.89 = (f32[256]{0:T(256)}, f32[256]{0:T(256)S(1)}, u32[]{:S(2)}) copy-start(f32[256]{0:T(256)S(1)} %add_rsqrt_fusion.3) | copy-start | bytes 3076
  420.7 8.6 %copy-start.69 = (f32[2,16,128]{2,1,0:T(8,128)}, f32[2,16,128]{2,1,0:T(8,128)S(1)}, u32[]{:S(2)}) copy-start(f32[2,16,128]{2,1,0:T(8,128)S(1)} %log_add_fusion.1) | copy-start | bytes 49156
  429.3 60.9 %copy-start.84 = (f32[256]{0:T(256)}, f32[256]{0:T(256)S(1)}, u32[]{:S(2)}) copy-start(f32[256]{0:T(256)S(1)} %broadcast_multiply_fusion.12) | copy-start | bytes 3076
  429.6 60.7 %copy-start.91 = (f32[256]{0:T(256)}, f32[256]{0:T(256)S(1)}, u32[]{:S(2)}) copy-start(f32[256]{0:T(256)S(1)} %add_rsqrt_fusion.2) | copy-start | bytes 3076
  437.3 20.3 %copy-start.87 = (f32[256]{0:T(256)}, f32[256]{0:T(256)S(1)}, u32[]{:S(2)}) copy-start(f32[256]{0:T(256)S(1)} %add_rsqrt_fusion.6) | copy-start | bytes 3076
  449.7 8.7 %copy-start.71 = (f32[2,16,128]{2,1,0:T(8,128)}, f32[2,16,128]{2,1,0:T(8,128)S(1)}, u32[]{:S(2)}) copy-start(f32[2,16,128]{2,1,0:T(8,128)S(1)} %log_add_fusion.2) | copy-start | bytes 49156
  458.5 18.5 %copy-start.8 = (f32[256,1024]{1,0:T(8,128)}, f32[256,1024]{1,0:T(8,128)S(1)}, u32[]{:S(2)}) copy-start(f32[256,1024]{1,0:T(8,128)S(1)} %get-tuple-element.307) | copy-start | bytes 3145732
  458.5 18.5 %copy-start.96 = (f32[256]{0:T(256)}, f32[256]{0:T(256)S(1)}, u32[]{:S(2)}) copy-start(f32[256]{0:T(256)S(1)} %broadcast_multiply_fusion.15) | copy-start | bytes 3076
  458.8 18.3 %copy-start.98 = (f32[256]{0:T(256)}, f32[256]{0:T(256)S(1)}, u32[]{:S(2)}) copy-start(f32[256]{0:T(256)S(1)} %add_rsqrt_fusion.5) | copy-start | bytes 3076
  459.1 20.0 %slice-start.6 = ((s8[6291456]{0:T(1024)(128)(4,1)}), s8[4194304]{0:T(1024)(128)(4,1)S(1)}, s32[]{:S(2)}) async-start(s8[6291456]{0:T(1024)(128)(4,1)} %bitcast.299), calls=%async_computation.11 | async-start | bytes 8388608
  465.6 11.3 %copy-start.112 = (f32[256,4096]{1,0:T(8,128)}, f32[256,4096]{1,0:T(8,128)S(1)}, u32[]{:S(2)}) copy-start(f32[256,4096]{1,0:T(8,128)S(1)} %fusion.365) | copy-start | bytes 12582916
  466.1 10.9 %copy-start.67 = (f32[256,512]{1,0:T(8,128)}, f32[256,512]{1,0:T(8,128)S(1)}, u32[]{:S(2)}) copy-start(f32[256,512]{1,0:T(8,128)S(1)} %fusion.366) | copy-start | bytes 1572868
  466.2 10.9 %copy-start.57 = (bf16[1,4,2,2,2,16,1024]{6,5,4,3,2,1,0:T(8,128)(2,1)S(1)}, bf16[1,4,2,2,2,16,1024]{6,5,4,3,2,1,0:T(8,128)(2,1)}, u32[]{:S(2)}) copy-start(bf16[1,4,2,2,2,16,1024]{6,5,4,3,2,1,0:T(8,128)(2,1)} %get-tuple-element.290) | copy-start | bytes 3145732
  466.2 12.9 %slice-start.7 = ((s8[6291456]{0:T(1024)(128)(4,1)}), s8[2097152]{0:T(1024)(128)(4,1)S(1)}, s32[]{:S(2)}) async-start(s8[6291456]{0:T(1024)(128)(4,1)} %bitcast.299), calls=%async_computation.12 | async-start | bytes 4194304
  484.0 9.1 %copy-start.73 = (f32[2,16,128]{2,1,0:T(8,128)}, f32[2,16,128]{2,1,0:T(8,128)S(1)}, u32[]{:S(2)}) copy-start(f32[2,16,128]{2,1,0:T(8,128)S(1)} %log_add_fusion) | copy-start | bytes 49156
  493.1 164.2 %copy-start.10 = (f32[256,1024]{1,0:T(8,128)}, f32[256,1024]{1,0:T(8,128)S(1)}, u32[]{:S(2)}) copy-start(f32[256,1024]{1,0:T(8,128)S(1)} %get-tuple-element.317) | copy-start | bytes 3145732
  494.1 17.6 %copy-start.66 = (f32[256,512]{1,0:T(8,128)}, f32[256,512]{1,0:T(8,128)S(1)}, u32[]{:S(2)}) copy-start(f32[256,512]{1,0:T(8,128)S(1)} %fusion.368) | copy-start | bytes 1572868
  500.9 10.8 %copy-start.113 = (f32[256,4096]{1,0:T(8,128)}, f32[256,4096]{1,0:T(8,128)S(1)}, u32[]{:S(2)}) copy-start(f32[256,4096]{1,0:T(8,128)S(1)} %fusion.367) | copy-start | bytes 12582916
  500.9 10.8 %copy-start.58 = (bf16[1,4,2,2,2,16,1024]{6,5,4,3,2,1,0:T(8,128)(2,1)S(1)}, bf16[1,4,2,2,2,16,1024]{6,5,4,3,2,1,0:T(8,128)(2,1)}, u32[]{:S(2)}) copy-start(bf16[1,4,2,2,2,16,1024]{6,5,4,3,2,1,0:T(8,128)(2,1)} %get-tuple-element.289) | copy-start | bytes 3145732
  511.8 21.9 %copy-start.106 = (s32[8,128]{1,0:T(8,128)S(1)}, s32[8,128]{1,0:T(8,128)}, u32[]{:S(2)}) copy-start(s32[8,128]{1,0:T(8,128)} %param.53) | copy-start | bytes 12292
  513.4 127.1 %copy-start.14 = (f32[256,1024]{1,0:T(8,128)}, f32[256,1024]{1,0:T(8,128)S(1)}, u32[]{:S(2)}) copy-start(f32[256,1024]{1,0:T(8,128)S(1)} %get-tuple-element.319) | copy-start | bytes 3145732
  514.8 122.2 %reduce-scatter.5.cloned.1.call-start = ((), (), s32[]{:S(2)}) async-start(), calls=%async_computation.4 | async-start | bytes 2621440 | tf_op jit(solution)/shard_map/reduce_scatter | solution.py:780
  640.5 14.6 %copy-start.18 = (bf16[1,4,2,2,2,32,512]{6,5,4,3,2,1,0:T(8,128)(2,1)S(1)}, bf16[1,4,2,2,2,32,512]{6,5,4,3,2,1,0:T(8,128)(2,1)}, u32[]{:S(2)}) copy-start(bf16[1,4,2,2,2,32,512]{6,5,4,3,2,1,0:T(8,128)(2,1)} %get-tuple-element.287) | copy-start | bytes 3145732
  673.2 11.3 %copy-start.55 = (f32[256,1024]{1,0:T(8,128)}, f32[256,1024]{1,0:T(8,128)S(1)}, u32[]{:S(2)}) copy-start(f32[256,1024]{1,0:T(8,128)S(1)} %subtract_multiply_fusion.2) | copy-start | bytes 3145732
  673.2 13.4 %copy-start.9 = (f32[256,1024]{1,0:T(8,128)S(1)}, f32[256,1024]{1,0:T(8,128)}, u32[]{:S(2)}) copy-start(f32[256,1024]{1,0:T(8,128)} %copy-done.8) | copy-start | bytes 3145732
  673.2 13.4 %copy-start.16 = (bf16[1,4,2,2,2,32,512]{6,5,4,3,2,1,0:T(8,128)(2,1)S(1)}, bf16[1,4,2,2,2,32,512]{6,5,4,3,2,1,0:T(8,128)(2,1)}, u32[]{:S(2)}) copy-start(bf16[1,4,2,2,2,32,512]{6,5,4,3,2,1,0:T(8,128)(2,1)} %copy-done.15) | copy-start | bytes 3145732
  673.2 13.4 %copy-start.83 = (f32[1024]{0:T(1024)S(1)}, f32[1024]{0:T(1024)}, u32[]{:S(2)}) copy-start(f32[1024]{0:T(1024)} %copy-done.82) | copy-start | bytes 12292
  673.3 13.4 %copy-start.97 = (f32[256]{0:T(256)S(1)}, f32[256]{0:T(256)}, u32[]{:S(2)}) copy-start(f32[256]{0:T(256)} %copy-done.96) | copy-start | bytes 3076
  673.3 13.4 %copy-start.99 = (f32[256]{0:T(256)S(1)}, f32[256]{0:T(256)}, u32[]{:S(2)}) copy-start(f32[256]{0:T(256)} %copy-done.98) | copy-start | bytes 3076
  708.2 8.2 copy-start.2
  708.2 8.1 copy-start.70
  754.0 55.7 %copy-start.86 = (f32[14,32]{1,0:T(8,128)S(1)}, f32[14,32]{1,0:T(8,128)}, u32[]{:S(2)}) copy-start(f32[14,32]{1,0:T(8,128)} %refs_0_.1) | copy-start | bytes 5380
  754.0 55.7 %copy-start.102 = (f32[14,32]{1,0:T(8,128)S(1)}, f32[14,32]{1,0:T(8,128)}, u32[]{:S(2)}) copy-start(f32[14,32]{1,0:T(8,128)} %param.71) | copy-start | bytes 5380
  754.0 55.7 %copy-start.103 = (f32[14,32]{1,0:T(8,128)S(1)}, f32[14,32]{1,0:T(8,128)}, u32[]{:S(2)}) copy-start(f32[14,32]{1,0:T(8,128)} %param.70) | copy-start | bytes 5380
  754.0 56.4 %copy-start.63 = (f32[2,16,1024]{2,1,0:T(8,128)S(1)}, f32[2,16,1024]{2,1,0:T(8,128)}, u32[]{:S(2)}) copy-start(f32[2,16,1024]{2,1,0:T(8,128)} %param.64) | copy-start | bytes 393220
  754.0 56.4 %copy-start.75 = (f32[2,16,1024]{2,1,0:T(8,128)S(1)}, f32[2,16,1024]{2,1,0:T(8,128)}, u32[]{:S(2)}) copy-start(f32[2,16,1024]{2,1,0:T(8,128)} %param.69) | copy-start | bytes 393220
  754.1 56.4 %copy-start.76 = (f32[2,16,1024]{2,1,0:T(8,128)S(1)}, f32[2,16,1024]{2,1,0:T(8,128)}, u32[]{:S(2)}) copy-start(f32[2,16,1024]{2,1,0:T(8,128)} %param.68) | copy-start | bytes 393220
  754.1 57.2 %copy-start.65 = (f32[2,32,512]{2,1,0:T(8,128)S(1)}, f32[2,32,512]{2,1,0:T(8,128)}, u32[]{:S(2)}) copy-start(f32[2,32,512]{2,1,0:T(8,128)} %param.63) | copy-start | bytes 393220
  754.1 57.2 %copy-start.77 = (f32[2,32,512]{2,1,0:T(8,128)S(1)}, f32[2,32,512]{2,1,0:T(8,128)}, u32[]{:S(2)}) copy-start(f32[2,32,512]{2,1,0:T(8,128)} %param.67) | copy-start | bytes 393220
  754.1 57.2 %copy-start.78 = (f32[2,32,512]{2,1,0:T(8,128)S(1)}, f32[2,32,512]{2,1,0:T(8,128)}, u32[]{:S(2)}) copy-start(f32[2,32,512]{2,1,0:T(8,128)} %param.66) | copy-start | bytes 393220
  (79 other events, 288.6 us)
Sparse Core Ops, SparseCore 0:
  31.0 68.3 reduce-scatter.2
  514.9 20.0 all-gather.1
  604.2 32.7 reduce-scatter.4

commit v3 on v0

v3 whole, which is shorter than its diff:
```python
import functools

import jax
import jax.numpy as jnp
from jax import lax
from jax.experimental import pallas as pl
from jax.experimental.pallas import tpu as pltpu
from jax.sharding import PartitionSpec as P

MESH_ID = pl.DeviceIdType.MESH
TASKS = 4
STEP = 10
CLIP_LIMIT = 0.002
BETA_FIRST = 0.9
BETA_SECOND = 0.999
ADAM_EPSILON = 1e-08
WEIGHT_DECAY = 0.01
RATE_ADAPTER = 0.02
RATE_NORMS = 0.2


def grid_of(dp, vocab):
    cores = 2
    across = vocab // cores
    return {"z": dp // across, "y": across, "x": across, "c": cores}


def position(sizes):
    dp, vocab = lax.axis_index("dp"), lax.axis_index("vocab")
    return {
        "z": dp // sizes["y"],
        "y": dp % sizes["y"],
        "x": vocab // sizes["c"],
        "c": vocab % sizes["c"],
    }


def device_at(here, sizes, **moved):
    at = dict(here)
    at.update(moved)
    return (at["z"] * sizes["y"] + at["y"], at["x"] * sizes["c"] + at["c"])


def lines_barrier(here, sizes):
    barrier = pltpu.get_barrier_semaphore()
    peers = 0
    for axis in "zyxc":
        for step in range(1, sizes[axis]):
            other = (here[axis] + step) % sizes[axis]
            pl.semaphore_signal(
                barrier, inc=1, device_id=device_at(here, sizes, **{axis: other}), device_id_type=MESH_ID
            )
            peers += 1
    pl.semaphore_wait(barrier, peers)


def reduce_kernel(sizes, *refs):
    grads = refs[0:4]
    small = refs[4]
    shards = refs[5:9]
    small_out, square_out = refs[9:11]
    sums, core_send, core_recv = refs[11:15], refs[15:19], refs[19:23]
    wide_send, wide_recv, mid_send, mid_recv, last_send, last_recv = (
        refs[23:27], refs[27:31], refs[31:35], refs[35:39], refs[39:43], refs[43:47]
    )
    small_slots, square_slots = refs[47:51], refs[51:55]
    send_sem, recv_sem = refs[55:57]
    here = position(sizes)
    lines_barrier(here, sizes)
    used = [0]
    started = []

    def copy_to(src, dst, **moved):
        number = used[0]
        used[0] += 1
        copy = pltpu.make_async_remote_copy(
            src_ref=src,
            dst_ref=dst,
            send_sem=send_sem.at[number],
            recv_sem=recv_sem.at[number],
            device_id=device_at(here, sizes, **moved),
            device_id_type=MESH_ID,
        )
        copy.start()
        started.append(copy)
        return copy

    def low(value):
        return value.astype(jnp.bfloat16)

    mine = here["c"]

    def share(slots, value, axis):
        slots[here[axis]] = value
        return [
            copy_to(slots.at[here[axis]], slots.at[here[axis]], **{axis: (here[axis] + step) % sizes[axis]})
            for step in range(1, sizes[axis])
        ]

    def total(slots, axis, copies):
        for copy in copies:
            copy.wait_recv()
        value = slots[0]
        for index in range(1, sizes[axis]):
            value = value + slots[index]
        return value

    first = []
    for part in range(4):
        core_send[part][...] = low(grads[part][:, :, :, 1 - mine])
        first.append(copy_to(core_send[part], core_recv[part], c=1 - mine))
    copies = share(small_slots[0], small[...], "c")
    plans = (("x", "y"), ("x", "y"), ("y", "x"), ("y", "x"))

    second = []
    for part in range(4):
        first[part].wait_recv()
        sums[part][...] = grads[part][:, :, :, mine] + core_recv[part][...].astype(jnp.float32)
        axis = plans[part][0]
        found = []
        for step in range(1, sizes[axis]):
            other = (here[axis] + step) % sizes[axis]
            piece = sums[part][:, :, other] if axis == "x" else sums[part][:, other]
            wide_send[part][step - 1] = low(piece)
            found.append(copy_to(wide_send[part].at[step - 1], wide_recv[part].at[step - 1], **{axis: other}))
        second.append(found)
    copies = share(small_slots[1], total(small_slots[0], "c", copies), "x")
    third = []
    for part in range(4):
        axis, later = plans[part]
        held = sums[part].at[:, :, here["x"]] if axis == "x" else sums[part].at[:, here["y"]]
        value = held[...]
        for step, copy in enumerate(second[part]):
            copy.wait_recv()
            value = value + wide_recv[part][step].astype(jnp.float32)
        held[...] = value
        found = []
        for step in range(1, sizes[later]):
            other = (here[later] + step) % sizes[later]
            mid_send[part][step - 1] = low(held[:, other])
            found.append(copy_to(mid_send[part].at[step - 1], mid_recv[part].at[step - 1], **{later: other}))
        third.append(found)
    copies = share(small_slots[2], total(small_slots[1], "x", copies), "y")
    fourth = []
    for part in range(4):
        axis, later = plans[part]
        held = sums[part].at[:, here["y"], here["x"]]
        value = held[...]
        for step, copy in enumerate(third[part]):
            copy.wait_recv()
            value = value + mid_recv[part][step].astype(jnp.float32)
        held[...] = value
        found = []
        for step in range(1, sizes["z"]):
            other = (here["z"] + step) % sizes["z"]
            last_send[part][step - 1] = low(held[other])
            found.append(copy_to(last_send[part].at[step - 1], last_recv[part].at[step - 1], z=other))
        fourth.append(found)
    copies = share(small_slots[3], total(small_slots[2], "y", copies), "z")
    square = jnp.zeros((1, 1), jnp.float32)
    for part in range(4):
        value = sums[part][here["z"], here["y"], here["x"]]
        for step, copy in enumerate(fourth[part]):
            copy.wait_recv()
            value = value + last_recv[part][step].astype(jnp.float32)
        shards[part][...] = value
        square = square + jnp.sum(value * value, keepdims=True)
    square = jnp.broadcast_to(square, (8, 128))
    for place, axis in enumerate("cxyz"):
        parts = share(square_slots[place], square, axis)
        if place == 0:
            whole = total(small_slots[3], "z", copies)
            small_out[...] = whole
            norm_square = jnp.sum(whole[:14] * whole[:14], keepdims=True)
        square = total(square_slots[place], axis, parts)
    square_out[...] = square + norm_square
    for copy in started:
        copy.wait_send()


def reduce_gradients(down_enc, up_enc, down_dec, up_dec, small, dp, vocab):
    sizes = grid_of(dp, vocab)
    grid = tuple(sizes[axis] for axis in "zyxc")
    whole = dp * vocab
    grads = [
        value.reshape(grid + (value.shape[0] // whole, value.shape[1]))
        for value in (down_enc, up_enc, down_dec, up_dec)
    ]
    z, y, x, c = grid
    tails = [value.shape[4:] for value in grads]
    vmem = pl.BlockSpec(memory_space=pltpu.VMEM)
    scratch = [pltpu.VMEM((z, y, x) + tail, jnp.float32) for tail in tails]
    for _ in range(2):
        scratch += [pltpu.VMEM((z, y, x) + tail, jnp.bfloat16) for tail in tails]
    for _ in range(2):
        scratch += [
            pltpu.VMEM(((x - 1, z, y) if place < 2 else (y - 1, z, x)) + tail, jnp.bfloat16)
            for place, tail in enumerate(tails)
        ]
    for _ in range(2):
        scratch += [
            pltpu.VMEM(((y - 1, z) if place < 2 else (x - 1, z)) + tail, jnp.bfloat16)
            for place, tail in enumerate(tails)
        ]
    for _ in range(2):
        scratch += [pltpu.VMEM((z - 1,) + tail, jnp.bfloat16) for tail in tails]
    scratch += [pltpu.VMEM((sizes[axis],) + small.shape, jnp.float32) for axis in "cxyz"]
    scratch += [pltpu.VMEM((sizes[axis], 8, 128), jnp.float32) for axis in "cxyz"]
    links = 6 * (x + y + z + c)
    scratch += [pltpu.SemaphoreType.DMA((links,)), pltpu.SemaphoreType.DMA((links,))]
    return pl.pallas_call(
        functools.partial(reduce_kernel, sizes),
        out_shape=[jax.ShapeDtypeStruct(tail, jnp.float32) for tail in tails]
        + [jax.ShapeDtypeStruct(small.shape, jnp.float32), jax.ShapeDtypeStruct((8, 128), jnp.float32)],
        in_specs=[vmem] * 5,
        out_specs=[vmem] * 6,
        scratch_shapes=scratch,
        compiler_params=pltpu.CompilerParams(
            collective_id=1, has_side_effects=True, vmem_limit_bytes=48 * 2**20
        ),
    )(*grads, small)


ORDERS = ("xzy", "yzx", "zyx", "xzy", "yzx", "zxy")
SEQUENCE = (
    ("norms", 0), ("attn_in", 0), ("attn_out", 0), ("down", 0), ("widen", 0), ("up", 0), ("narrow", 0),
    ("attn_in", 1), ("attn_out", 1), ("attn_in", 2), ("attn_out", 2), ("down", 1), ("widen", 1), ("up", 1),
    ("narrow", 1),
)
COLUMNS = {"norms": 128, "attn_in": 512, "attn_out": 512, "down": 512, "widen": 512, "up": 512, "narrow": 256}
LAG = 3.0
PACE = 0.7
HEADS = 16
LEN = 128
MICRO = 2
ROWS = 256
NORM_EPS = 1e-05
NEGATIVE = -1000000000.0
BRANCH_SCALE = 4.0


def hops_of(order, sizes):
    return [(axis, hop) for axis in order for hop in range(1, sizes[axis])]


def plan_units(shapes, names, devices):
    units, clock = [], 0.0
    for name, layer in SEQUENCE:
        if name not in names:
            continue
        rows, columns = shapes[name]
        step = min(COLUMNS[name], columns)
        for left in range(0, columns, step):
            units.append((name, layer, left, step, clock))
            clock += rows * devices * step / 2**19
    return units


def dot(left, right):
    return jnp.dot(left, right, preferred_element_type=jnp.float32)


def dot_rows(left, right):
    return lax.dot_general(left, right, (((1,), (1,)), ((), ())), preferred_element_type=jnp.float32)


def dot_columns(left, right):
    return lax.dot_general(left, right, (((0,), (0,)), ((), ())), preferred_element_type=jnp.float32)


def low(value):
    return value.astype(jnp.bfloat16)


def wide(value):
    return value.astype(jnp.float32)


def norm_rows(value, gain, bias):
    centred = value - jnp.mean(value, -1, keepdims=True)
    inv_std = lax.rsqrt(jnp.mean(centred * centred, -1, keepdims=True) + NORM_EPS)
    normed = centred * inv_std
    return normed * gain + bias, normed, inv_std


def gelu_pair(value):
    half = 0.5 * (1.0 + lax.erf(value * 0.7071067811865476))
    return value * half, half + value * jnp.exp(-0.5 * value * value) * 0.3989422804014327


def lane_masks():
    lanes = lax.broadcasted_iota(jnp.int32, (LEN, 128), 1)
    first = (lanes < 64).astype(jnp.float32).astype(jnp.bfloat16)
    return first, (lanes >= 64).astype(jnp.float32).astype(jnp.bfloat16)


def stack_heads(value, masks):
    return jnp.concatenate([value * masks[0], value * masks[1]], 0)


def attend_pair(qkv, probs, attended, seq, pair, keep):
    masks = lane_masks()
    rows = pl.ds(pl.multiple_of(seq * LEN, LEN), LEN)

    def columns(part):
        return pl.ds(pl.multiple_of(part * 1024 + pair * 128, 128), 128)

    queries, keys, values = (qkv[rows, columns(part)] for part in range(3))
    scores = dot_rows(stack_heads(queries, masks), keys) * 0.125
    scores = jnp.where(keep(seq), scores, NEGATIVE)
    spread = jnp.exp(scores - jnp.max(scores, -1, keepdims=True))
    chance = low(spread / jnp.sum(spread, -1, keepdims=True))
    probs[seq, pair] = chance
    side = jnp.concatenate([chance[:LEN], chance[LEN:]], 1)
    attended[rows, columns(0)] = low(dot(side, stack_heads(values, masks)))


def forward_kernel(sizes, units, names, *refs):
    refs = list(refs)

    def take(count):
        found = refs[:count]
        del refs[:count]
        return found

    count = len(names)
    ins = dict(zip(names, take(count)))
    picked, places, key_keep = take(3)
    extra_up = None if "up" in names else take(1)[0]
    outs = dict(zip(names, take(count)))
    saved_out = take(8)
    send_sem, recv_sem, local_sem, sib_send, sib_recv = take(5)
    saved = take(8)
    qkv_all, probs_all, normed_all, inv_all, feed_in, slopes, bottles, decoded = saved
    embed_sem, embed_here, embed_core, embed_line = take(4)
    norm_tile, norms = take(2)
    stream, stream_low, memory, attended, branch, hidden = take(6)
    tiles, tall_tiles, tile_sem, tall_sem, save_sem = take(5)
    here = position(sizes)

    def at_device(**moved):
        return device_at(here, sizes, **moved)

    barrier = pltpu.get_barrier_semaphore()
    pl.semaphore_signal(barrier, inc=1, device_id=at_device(c=1 - here["c"]), device_id_type=MESH_ID)
    peers = jnp.int32(1)
    for step in range(1, sizes["x"]):
        other = (here["x"] + step) % sizes["x"]
        pl.semaphore_signal(barrier, inc=1, device_id=at_device(x=other), device_id_type=MESH_ID)
        peers = peers + 1
    for axis in "zy":
        for step in (-1, 1):
            ok = (here[axis] + step >= 0) & (here[axis] + step < sizes[axis])
            peers = peers + ok.astype(jnp.int32)

            @pl.when(ok)
            def _(axis=axis, step=step):
                pl.semaphore_signal(
                    barrier, inc=1, device_id=at_device(**{axis: here[axis] + step}), device_id_type=MESH_ID
                )

    pl.semaphore_wait(barrier, peers)

    everything = slice(None)

    def own_source(unit):
        name, layer, left, width, _ = unit
        return ins[name].at[layer, :, pl.ds(left, width)]

    def piece(unit, index):
        name, layer, left, width, _ = unit
        return outs[name].at[(layer,) + index + (everything, pl.ds(left, width))]

    def view(unit, order, axis, coordinate):
        place = order.index(axis)
        at = {other: everything if order.index(other) < place else here[other] for other in "zyx"}
        at[axis] = coordinate
        return piece(unit, (at["z"], at["y"], at["x"], here["c"]))

    def sends(number, stage):
        unit, order = units[number], ORDERS[number % len(ORDERS)]
        axis, hop = hops_of(order, sizes)[stage]
        size, mine = sizes[axis], here[axis]
        first = order.index(axis) == 0
        found = []
        for way, step in enumerate((1, -1)):
            origin = mine - step * (hop - 1)
            ok = (origin >= 0) & (origin < size) & (mine + step >= 0) & (mine + step < size)
            origin_r = mine - step * hop
            ok_r = (origin_r >= 0) & (origin_r < size)

            def build(receive, step=step, way=way, origin=origin, origin_r=origin_r):
                which = origin_r if receive else origin
                fresh = first and hop == 1 and not receive
                return pltpu.make_async_remote_copy(
                    src_ref=own_source(unit) if fresh else view(unit, order, axis, which),
                    dst_ref=view(unit, order, axis, which),
                    send_sem=send_sem.at[number, stage * 2 + way],
                    recv_sem=recv_sem.at[number, stage * 2 + way],
                    device_id=at_device(**{axis: mine + step}),
                    device_id_type=MESH_ID,
                )

            found.append((ok, ok_r, build))
        return found

    def local_copy(number):
        index = tuple(here[axis] for axis in "zyxc")
        return pltpu.make_async_copy(own_source(units[number]), piece(units[number], index), local_sem.at[number])

    def sibling(number):
        plane = piece(units[number], (everything, everything, everything, here["c"]))
        return pltpu.make_async_remote_copy(
            src_ref=plane,
            dst_ref=plane,
            send_sem=sib_send.at[number],
            recv_sem=sib_recv.at[number],
            device_id=at_device(c=1 - here["c"]),
            device_id_type=MESH_ID,
        )

    depth = sum(sizes[axis] - 1 for axis in "zyx")

    def comm_step(number, stage):
        if stage == 0:
            local_copy(number).start()
        if 1 <= stage <= depth:
            for _, ok_r, build in sends(number, stage - 1):

                @pl.when(ok_r)
                def _(build=build):
                    build(True).wait_recv()

        if stage == sizes[ORDERS[number % len(ORDERS)][0]] - 1:
            local_copy(number).wait()
        if stage < depth:
            for ok, _, build in sends(number, stage):

                @pl.when(ok)
                def _(build=build):
                    build(False).start()

        if stage == depth:
            sibling(number).start()
        if stage == depth + 1:
            sibling(number).wait_recv()

    mine, column = here["c"], here["x"]

    def embed_first(group):
        return pltpu.make_async_remote_copy(
            src_ref=picked.at[:, 1 - mine, group],
            dst_ref=embed_core.at[group],
            send_sem=embed_sem.at[0, group],
            recv_sem=embed_sem.at[1, group],
            device_id=at_device(c=1 - mine),
            device_id_type=MESH_ID,
        )

    def embed_local(group):
        return pltpu.make_async_copy(picked.at[:, mine, group], embed_here.at[group], embed_sem.at[2, group])

    def embed_second(group, step):
        other = (column + step) % sizes["x"]
        return pltpu.make_async_remote_copy(
            src_ref=embed_here.at[group, other],
            dst_ref=embed_line.at[group, step - 1],
            send_sem=embed_sem.at[2 + step * 2 - 1, group],
            recv_sem=embed_sem.at[2 + step * 2, group],
            device_id=at_device(x=other),
            device_id_type=MESH_ID,
        )

    def embed_pass(group):
        embed_first(group).wait_recv()
        embed_local(group).wait()
        embed_here[group] = embed_here[group] + embed_core[group]
        for step in range(1, sizes["x"]):
            embed_second(group, step).start()

    def embed_rows(group):
        rows = wide(embed_here[group, column])
        for step in range(1, sizes["x"]):
            embed_second(group, step).wait_recv()
            rows = rows + wide(embed_line[group, step - 1])
        place = wide(places[group])
        return rows + jnp.concatenate([place] * MICRO, 0)

    saves = []

    def save(place, index):
        def build(number=len(saves)):
            return pltpu.make_async_copy(
                saved[place].at[index] if index else saved[place],
                saved_out[place].at[index] if index else saved_out[place],
                save_sem.at[number],
            )

        saves.append(build)
        build().start()

    def norm_step(value, which, side):
        result, normed, inv_std = norm_rows(value, norms[which : which + 1, :], norms[which + 7 : which + 8, :])
        normed_all[which] = normed
        inv_all[which] = jnp.broadcast_to(inv_std, (ROWS, 128))
        save(2, (which,))
        save(3, (which,))
        stream[side] = result
        stream_low[side] = low(result)

    def begin(side):
        def run():
            if side == 0:
                copy = pltpu.make_async_copy(outs["norms"].at[0], norm_tile, tile_sem.at[len(tiles_used)])
                copy.start()
                copy.wait()
                columns = norm_tile[...].reshape(-1, 128)
                norms[...] = columns.T[:16]
            norm_step(embed_rows(side), 3 * side, side)

        return run

    tiles_used = [None] * tiles.shape[0]

    def project(which, left, side, from_memory):
        def run(tile):
            source = memory[...] if from_memory else stream_low[side]
            qkv_all[which, :, pl.ds(left, 512)] = low(dot(source, tile()))

        return run

    def attention(which, start, keep):
        def run():
            def body(number, _):
                seq, pair = number // 8, number % 8
                attend_pair(qkv_all.at[which], probs_all.at[which], attended, seq, pair, keep)
                return 0

            lax.fori_loop(start, start + 4, body, 0)

        return run

    def project_out(left):
        def run(tile):
            branch[:, pl.ds(left, 512)] = dot(attended[...], tile())

        return run

    def finish_attention(which, norm, side):
        def run():
            save(0, (which,))
            save(1, (which,))
            norm_step(stream[side] + branch[...], norm, side)

        return run

    def narrow_down(side):
        def run(tile):
            feed_in[side] = stream_low[side]
            value, slope = gelu_pair(dot(stream_low[side], tile()))
            bottles[side, 0] = low(value)
            bottles[side, 1] = low(slope)
            save(4, (side,))
            save(6, (side,))

        return run

    def widen(left, side):
        def run(tile):
            value, slope = gelu_pair(dot(stream_low[side], tile()))
            hidden[:, pl.ds(left, 512)] = low(value)
            slopes[side, :, pl.ds(left, 512)] = low(slope)

        return run

    def raise_up(left, side):
        def run(tile):
            branch[:, pl.ds(left, 512)] = BRANCH_SCALE * dot(bottles[side, 0], tile())

        return run

    def narrow(left, side):
        def run(tile):
            branch[:, pl.ds(left, 256)] += dot(hidden[...], tile())

        return run

    def finish_feed(norm, side):
        def run():
            save(5, (side,))
            norm_step(stream[side] + branch[...], norm, side)
            if side == 0:
                memory[...] = stream_low[0]
            else:
                decoded[...] = stream_low[1]
                save(7, ())

        return run

    def source_keep(seq):
        return jnp.broadcast_to(key_keep[seq, 0:1, :] > 0.0, (2 * LEN, LEN))

    def causal_keep(seq):
        query = lax.broadcasted_iota(jnp.int32, (2 * LEN, LEN), 0) % LEN
        return lax.broadcasted_iota(jnp.int32, (2 * LEN, LEN), 1) <= query

    steps = []
    unit_of = {}
    for number, unit in enumerate(units):
        unit_of[unit[:3]] = number

    def add(run, cost, unit=None, clock=0.0):
        steps.append((unit, cost, clock, run))

    def attention_steps(which, norm, side, keep):
        for left in range(0, 3072, 512):
            from_memory = which == 2 and left >= 1024
            add(project(which, left, side, from_memory), 0.6, unit_of["attn_in", which, left])
        for start in range(0, 16, 4):
            add(attention(which, start, keep), 2.0)
        for left in range(0, 1024, 512):
            add(project_out(left), 0.6, unit_of["attn_out", which, left])
        add(finish_attention(which, norm, side), 1.0)

    def feed_steps(norm, side):
        add(narrow_down(side), 1.3, unit_of["down", side, 0])
        for left in range(0, 4096, 512):
            add(widen(left, side), 1.3, unit_of["widen", side, left])
        for left in range(0, 1024, 512):
            if "up" in names:
                add(raise_up(left, side), 0.4, unit_of["up", side, left])
            else:
                part = functools.partial(lambda left, side: extra_up[side, :, pl.ds(left, 512)], left, side)
                add(functools.partial(raise_up(left, side), part), 0.4)
        for left in range(0, 1024, 256):
            add(narrow(left, side), 1.0, unit_of["narrow", side, left])
        add(finish_feed(norm, side), 1.0)

    add(begin(0), 2.0, unit_of["norms", 0, 0], 8.0)
    attention_steps(0, 1, 0, source_keep)
    feed_steps(2, 0)
    add(begin(1), 1.5, None, 20.0)
    attention_steps(1, 4, 1, causal_keep)
    attention_steps(2, 5, 1, source_keep)
    feed_steps(6, 1)

    loads = [step[0] for step in steps if isinstance(step[0], int) and units[step[0]][0] != "norms"]
    slot_of, rings = {}, {"tall": [], "flat": []}
    for unit in loads:
        kind = "tall" if units[unit][0] == "narrow" else "flat"
        ring = rings[kind]
        size = (tall_tiles if kind == "tall" else tiles).shape[0]
        slot_of[unit] = (kind, len(ring) % size, ring[len(ring) - size] if len(ring) >= size else None)
        ring.append(unit)

    def tile_parts(unit):
        kind, slot, _ = slot_of[unit]
        name, layer, left, width, _ = units[unit]
        source = outs[name].at[layer, :, :, :, :, :, pl.ds(left, width)]
        buffer = (tall_tiles if kind == "tall" else tiles).at[slot]
        sem = (tall_sem if kind == "tall" else tile_sem).at[slot]
        rows = ins[name].shape[1] * sizes["z"] * sizes["y"] * sizes["x"] * sizes["c"]
        target = buffer.at[pl.ds(0, rows)]
        shape = tuple(sizes[axis] for axis in "zyxc") + (ins[name].shape[1], width)
        return pltpu.make_async_copy(source, target.reshape(shape), sem), target

    complete, loaded, done = set(), set(), set()
    waiting = list(loads)

    def try_loads():
        while waiting:
            unit = waiting[0]
            before = slot_of[unit][2]
            if unit not in complete or (before is not None and before not in done):
                return
            tile_parts(unit)[0].start()
            loaded.add(unit)
            waiting.pop(0)

    queue = list(steps)

    def run_step():
        unit, cost, _, run = queue.pop(0)
        if unit is None or units[unit][0] == "norms":
            run()
        else:
            copy, target = tile_parts(unit)
            copy.wait()
            run(lambda: target[...])
            done.add(unit)
        try_loads()
        return cost

    def ready(clock):
        if not queue:
            return False
        unit, _, earliest, _ = queue[0]
        if earliest > clock:
            return False
        if unit is None:
            return True
        return unit in complete if units[unit][0] == "norms" else unit in loaded

    for group in range(2):
        embed_first(group).start()
        embed_local(group).start()
    events = sorted(
        (unit[4] + LAG * stage, -stage, number) for number, unit in enumerate(units) for stage in range(depth + 2)
    )
    embed_done, credit, last = [], 0.0, 0.0
    for clock, minus, number in events:
        stage = -minus
        comm_step(number, stage)
        for group in range(2):
            if group not in embed_done and clock >= 1.5 + 1.5 * group:
                embed_done.append(group)
                embed_pass(group)
        if stage == depth + 1:
            complete.add(number)
            try_loads()
        credit = min(credit + 3.7 * PACE * (clock - last) , 4.0)
        last = clock
        while ready(clock) and credit > 0.0:
            credit -= run_step()
    while queue:
        run_step()
    for build in saves:
        build().wait()
    for group in range(2):
        embed_first(group).wait_send()
        for step in range(1, sizes["x"]):
            embed_second(group, step).wait_send()
    for number in range(len(units)):
        sibling(number).wait_send()
        for stage in range(depth):
            for ok, _, build in sends(number, stage):

                @pl.when(ok)
                def _(build=build):
                    build(False).wait_send()


def run_forward(arrays, picked, places, key_keep, dp, vocab):
    sizes = grid_of(dp, vocab)
    devices = dp * vocab
    grid = tuple(sizes[axis] for axis in "zyxc")
    extra = []
    arrays = dict(arrays)
    if arrays["up"].shape[1] % 8:
        extra = [lax.all_gather(arrays.pop("up"), ("dp", "vocab"), axis=1, tiled=True)]
    names = list(arrays)
    shapes = {name: arrays[name].shape[1:] for name in names}
    units = plan_units(shapes, names, devices)
    depth = sum(sizes[axis] - 1 for axis in "zyx")
    anywhere, vmem = pl.BlockSpec(memory_space=pl.ANY), pl.BlockSpec(memory_space=pltpu.VMEM)
    f32, b16 = jnp.float32, jnp.bfloat16
    saved = [
        ((3, ROWS, 3072), b16),
        ((3, MICRO, 8, 2 * LEN, LEN), b16),
        ((7, ROWS, 1024), f32),
        ((7, ROWS, 128), f32),
        ((2, ROWS, 1024), b16),
        ((2, ROWS, 4096), b16),
        ((2, 2, ROWS, 512), b16),
        ((ROWS, 1024), b16),
    ]
    out_shape = [
        jax.ShapeDtypeStruct((arrays[name].shape[0],) + grid + arrays[name].shape[1:], arrays[name].dtype)
        for name in names
    ] + [jax.ShapeDtypeStruct(shape, kind) for shape, kind in saved]
    x, n = sizes["x"], len(units)
    dma = pltpu.SemaphoreType.DMA
    out = pl.pallas_call(
        functools.partial(forward_kernel, sizes, units, names),
        out_shape=out_shape,
        in_specs=[anywhere] * (len(names) + 1) + [vmem] * (2 + len(extra)),
        out_specs=[anywhere] * len(out_shape),
        scratch_shapes=[dma((n, 2 * depth)), dma((n, 2 * depth)), dma((n,)), dma((n,)), dma((n,))]
        + [pltpu.VMEM(shape, kind) for shape, kind in saved]
        + [
            dma((3 + 2 * x, 2)),
            pltpu.VMEM((2, x, ROWS, 1024), b16),
            pltpu.VMEM((2, x, ROWS, 1024), b16),
            pltpu.VMEM((2, x - 1, ROWS, 1024), b16),
            pltpu.VMEM(grid + arrays["norms"].shape[1:], f32),
            pltpu.VMEM((16, 1024), f32),
            pltpu.VMEM((2, ROWS, 1024), f32),
            pltpu.VMEM((2, ROWS, 1024), b16),
            pltpu.VMEM((ROWS, 1024), b16),
            pltpu.VMEM((ROWS, 1024), b16),
            pltpu.VMEM((ROWS, 1024), f32),
            pltpu.VMEM((ROWS, 4096), b16),
            pltpu.VMEM((4, 1024, 512), b16),
            pltpu.VMEM((2, 4096, 256), b16),
            dma((5,)),
            dma((2,)),
            dma((32,)),
        ],
        compiler_params=pltpu.CompilerParams(
            collective_id=0, has_side_effects=True, vmem_limit_bytes=61 * 2**20
        ),
    )(*[arrays[name] for name in names], picked, places, key_keep, *extra)
    held = dict(zip(names, out[: len(names)]))
    held = {name: value.reshape(value.shape[0], -1, value.shape[-1]) for name, value in held.items()}
    if extra:
        held["up"] = extra[0]
    return held, out[len(names) :]


def attend_back(grad_low, queries, key_rows, values, probs, scale):
    grad_heads = split_heads(grad_low)
    grad_probs = jnp.einsum(
        "bqhd,bkhd->bhqk", grad_heads, split_heads(values), preferred_element_type=jnp.float32
    )
    grad_values = jnp.einsum("bhqk,bqhd->bkhd", probs, grad_heads, preferred_element_type=jnp.float32)
    probs = wide(probs)
    grad_scores = low(probs * (grad_probs - jnp.sum(probs * grad_probs, -1, keepdims=True)))
    grad_queries = (
        jnp.einsum("bhqk,bkhd->bqhd", grad_scores, split_heads(key_rows), preferred_element_type=jnp.float32)
        * scale
    )
    grad_keys = (
        jnp.einsum("bhqk,bqhd->bkhd", grad_scores, split_heads(queries), preferred_element_type=jnp.float32)
        * scale
    )
    return tuple(value.reshape(ROWS, -1) for value in (grad_queries, grad_keys, grad_values))


def split_heads(value):
    return value.reshape(MICRO, LEN, HEADS, value.shape[1] // HEADS)


def norm_back(grad_out, normed, inv_std, norm_gain):
    scaled = grad_out * norm_gain
    grad_in = inv_std * (
        scaled
        - jnp.mean(scaled, -1, keepdims=True)
        - normed * jnp.mean(scaled * normed, -1, keepdims=True)
    )
    return grad_in, jnp.sum(grad_out * normed, 0), jnp.sum(grad_out, 0)


def backward(grad_decoded, held, norms, saved):
    qkv_all, probs_all, normed_all, inv_all, feed_in, slopes, bottles = saved
    gains, biases = [None] * 7, [None] * 7

    def norm(grad, which):
        grad, gains[which], biases[which] = norm_back(grad, normed_all[which], inv_all[which, :, :1], norms[which])
        return grad

    def feed(grad, side, which):
        grad_sum = norm(grad, which)
        low_grad = low(grad_sum)
        grad_hidden = low(dot_rows(low_grad, held["narrow"][side]) * wide(slopes[side]))
        grad_bottle = low(BRANCH_SCALE * dot_rows(low_grad, held["up"][side]) * wide(bottles[side, 1]))
        grad_in = grad_sum + dot_rows(grad_hidden, held["widen"][side]) + dot_rows(grad_bottle, held["down"][side])
        grad_up = BRANCH_SCALE * dot_columns(bottles[side, 0], low_grad)
        return grad_in, dot_columns(feed_in[side], grad_bottle), grad_up

    def attend(grad, layer, which):
        grad_sum = norm(grad, which)
        grad_att = low(dot_rows(low(grad_sum), held["attn_out"][layer]))
        qkv = qkv_all[layer]
        probs = probs_all[layer].reshape(MICRO, HEADS, LEN, LEN)
        parts = attend_back(grad_att, qkv[:, :1024], qkv[:, 1024:2048], qkv[:, 2048:], probs, 0.125)
        packed = low(jnp.concatenate(parts, 1))
        w_in = held["attn_in"][layer]
        if layer == 2:
            return grad_sum + dot_rows(packed[:, :1024], w_in[:, :1024]), dot_rows(packed[:, 1024:], w_in[:, 1024:])
        return grad_sum + dot_rows(packed, w_in), None

    grad, down_dec, up_dec = feed(grad_decoded, 1, 6)
    grad, grad_memory = attend(grad, 2, 5)
    grad, _ = attend(grad, 1, 4)
    norm(grad, 3)
    grad, down_enc, up_enc = feed(grad_memory, 0, 2)
    grad, _ = attend(grad, 0, 1)
    norm(grad, 0)
    return down_enc, up_enc, down_dec, up_dec, jnp.stack(gains + biases)


def adam_step(weight, first, second, grad, rate):
    first = BETA_FIRST * first + (1.0 - BETA_FIRST) * grad
    second = BETA_SECOND * second + (1.0 - BETA_SECOND) * grad * grad
    first_hat = first / (1.0 - BETA_FIRST**STEP)
    second_hat = second / (1.0 - BETA_SECOND**STEP)
    weight = weight - rate * (
        first_hat / (jnp.sqrt(second_hat) + ADAM_EPSILON) + WEIGHT_DECAY * weight
    )
    return (first, second, weight)


def head(decoded, vocab_table, target_ids, target_length, seq_scale, groups, vocab_rank):
    rows_local = vocab_table.shape[0]
    key_index = jnp.arange(LEN)
    head_rows = lax.all_gather(decoded, "vocab", axis=0, tiled=True)
    logits = dot_rows(head_rows, vocab_table)
    local_target = target_ids.reshape(-1) - vocab_rank * rows_local
    target_hot = lax.broadcasted_iota(jnp.int32, logits.shape, 1) == local_target[:, None]
    target_logit = jnp.sum(jnp.where(target_hot, logits, 0.0), 1)
    local_max = jnp.max(logits, 1)
    row_max = lax.pmax(local_max, "vocab")
    row_total, row_target = lax.psum(
        (jnp.sum(jnp.exp(logits - row_max[:, None]), 1), target_logit), "vocab"
    )
    log_total = row_max + jnp.log(row_total)
    row_mask = (key_index[None, :] < target_length[:, None]).astype(jnp.float32)
    row_weight = (row_mask * seq_scale[:, None]).reshape(-1)
    row_loss = (log_total - row_target).reshape(-1, LEN) * row_mask
    own_loss = lax.dynamic_slice_in_dim(row_loss, vocab_rank * MICRO, MICRO)
    grad_logits = low(
        row_weight[:, None] * (jnp.exp(logits - log_total[:, None]) - target_hot.astype(jnp.float32))
    )
    grad_decoded = lax.psum_scatter(
        dot(grad_logits, vocab_table).astype(jnp.bfloat16), "vocab", scatter_dimension=0, tiled=True
    ).astype(jnp.float32)
    return grad_decoded, jnp.sum(own_loss, 1)


def local(
    source_ids,
    target_in,
    target_ids,
    source_length,
    target_length,
    task_ids,
    vocab_table,
    positions,
    attention_in,
    attention_out,
    widen_weight,
    narrow_weight,
    adapt_down,
    adapt_up,
    norm_params,
    down_first,
    down_second,
    up_first,
    up_second,
    norm_first,
    norm_second,
):
    dp, groups = lax.axis_size("dp"), lax.axis_size("vocab")
    vocab_rank = lax.axis_index("vocab")
    rows_local, width = vocab_table.shape
    joined_ids = (
        jnp.stack([source_ids.reshape(groups, -1), target_in.reshape(groups, -1)], 1).reshape(-1)
        - vocab_rank * rows_local
    )
    inside = (joined_ids >= 0) & (joined_ids < rows_local)
    picked = jnp.where(
        inside[:, None],
        jnp.take(vocab_table, jnp.clip(joined_ids, 0, rows_local - 1), axis=0),
        jnp.zeros((), jnp.bfloat16),
    ).reshape(groups // 2, 2, 2, ROWS, width)
    task_hot = (task_ids[:, None] == jnp.arange(TASKS)[None, :]).astype(jnp.float32)
    task_counts = lax.psum(jnp.sum(task_hot * target_length[:, None].astype(jnp.float32), 0), "dp")
    seq_scale = jnp.sum(task_hot * (1.0 / (TASKS * task_counts))[None, :], 1)
    own = vocab_rank * MICRO
    source_count = lax.dynamic_slice_in_dim(source_length, own, MICRO)
    key_keep = jnp.broadcast_to(
        (jnp.arange(LEN)[None, None, :] < source_count[:, None, None]).astype(jnp.float32), (MICRO, 8, LEN)
    )
    parts = {
        "norms": jnp.pad(norm_params.T, ((0, 0), (0, 114)))[None],
        "attn_in": attention_in,
        "attn_out": attention_out,
        "widen": widen_weight,
        "narrow": narrow_weight,
        "down": low(adapt_down),
        "up": low(adapt_up),
    }
    held, saved = run_forward(parts, picked, positions, key_keep, dp, groups)
    norms = held["norms"][0, :, :14].T
    decoded = saved[7]
    grad_decoded, own_loss = head(decoded, vocab_table, target_ids, target_length, seq_scale, groups, vocab_rank)
    task_local = jnp.sum(lax.dynamic_slice_in_dim(task_hot, own, MICRO) * own_loss[:, None], 0)
    down_enc, up_enc, down_dec, up_dec, norm_grads = backward(grad_decoded, held, norms, saved[:7])
    small = jnp.concatenate(
        [norm_grads, jnp.pad(task_local[None], ((0, 1), (0, width - TASKS)))], 0
    )
    down_enc, up_enc, down_dec, up_dec, small, square = reduce_gradients(
        down_enc, up_enc, down_dec, up_dec, small, dp, groups
    )
    shard_down = jnp.stack([down_enc, down_dec])
    shard_up = jnp.stack([up_enc, up_dec])
    full_norm, task_sums = small[:14], small[14, :TASKS]
    cut = norm_params.shape[1]
    shard_norm = lax.dynamic_slice_in_dim(full_norm, lax.axis_index(("dp", "vocab")) * cut, cut, 1)
    grad_norm = jnp.sqrt(square[0, 0])
    factor = CLIP_LIMIT / jnp.maximum(grad_norm, CLIP_LIMIT)
    down_new = adam_step(adapt_down, down_first, down_second, shard_down * factor, RATE_ADAPTER)
    up_new = adam_step(adapt_up, up_first, up_second, shard_up * factor, RATE_ADAPTER)
    norm_new = adam_step(norm_params, norm_first, norm_second, shard_norm * factor, RATE_NORMS)
    return (*down_new, *up_new, *norm_new, grad_norm, task_sums, task_counts)


def solution(mesh):
    return jax.shard_map(
        local,
        mesh=mesh,
        in_specs=(
            P("dp", None),
            P("dp", None),
            P("dp", None),
            P("dp"),
            P("dp"),
            P("dp"),
            P("vocab", None),
            P(),
            P(None, ("dp", "vocab"), None),
            P(None, ("dp", "vocab"), None),
            P(None, ("dp", "vocab"), None),
            P(None, ("dp", "vocab"), None),
            P(None, ("dp", "vocab"), None),
            P(None, ("dp", "vocab"), None),
            P(None, ("dp", "vocab")),
            P(None, ("dp", "vocab"), None),
            P(None, ("dp", "vocab"), None),
            P(None, ("dp", "vocab"), None),
            P(None, ("dp", "vocab"), None),
            P(None, ("dp", "vocab")),
            P(None, ("dp", "vocab")),
        ),
        out_specs=(
            P(None, ("dp", "vocab"), None),
            P(None, ("dp", "vocab"), None),
            P(None, ("dp", "vocab"), None),
            P(None, ("dp", "vocab"), None),
            P(None, ("dp", "vocab"), None),
            P(None, ("dp", "vocab"), None),
            P(None, ("dp", "vocab")),
            P(None, ("dp", "vocab")),
            P(None, ("dp", "vocab")),
            P(),
            P(),
            P(),
        ),
        check_vma=False,
    )
```

time: 1170 us -> 685 us (0.59)
  waiting for transfers between devices: 598 us -> 0.05 us
  Pallas kernels: 0 us -> 345 us
  matrix products: 312 us -> 120 us
  blocking collectives: 119 us -> 31.5 us
  local copies, waits for them, and re-layouts: 59.4 us -> 136 us
  other arithmetic: 52.6 us -> 26 us
    all_gather x8 -> x1, waiting for transfers between devices: 444 us -> 0.01 us  [head(): head_rows = lax.all_gather(decoded, 'vocab', axis=0, tiled=True)]
    pallas_call x0 -> x2, Pallas kernels: none -> 345 us  [the longest x1 294 us: run_forward(): pl.pallas_call(functools.partial(forward_kernel, sizes, units, names), ou...]
    dot_general x104 -> x31, matrix products: 312 us -> 120 us  [the longest x14 78.8 us: dot_rows(): lax.dot_general(left, right, (((1,), (1,)), ((), ())), preferred_element_...]
    psum x1 -> x0, waiting for transfers between devices: 119 us -> none  [local(): lax.psum((grad_down, grad_up, norm_grads, task_local), ('dp', 'vocab'))]
    all_gather x1 -> x0, blocking collectives: 45.2 us -> none  [local(): norms = lax.all_gather(norm_params, ('dp', 'vocab'), axis=1, tiled=True)]
    slice x25 -> x12, local copies, waits for them, and re-layouts: 12.6 us -> 56 us  [the longest x1 15.6 us: attend(): w_in = held['attn_in'][layer]]
    psum x2 -> x1, blocking collectives: 47.4 us -> 6.72 us  [head(): lax.psum((jnp.sum(jnp.exp(logits - row_max[:, None]), 1), target_logit),...]
    reshape x2 -> x15, local copies, waits for them, and re-layouts: 0.17 us -> 34.7 us  [split_heads(): return value.reshape(MICRO, LEN, HEADS, value.shape[1] // HEADS)]
  transfers between devices with their start and end apart: 12 -> 2, of which waited for: 9 -> 0; matrix products, arithmetic and copies ran while one was open for 10% -> 13% of each run, Pallas kernels for 0% -> 0%
where the time goes in v3:
time: 685 us; the launch traced here: 676 us
  Pallas kernels  345 us (50%)
  local copies, waits for them, and re-layouts  136 us (20%)
  matrix products  120 us (18%)
  blocking collectives  31.5 us (5%)
  other arithmetic  26 us (4%)
  between operations  17.3 us (3%)
    pallas_call x1, Pallas kernels, run_forward(): pl.pallas_call(functools.partial(forward_kernel, sizes, units, names), ou...  294 us
    dot_general x14, matrix products, dot_rows(): lax.dot_general(left, right, (((1,), (1,)), ((), ())), preferred_element_...  78.8 us
    pallas_call x1, Pallas kernels, reduce_gradients(): pl.pallas_call(functools.partial(reduce_kernel, sizes), out_shape=[jax.Sh...  50.8 us
    reshape x15, local copies, waits for them, and re-layouts, split_heads(): return value.reshape(MICRO, LEN, HEADS, value.shape[1] // HEADS)  34.7 us
    dot_general x1, matrix products, dot(): return jnp.dot(left, right, preferred_element_type=jnp.float32)  24.7 us
    psum x1, blocking collectives, local(): lax.psum(jnp.sum(task_hot * target_length[:, None].astype(jnp.float32), 0...  19.1 us
    gather x1, local copies, waits for them, and re-layouts, local(): jnp.take(vocab_table, jnp.clip(joined_ids, 0, rows_local - 1), axis=0)  17.4 us
    slice x1, local copies, waits for them, and re-layouts, attend(): w_in = held['attn_in'][layer]  15.6 us
  transfers between devices with their start and end apart: 2, of which 0 were waited for; matrix products, arithmetic and copies ran while one was open for 13% of the time, Pallas kernels for 0%

profile of v3, /device:TPU:0, one launch (start us, length us, event | category | flops | bytes accessed | tf_op | source)
XLA Modules:
  0.0 676.0 jit_solution(17091305243777094892)
XLA Ops:
  13.3 17.4 %gather_fusion = bf16[2048,1024]{1,0:T(8,128)(2,1)} fusion(bf16[6400,1024]{1,0:T(8,128)(2,1)} %param.27, s32[2048]{0:T(1024)S(1)} %broadcast_clamp_fusion), kind=kCustom, calls=%fused_computation | custom fusion | bytes 8396800 | tf_op jit(solution)/shard_map/jit(_take)/gather | solution.py:953
  30.8 4.0 select_select_fusion.refs_7_
  35.4 294.3 %shard_map.292 = (f32[1,4,2,2,2,32,128]{6,5,4,3,2,1,0:T(8,128)}, bf16[3,4,2,2,2,32,3072]{6,5,4,3,2,1,0:T(8,128)(2,1)}, bf16[3,4,2,2,2,32,1024]{6,5,4,3,2,1,0:T(8...) custom-call(f32[1,32,128]{2,1,0:T(8,128)} %pad_bitcast_fusion.refs_0, ...), custom_call_target="tpu_custom_call" | custom-call | tf_op jit(solution)/shard_map/pallas_call | solution.py:773
  330.0 4.7 slice_bitcast_fusion.1
  335.7 19.1 %psum.21 = f32[4]{0:T(128)S(1)} all-reduce(f32[4]{0:T(128)S(1)} %select_reduce_fusion.2), channel_id=1, replica_groups=mesh['dp'=8,'vocab'=4] {'dp'}, use_global_device_ids=true, to_apply=%region_1.2 | all-reduce | flops 4 | bytes 32 | tf_op jit(solution)/shard_map/psum | solution.py:957
  356.0 2.1 fusion.141
  359.8 2.6 fusion.146
  362.4 2.5 reshape.366
  364.8 2.5 reshape.365
  367.4 2.5 reshape.370
  369.9 2.0 copy.135
  373.2 3.3 fusion.144
  376.5 2.5 reshape.372
  379.0 2.5 reshape.373
  381.5 1.7 reshape.371
  391.1 3.2 fusion.143
  395.5 6.0 fusion.140
  401.5 22.7 %fusion.148 = (f32[1024]{0:T(1024)S(1)}, f32[1024,6400]{1,0:T(8,128)}) fusion(bf16[1024,1024]{1,0:T(8,128)(2,1)} %all-gather.2.cloned.1.call-done, bf16[6400,1024]{1,0:T(8,128)(2,1)} %param.27), kind=kOutput, calls=%fused_computation.247 | convolution fusion | flops 13428325376 | bytes 41422848 | tf_op jit(solution)/shard_map/dot_general | solution.py:264
  424.2 5.6 pmax.7
  429.9 10.3 %select_reduce_fusion = (f32[1024]{0:T(1024)S(1)}, f32[1024]{0:T(1024)S(1)}) fusion(f32[1024,6400]{1,0:T(8,128)} %get-tuple-element.140, s32[1024]{0:T(1024)S(1)} %subtract_bitcast_fusion, f32[1024]{0:T(1024)S(1)} %pmax.7), kind=kLoop, calls=%fused_computation.1 | loop fusion | flops 32765952 | bytes 26230784 | tf_op jit(solution)/shard_map/reduce_sum | solution.py:900
  440.1 6.7 all-reduce.2
  446.9 24.7 %fusion.16 = bf16[1024,1024]{1,0:T(8,128)(2,1)} fusion(bf16[6400,1024]{1,0:T(8,128)(2,1)} %param.27, f32[1024,6400]{1,0:T(8,128)} %get-tuple-element.140, s32[1024]{0:T(1024)S(1)} %subtract_bitcast_fusion, f32[1024]{0:T(1024)S(1)} %get-tuple-element.98, f32[1024]{0:T(1024)S(1)} %get-tuple-element.138), kind=kOutput, calls=%fused_computation.30 | convolution fusion | flops 13462142976 | bytes 41431040 | tf_op jit(solution)/shard_map/dot_general | solution.py:260
  471.6 15.6 %fusion.137 = (bf16[1,4,2,2,2,32,3072]{6,5,4,3,2,1,0:T(8,128)(2,1)}, bf16[1,4,2,2,2,32,3072]{6,5,4,3,2,1,0:T(8,128)(2,1)}, bf16[1,4,2,2,2,32,3072]{6,5,4,3,2,1,0:T(8,128)(2,1)}) fusion(bf16[3,4,2,2,2,32,3072]{6,5,4,3,2,1,0:T(8,128)(2,1)} %get-tuple-element.47), kind=kLoop, calls=%fused_computation.236 | loop fusion | bytes 37748736 | tf_op jit(solution)/shard_map/slice | solution.py:867
  487.3 13.6 %fusion.138 = (bf16[1,4,2,2,2,128,1024]{6,5,4,3,2,1,0:T(8,128)(2,1)}, bf16[1,4,2,2,2,128,1024]{6,5,4,3,2,1,0:T(8,128)(2,1)}) fusion(bf16[2,4,2,2,2,128,1024]{6,5,4,3,2,1,0:T(8,128)(2,1)} %get-tuple-element.40), kind=kLoop, calls=%fused_computation.237 | loop fusion | bytes 33554432 | tf_op jit(solution)/shard_map/slice | solution.py:854
  500.9 6.5 fusion.139
  507.7 1.8 fusion.63
  509.5 2.3 fusion.59
  511.8 13.4 %convolution_add_fusion.3 = f32[256,1024]{1,0:T(8,128)} fusion(bf16[1024,4096]{1,0:T(8,128)(2,1)} %bitcast.345, bf16[4096,1024]{1,0:T(8,128)(2,1)} %bitcast.344, bf16[2,256,4096]{2,1,0:T(8,128)(2,1)} %get-tuple-element.41, f32[256]{0:T(256)S(1)} %get-tuple-element.150, f32[7,256,1024]{2,1,0:T(8,128)} %get-tuple-element.39, f32[256]{0:T(256)S(1)} %get-tuple-element.151, ...), kind=kOutput, calls=%fused_computation.66 | convolution fusion | flops 4301783040 | bytes 23083008 | tf_op jit(solution)/shard_map/dot_general | solution.py:264
  525.2 2.2 fusion.95
  528.4 2.9 convolution_convert_fusion.5
  531.3 2.8 reshape.374
  534.0 2.0 copy.128
  542.5 3.4 fusion.75
  545.9 1.9 fusion.88
  547.9 1.8 convolution_multiply_fusion.3
  550.2 1.7 fusion.102.refs_2_
  551.9 3.0 convolution_convert_fusion.1
  554.9 2.7 reshape.376
  557.7 2.8 copy.159
  569.3 11.9 %convolution_add_fusion.2 = f32[256,1024]{1,0:T(8,128)} fusion(f32[256,1024]{1,0:T(8,128)S(1)} %fusion.88, bf16[1024,4096]{1,0:T(8,128)(2,1)} %bitcast.343, bf16[4096,1024]{1,0:T(8,128)(2,1)} %bitcast.342, bf16[2,256,4096]{2,1,0:T(8,128)(2,1)} %get-tuple-element.41), kind=kOutput, calls=%fused_computation.65 | convolution fusion | flops 4298637312 | bytes 22020096 | tf_op jit(solution)/shard_map/dot_general | solution.py:264
  581.2 5.9 fusion.35
  587.1 2.8 fusion.85
  590.9 2.9 convolution_convert_fusion.3
  593.8 2.5 reshape.375
  596.3 2.8 copy.140
  605.4 3.7 fusion.133
  609.2 3.4 convolution_multiply_fusion.2
  612.7 50.8 %shard_map.293 = (f32[32,512]{1,0:T(8,128)S(1)}, f32[16,1024]{1,0:T(8,128)S(1)}, f32[32,512]{1,0:T(8,128)S(1)}, f32[16,1024]{1,0:T(8,128)S(1)}, f32[16,1024]{1,0:T(8,128)S(1)}, /*index=5*/f32[8,128]{1,0:T(8,128)S(1)}) custom-call(f32[4,2,2,2,32,512]{5,4,3,2,1,0:T(8,128)S(1)} %fusion.104.refs_0_, f32[4,2,2,2,16,1024]{5,4,3,2,1,0:T(8,128)S(1)} %bitcast.323, ...), custom_call_target="tpu_custom_call" | custom-call | tf_op jit(solution)/shard_map/pallas_call | solution.py:211
  (233 shorter events, 48.8 us)
Async XLA Ops:
  7.2 394.3 %all-gather.2.cloned.1.call-start = ((), (), s32[]{:S(2)}) async-start(), calls=%async_computation.1 | async-start | bytes 2621440 | tf_op jit(solution)/shard_map/all_gather | solution.py:896
  13.3 17.4 %copy-start.50 = (s32[8,128]{1,0:T(8,128)S(1)}, s32[8,128]{1,0:T(8,128)}, u32[]{:S(2)}) copy-start(s32[8,128]{1,0:T(8,128)} %param.22) | copy-start | bytes 12292
  13.3 17.4 %copy-start.51 = (s32[8,128]{1,0:T(8,128)S(1)}, s32[8,128]{1,0:T(8,128)}, u32[]{:S(2)}) copy-start(s32[8,128]{1,0:T(8,128)} %param.21) | copy-start | bytes 12292
  34.8 295.2 %copy-start.60 = (s32[8]{0:T(128)S(1)}, s32[8]{0:T(128)}, u32[]{:S(2)}) copy-start(s32[8]{0:T(128)} %param.25) | copy-start | bytes 100
  329.7 177.9 %reduce-scatter.2.cloned.1.call-start = ((), (), s32[]{:S(2)}) async-start(), calls=%async_computation.2 | async-start | bytes 2621440 | tf_op jit(solution)/shard_map/reduce_scatter | solution.py:914
  330.0 4.8 copy-start.59
  330.0 4.9 copy-start.33
  330.0 25.9 %copy-start.41 = (f32[1,4,2,2,2,32,128]{6,5,4,3,2,1,0:T(8,128)S(1)}, f32[1,4,2,2,2,32,128]{6,5,4,3,2,1,0:T(8,128)}, u32[]{:S(2)}) copy-start(f32[1,4,2,2,2,32,128]{6,5,4,3,2,1,0:T(8,128)} %get-tuple-element.38) | copy-start | bytes 1572868
  354.8 34.6 %copy-start.61 = (f32[4]{0:T(128)}, f32[4]{0:T(128)S(1)}, u32[]{:S(2)}) copy-start(f32[4]{0:T(128)S(1)} %psum.21) | copy-start | bytes 52
  358.1 9.3 %copy-start.5 = (bf16[1,2,8,256,128]{4,3,2,1,0:T(8,128)(2,1)}, bf16[1,2,8,256,128]{4,3,2,1,0:T(8,128)(2,1)S(1)}, u32[]{:S(2)}) copy-start(bf16[1,2,8,256,128]{4,3,2,1,0:T(8,128)(2,1)S(1)} %get-tuple-element.114) | copy-start | bytes 3145732
  358.1 13.8 %copy-start.3 = (bf16[1,2,8,256,128]{4,3,2,1,0:T(8,128)(2,1)}, bf16[1,2,8,256,128]{4,3,2,1,0:T(8,128)(2,1)S(1)}, u32[]{:S(2)}) copy-start(bf16[1,2,8,256,128]{4,3,2,1,0:T(8,128)(2,1)S(1)} %get-tuple-element.113) | copy-start | bytes 3145732
  358.1 25.1 %copy-start.1 = (bf16[1,2,8,256,128]{4,3,2,1,0:T(8,128)(2,1)}, bf16[1,2,8,256,128]{4,3,2,1,0:T(8,128)(2,1)S(1)}, u32[]{:S(2)}) copy-start(bf16[1,2,8,256,128]{4,3,2,1,0:T(8,128)(2,1)S(1)} %get-tuple-element.112) | copy-start | bytes 3145732
  381.5 9.0 %copy-start.56 = (s32[8,128]{1,0:T(8,128)S(1)}, s32[8,128]{1,0:T(8,128)}, u32[]{:S(2)}) copy-start(s32[8,128]{1,0:T(8,128)} %param.23) | copy-start | bytes 12292
  384.5 5.1 copy-start.42
  389.4 4.9 copy-start.30
  471.6 29.3 %slice-start = ((s8[16777216]{0:T(1024)(128)(4,1)}), s8[4194304]{0:T(1024)(128)(4,1)S(1)}, s32[]{:S(2)}) async-start(s8[16777216]{0:T(1024)(128)(4,1)} %bitcast.330), calls=%async_computation.3 | async-start | bytes 8388608
  471.6 29.3 %slice-start.1 = ((s8[16777216]{0:T(1024)(128)(4,1)}), s8[4194304]{0:T(1024)(128)(4,1)S(1)}, s32[]{:S(2)}) async-start(s8[16777216]{0:T(1024)(128)(4,1)} %bitcast.330), calls=%async_computation.4 | async-start | bytes 8388608
  471.6 29.3 %slice-start.2 = ((s8[16777216]{0:T(1024)(128)(4,1)}), s8[4194304]{0:T(1024)(128)(4,1)S(1)}, s32[]{:S(2)}) async-start(s8[16777216]{0:T(1024)(128)(4,1)} %bitcast.330), calls=%async_computation.5 | async-start | bytes 8388608
  487.3 13.6 %slice-start.3 = ((s8[16777216]{0:T(1024)(128)(4,1)}), s8[4194304]{0:T(1024)(128)(4,1)S(1)}, s32[]{:S(2)}) async-start(s8[16777216]{0:T(1024)(128)(4,1)} %bitcast.330), calls=%async_computation.6 | async-start | bytes 8388608
  511.8 13.4 %copy-start.36 = (bf16[256,512]{1,0:T(8,128)(2,1)}, bf16[256,512]{1,0:T(8,128)(2,1)S(1)}, u32[]{:S(2)}) copy-start(bf16[256,512]{1,0:T(8,128)(2,1)S(1)} %fusion.59) | copy-start | bytes 786436
  527.4 8.6 %copy-start.6 = (bf16[1,2,8,256,128]{4,3,2,1,0:T(8,128)(2,1)S(1)}, bf16[1,2,8,256,128]{4,3,2,1,0:T(8,128)(2,1)}, u32[]{:S(2)}) copy-start(bf16[1,2,8,256,128]{4,3,2,1,0:T(8,128)(2,1)} %copy-done.5) | copy-start | bytes 3145732
  531.3 5.9 copy-start.9
  542.4 5.4 copy-start.38
  545.9 6.0 copy-start.34
  545.9 3.8 copy-start.25
  545.9 4.2 copy-start.32
  545.9 4.2 copy-start.37
  547.8 4.1 copy-start.11
  547.8 4.1 copy-start.58
  551.9 8.6 %copy-start.4 = (bf16[1,2,8,256,128]{4,3,2,1,0:T(8,128)(2,1)S(1)}, bf16[1,2,8,256,128]{4,3,2,1,0:T(8,128)(2,1)}, u32[]{:S(2)}) copy-start(bf16[1,2,8,256,128]{4,3,2,1,0:T(8,128)(2,1)} %copy-done.3) | copy-start | bytes 3145732
  554.9 8.5 %copy-start.8 = (bf16[2,16,128,128]{2,3,1,0:T(8,128)(2,1)S(1)}, bf16[2,16,128,128]{2,3,1,0:T(8,128)(2,1)}, u32[]{:S(2)}) copy-start(bf16[2,16,128,128]{2,3,1,0:T(8,128)(2,1)} %copy.156) | copy-start | bytes 3145732
  564.7 4.2 copy-start.31
  581.2 5.9 copy-start.26
  581.2 5.9 copy-start.35
  581.2 5.9 copy-start.47
  587.1 3.8 copy-start.10
  587.1 3.8 copy-start.57
  589.9 9.2 %copy-start.2 = (bf16[1,2,8,256,128]{4,3,2,1,0:T(8,128)(2,1)S(1)}, bf16[1,2,8,256,128]{4,3,2,1,0:T(8,128)(2,1)}, u32[]{:S(2)}) copy-start(bf16[1,2,8,256,128]{4,3,2,1,0:T(8,128)(2,1)} %copy-done.1) | copy-start | bytes 3145732
  605.4 3.8 copy-start.29
  612.6 52.7 %copy-start.39 = (f32[2,32,512]{2,1,0:T(8,128)S(1)}, f32[2,32,512]{2,1,0:T(8,128)}, u32[]{:S(2)}) copy-start(f32[2,32,512]{2,1,0:T(8,128)} %param.33) | copy-start | bytes 393220
  612.6 52.7 %copy-start.43 = (f32[2,32,512]{2,1,0:T(8,128)S(1)}, f32[2,32,512]{2,1,0:T(8,128)}, u32[]{:S(2)}) copy-start(f32[2,32,512]{2,1,0:T(8,128)} %param.37) | copy-start | bytes 393220
  612.6 52.7 %copy-start.44 = (f32[2,32,512]{2,1,0:T(8,128)S(1)}, f32[2,32,512]{2,1,0:T(8,128)}, u32[]{:S(2)}) copy-start(f32[2,32,512]{2,1,0:T(8,128)} %param.36) | copy-start | bytes 393220
  612.6 53.5 %copy-start.40 = (f32[2,16,1024]{2,1,0:T(8,128)S(1)}, f32[2,16,1024]{2,1,0:T(8,128)}, u32[]{:S(2)}) copy-start(f32[2,16,1024]{2,1,0:T(8,128)} %param.34) | copy-start | bytes 393220
  612.6 53.4 %copy-start.45 = (f32[2,16,1024]{2,1,0:T(8,128)S(1)}, f32[2,16,1024]{2,1,0:T(8,128)}, u32[]{:S(2)}) copy-start(f32[2,16,1024]{2,1,0:T(8,128)} %param.39) | copy-start | bytes 393220
  612.7 53.4 %copy-start.46 = (f32[2,16,1024]{2,1,0:T(8,128)S(1)}, f32[2,16,1024]{2,1,0:T(8,128)}, u32[]{:S(2)}) copy-start(f32[2,16,1024]{2,1,0:T(8,128)} %param.38) | copy-start | bytes 393220
  612.7 54.2 %copy-start.48 = (f32[14,32]{1,0:T(8,128)S(1)}, f32[14,32]{1,0:T(8,128)}, u32[]{:S(2)}) copy-start(f32[14,32]{1,0:T(8,128)} %param.35) | copy-start | bytes 5380
  612.7 54.2 %copy-start.53 = (f32[14,32]{1,0:T(8,128)S(1)}, f32[14,32]{1,0:T(8,128)}, u32[]{:S(2)}) copy-start(f32[14,32]{1,0:T(8,128)} %param.41) | copy-start | bytes 5380
  612.7 54.2 %copy-start.54 = (f32[14,32]{1,0:T(8,128)S(1)}, f32[14,32]{1,0:T(8,128)}, u32[]{:S(2)}) copy-start(f32[14,32]{1,0:T(8,128)} %param.40) | copy-start | bytes 5380
  (24 other events, 52.3 us)
Sparse Core Ops, SparseCore 0:
  329.8 22.6 all-gather.1
  471.7 28.2 reduce-scatter.1

commit v4 on v3

--- a/solution.py
+++ b/solution.py
@@ -801,10 +801,616 @@
         ),
     )(*[arrays[name] for name in names], picked, places, key_keep, *extra)
     held = dict(zip(names, out[: len(names)]))
-    held = {name: value.reshape(value.shape[0], -1, value.shape[-1]) for name, value in held.items()}
     if extra:
         held["up"] = extra[0]
     return held, out[len(names) :]
+
+
+TILE = 1280
+
+
+def head_kernel(sizes, *refs):
+    decoded, targets, weight, table_hbm, grad_out, loss_out = refs[:6]
+    rows, table, logits, partial, core_send, core_part, line_send, line_part, stats = refs[6:15]
+    table_sem, row_sem, stat_sem, core_sem, line_sem, send_sem = refs[15:]
+    here = position(sizes)
+    mine, column, cores, across = here["c"], here["x"], sizes["c"], sizes["x"]
+    owners = across * cores
+    me, twin = column * cores + mine, column * cores + 1 - mine
+    count = table.shape[0]
+    steps = count // TILE
+
+    def table_copy(number):
+        part = pl.ds(number * TILE, TILE)
+        return pltpu.make_async_copy(table_hbm.at[part], table.at[part], table_sem.at[number])
+
+    for number in range(steps):
+        table_copy(number).start()
+    barrier = pltpu.get_barrier_semaphore()
+    for step in range(1, owners):
+        other = (me + step) % owners
+        pl.semaphore_signal(
+            barrier,
+            inc=1,
+            device_id=device_at(here, sizes, x=other // cores, c=other % cores),
+            device_id_type=MESH_ID,
+        )
+    pl.semaphore_wait(barrier, owners - 1)
+    started = []
+
+    def remote(src, dst, arrival, **moved):
+        copy = pltpu.make_async_remote_copy(
+            src_ref=src,
+            dst_ref=dst,
+            send_sem=send_sem.at[len(started)],
+            recv_sem=arrival,
+            device_id=device_at(here, sizes, **moved),
+            device_id_type=MESH_ID,
+        )
+        copy.start()
+        started.append(copy)
+
+    def arrived(ref, arrival):
+        pltpu.make_async_remote_copy(
+            src_ref=ref,
+            dst_ref=ref,
+            send_sem=send_sem.at[0],
+            recv_sem=arrival,
+            device_id=device_at(here, sizes, c=1 - mine),
+            device_id_type=MESH_ID,
+        ).wait_recv()
+
+    def far(step, core):
+        return (column + step) % across * cores + core
+
+    rows[me] = decoded[...]
+    for step in range(1, across):
+        remote(rows.at[me], rows.at[me], row_sem.at[me], x=(column + step) % across)
+    remote(rows.at[me], rows.at[me], row_sem.at[me], c=1 - mine)
+    lane = lax.broadcasted_iota(jnp.int32, (ROWS, 128), 1)
+
+    def first_pass(block, fresh=False):
+        wanted = targets[block] - me * count
+
+        def body(number, carry):
+            top, spread, hit = carry
+            start = pl.multiple_of(number * TILE, TILE)
+            if fresh:
+                part = pl.ds(start, TILE)
+                pltpu.make_async_copy(table_hbm.at[part], table.at[part], table_sem.at[number]).wait()
+            values = dot_rows(rows[block], table[pl.ds(start, TILE), :])
+            logits[block, :, pl.ds(start, TILE)] = values
+            parts = [values[:, at : at + 128] for at in range(0, TILE, 128)]
+            new_top = top
+            for part in parts:
+                new_top = jnp.maximum(new_top, part)
+            spread = spread * jnp.exp(top - new_top)
+            near = wanted - start - lane
+            for place, part in enumerate(parts):
+                spread = spread + jnp.exp(part - new_top)
+                hit = hit + jnp.where(near == place * 128, part, 0.0)
+            return new_top, spread, hit
+
+        zero = jnp.zeros((ROWS, 128), jnp.float32)
+        low_start = jnp.full((ROWS, 128), -3e38, jnp.float32)
+        top, spread, hit = lax.fori_loop(0, steps, body, (low_start, zero, zero))
+        whole = jnp.max(top, -1, keepdims=True)
+        spread = jnp.sum(spread * jnp.exp(top - whole), -1, keepdims=True)
+        hit = jnp.sum(hit, -1, keepdims=True)
+        stats[block, me] = jnp.where(lane == 0, whole, jnp.where(lane == 1, spread, hit)).T[:8]
+        for step in range(1, owners):
+            other = (me + step) % owners
+            remote(
+                stats.at[block, me],
+                stats.at[block, me],
+                stat_sem.at[block, me],
+                x=other // cores,
+                c=other % cores,
+            )
+
+    def second_pass(block, place):
+        for step in range(1, owners):
+            other = (me + step) % owners
+            arrived(stats.at[block, other], stat_sem.at[block, other])
+        found = [stats[block, index] for index in range(owners)]
+        top = found[0][0:1]
+        for value in found[1:]:
+            top = jnp.maximum(top, value[0:1])
+        spread, hit = jnp.zeros_like(top), jnp.zeros_like(top)
+        for value in found:
+            spread = spread + value[1:2] * jnp.exp(value[0:1] - top)
+            hit = hit + value[2:3]
+        log_total = top + jnp.log(spread)
+        level = jnp.broadcast_to(log_total, (128, ROWS)).T
+        wanted = targets[block] - me * count
+        partial[place] = jnp.zeros((ROWS, 1024), jnp.float32)
+
+        def body(number, _):
+            start = pl.multiple_of(number * TILE, TILE)
+            near = wanted - start - lane
+            values = logits[block, :, pl.ds(start, TILE)]
+            parts = []
+            for index in range(TILE // 128):
+                value = jnp.exp(values[:, index * 128 : (index + 1) * 128] - level)
+                parts.append(low(jnp.where(near == index * 128, value - 1.0, value)))
+            partial[place] += dot(jnp.concatenate(parts, 1), table[pl.ds(start, TILE), :])
+            return 0
+
+        lax.fori_loop(0, steps, body, 0)
+        return log_total - hit
+
+    first_pass(me, True)
+    arrived(rows.at[twin], row_sem.at[twin])
+    first_pass(twin)
+    for step in range(1, across):
+        block = far(step, mine)
+        arrived(rows.at[block], row_sem.at[block])
+        remote(rows.at[block], rows.at[block], row_sem.at[block], c=1 - mine)
+        first_pass(block)
+    for step in range(1, across):
+        block = far(step, 1 - mine)
+        arrived(rows.at[block], row_sem.at[block])
+        first_pass(block)
+    for step in range(1, across):
+        for core in range(cores):
+            second_pass(far(step, core), core)
+
+            @pl.when(mine != core)
+            def _(core=core, step=step):
+                core_send[step - 1] = low(partial[core])
+                pltpu.make_async_remote_copy(
+                    src_ref=core_send.at[step - 1],
+                    dst_ref=core_part.at[step - 1],
+                    send_sem=core_sem.at[0, step - 1],
+                    recv_sem=core_sem.at[1, step - 1],
+                    device_id=device_at(here, sizes, c=1 - mine),
+                    device_id_type=MESH_ID,
+                ).start()
+
+        arrived(core_part.at[step - 1], core_sem.at[1, step - 1])
+        line_send[step - 1] = low(partial[mine] + wide(core_part[step - 1]))
+        remote(
+            line_send.at[step - 1],
+            line_part.at[step - 1],
+            line_sem.at[step - 1],
+            x=(column + step) % across,
+        )
+    second_pass(twin, 0)
+    last = across - 1
+    core_send[last] = low(partial[0])
+    remote(core_send.at[last], core_part.at[last], core_sem.at[1, last], c=1 - mine)
+    loss = second_pass(me, 1)
+    loss_out[...] = jnp.broadcast_to(loss, (8, ROWS))
+    arrived(core_part.at[last], core_sem.at[1, last])
+    value = partial[1] + wide(core_part[last])
+    for step in range(1, across):
+        arrived(line_part.at[step - 1], line_sem.at[step - 1])
+        value = value + wide(line_part[step - 1])
+    grad_out[...] = value * weight[:, :1]
+    for copy in started:
+        copy.wait_send()
+    for step in range(1, across):
+        pltpu.make_async_remote_copy(
+            src_ref=core_send.at[step - 1],
+            dst_ref=core_part.at[step - 1],
+            send_sem=core_sem.at[0, step - 1],
+            recv_sem=core_sem.at[1, step - 1],
+            device_id=device_at(here, sizes, c=1 - mine),
+            device_id_type=MESH_ID,
+        ).wait_send()
+
+
+def run_head(decoded, targets, weight, table, dp, vocab):
+    sizes = grid_of(dp, vocab)
+    across, owners = sizes["x"], vocab
+    f32, b16 = jnp.float32, jnp.bfloat16
+    anywhere, vmem = pl.BlockSpec(memory_space=pl.ANY), pl.BlockSpec(memory_space=pltpu.VMEM)
+    dma = pltpu.SemaphoreType.DMA
+    return pl.pallas_call(
+        functools.partial(head_kernel, sizes),
+        out_shape=[jax.ShapeDtypeStruct((ROWS, 1024), f32), jax.ShapeDtypeStruct((8, ROWS), f32)],
+        in_specs=[vmem] * 3 + [anywhere],
+        out_specs=[vmem] * 2,
+        scratch_shapes=[
+            pltpu.VMEM((owners, ROWS, 1024), b16),
+            pltpu.VMEM(table.shape, b16),
+            pltpu.VMEM((owners, ROWS, table.shape[0]), f32),
+            pltpu.VMEM((2, ROWS, 1024), f32),
+            pltpu.VMEM((across, ROWS, 1024), b16),
+            pltpu.VMEM((across, ROWS, 1024), b16),
+            pltpu.VMEM((across - 1, ROWS, 1024), b16),
+            pltpu.VMEM((across - 1, ROWS, 1024), b16),
+            pltpu.VMEM((owners, owners, 8, ROWS), f32),
+            dma((table.shape[0] // TILE,)),
+            dma((owners,)),
+            dma((owners, owners)),
+            dma((2, across)),
+            dma((across,)),
+            dma((8 * owners,)),
+        ],
+        compiler_params=pltpu.CompilerParams(
+            collective_id=3, has_side_effects=True, vmem_limit_bytes=62 * 2**20
+        ),
+    )(
+        decoded,
+        jnp.broadcast_to(targets.reshape(owners, ROWS, 1), (owners, ROWS, 128)),
+        jnp.broadcast_to(weight.reshape(ROWS, 1), (ROWS, 128)),
+        table,
+    )
+
+
+def backward_kernel(sizes, *refs):
+    refs = list(refs)
+
+    def take(count):
+        found = refs[:count]
+        del refs[:count]
+        return found
+
+    grad_in, norms, extra = take(3)
+    names = ("attn_in", "attn_out", "widen", "narrow", "down", "up")
+    held = dict(zip(names, take(6)))
+    saved_in = take(7)
+    shards = take(4)
+    small_out, square_out = take(2)
+    saved = take(7)
+    qkv_all, probs_all, normed_ring, inv_all, feed_in, slopes, bottles = saved
+    saved_sem, normed_sem, tiles, tile_sem, down_tile, down_sem = take(6)
+    grads = take(4)
+    sums, core_send, core_recv = take(4), take(4), take(4)
+    wide_send, wide_recv, mid_send, mid_recv, last_send, last_recv = (take(4) for _ in range(6))
+    small, small_slots, square_slots = take(1)[0], take(4), take(4)
+    grad_low, grad_sum, grad_memory, grad_hidden, grad_att, packed = take(6)
+    send_sem, recv_sem = take(2)
+    here = position(sizes)
+    mine = here["c"]
+
+    loads = {}
+
+    def fetch(place, index):
+        if (place, index) not in loads:
+            copy = pltpu.make_async_copy(
+                saved_in[place].at[index], saved[place].at[index], saved_sem.at[len(loads)]
+            )
+            loads[place, index] = copy
+            copy.start()
+        return loads[place, index]
+
+    order = (6, 5, 4, 3, 2, 1, 0)
+
+    def normed_copy(number):
+        slot = number % normed_ring.shape[0]
+        return pltpu.make_async_copy(saved_in[2].at[order[number]], normed_ring.at[slot], normed_sem.at[slot])
+
+    plan = []
+    block = 1024
+    for kind, which in (("feed", 1), ("attend", 2), ("attend", 1), ("feed", 0), ("attend", 0)):
+        if kind == "feed":
+            for left in range(0, 4096, block):
+                plan += [("narrow", which, left), ("widen", which, left)]
+            plan.append(("up", which, 0))
+        else:
+            plan.append(("attn_out", which, 0))
+            plan += [("attn_in", which, left) for left in range(0, 3072, block)]
+    grid = tuple(sizes[axis] for axis in "zyxc")
+    depth = tiles.shape[0]
+
+    def tile_copy(number):
+        name, layer, left = plan[number]
+        rows, columns = held[name].shape[5:]
+        buffer = tiles.at[number % depth]
+        if name == "narrow":
+            planes = left // block
+            source, shape = held[name].at[layer, planes], grid[1:] + (rows, columns)
+        else:
+            columns = min(columns, block)
+            source = held[name].at[layer, :, :, :, :, :, pl.ds(left, columns)]
+            shape = grid + (rows, columns)
+        count = 1
+        for size in shape[:-1]:
+            count *= size
+        target = buffer.at[pl.ds(0, count), pl.ds(0, columns)]
+        return pltpu.make_async_copy(source, target.reshape(shape), tile_sem.at[number % depth]), target
+
+    def down_copy(side):
+        target = down_tile.reshape(grid + held["down"].shape[5:])
+        return pltpu.make_async_copy(held["down"].at[side], target, down_sem.at[0])
+
+    turn = [0]
+
+    def with_tile(use):
+        number = turn[0]
+        turn[0] += 1
+        copy, target = tile_copy(number)
+        copy.wait()
+        result = use(target[...])
+        if number + depth < len(plan):
+            tile_copy(number + depth)[0].start()
+        return result
+
+    for number in range(2):
+        normed_copy(number).start()
+    fetch(3, slice(None))
+    fetch(5, 1)
+    for number in range(depth):
+        tile_copy(number)[0].start()
+    down_copy(1).start()
+    for place, index in ((6, 1), (4, 1), (0, 2), (1, 2), (0, 1), (1, 1), (5, 0), (6, 0), (4, 0), (0, 0), (1, 0)):
+        fetch(place, index)
+    lines_barrier(here, sizes)
+
+    used, started = [0], []
+
+    def copy_to(src, dst, **moved):
+        number = used[0]
+        used[0] += 1
+        copy = pltpu.make_async_remote_copy(
+            src_ref=src,
+            dst_ref=dst,
+            send_sem=send_sem.at[number],
+            recv_sem=recv_sem.at[number],
+            device_id=device_at(here, sizes, **moved),
+            device_id_type=MESH_ID,
+        )
+        copy.start()
+        started.append(copy)
+        return copy
+
+    def share(slots, value, axis):
+        slots[here[axis]] = value
+        return [
+            copy_to(slots.at[here[axis]], slots.at[here[axis]], **{axis: (here[axis] + step) % sizes[axis]})
+            for step in range(1, sizes[axis])
+        ]
+
+    def total(slots, axis, copies):
+        for copy in copies:
+            copy.wait_recv()
+        value = slots[0]
+        for index in range(1, sizes[axis]):
+            value = value + slots[index]
+        return value
+
+    plans = (("x", "y"), ("y", "x"), ("x", "y"), ("y", "x"))
+    pending = [None] * 4
+
+    def phase_core(parts):
+        for part in parts:
+            core_send[part][...] = low(grads[part][:, :, :, 1 - mine])
+            pending[part] = copy_to(core_send[part], core_recv[part], c=1 - mine)
+
+    def phase_wide(parts):
+        for part in parts:
+            pending[part].wait_recv()
+            sums[part][...] = grads[part][:, :, :, mine] + wide(core_recv[part][...])
+            axis = plans[part][0]
+            found = []
+            for step in range(1, sizes[axis]):
+                other = (here[axis] + step) % sizes[axis]
+                value = sums[part][:, :, other] if axis == "x" else sums[part][:, other]
+                wide_send[part][step - 1] = low(value)
+                found.append(copy_to(wide_send[part].at[step - 1], wide_recv[part].at[step - 1], **{axis: other}))
+            pending[part] = found
+
+    def phase_mid(parts):
+        for part in parts:
+            axis, later = plans[part]
+            kept = sums[part].at[:, :, here["x"]] if axis == "x" else sums[part].at[:, here["y"]]
+            value = kept[...]
+            for step, copy in enumerate(pending[part]):
+                copy.wait_recv()
+                value = value + wide(wide_recv[part][step])
+            kept[...] = value
+            found = []
+            for step in range(1, sizes[later]):
+                other = (here[later] + step) % sizes[later]
+                mid_send[part][step - 1] = low(kept[:, other])
+                found.append(copy_to(mid_send[part].at[step - 1], mid_recv[part].at[step - 1], **{later: other}))
+            pending[part] = found
+
+    def phase_last(parts):
+        for part in parts:
+            kept = sums[part].at[:, here["y"], here["x"]]
+            value = kept[...]
+            for step, copy in enumerate(pending[part]):
+                copy.wait_recv()
+                value = value + wide(mid_recv[part][step])
+            kept[...] = value
+            found = []
+            for step in range(1, sizes["z"]):
+                other = (here["z"] + step) % sizes["z"]
+                last_send[part][step - 1] = low(kept[other])
+                found.append(copy_to(last_send[part].at[step - 1], last_recv[part].at[step - 1], z=other))
+            pending[part] = found
+
+    def phase_end(parts):
+        square = jnp.zeros((1, 1), jnp.float32)
+        for part in parts:
+            value = sums[part][here["z"], here["y"], here["x"]]
+            for step, copy in enumerate(pending[part]):
+                copy.wait_recv()
+                value = value + wide(last_recv[part][step])
+            shards[part][...] = value
+            square = square + jnp.sum(value * value, keepdims=True)
+        return square
+
+    norm_turn = [0]
+
+    def norm_back(grad_out, which):
+        number = norm_turn[0]
+        norm_turn[0] += 1
+        if number + 2 < len(order):
+            normed_copy(number + 2).start()
+        normed_copy(number).wait()
+        normed = normed_ring[number % normed_ring.shape[0]]
+        inv_std = inv_all[which][:, :1]
+        scaled = grad_out * norms[which : which + 1, :]
+        small[which : which + 1, :] = jnp.sum(grad_out * normed, 0, keepdims=True)
+        small[which + 7 : which + 8, :] = jnp.sum(grad_out, 0, keepdims=True)
+        grad = inv_std * (
+            scaled - jnp.mean(scaled, -1, keepdims=True) - normed * jnp.mean(scaled * normed, -1, keepdims=True)
+        )
+        grad_sum[...] = grad
+        grad_low[...] = low(grad)
+
+    def feed_back(side):
+        fetch(5, side).wait()
+        for left in range(0, 4096, block):
+
+            def first(tile, left=left):
+                slope = wide(slopes[side, :, pl.ds(left, block)])
+                grad_hidden[...] = low(dot_rows(grad_low[...], tile) * slope)
+
+            def second(tile):
+                grad_sum[...] += dot_rows(grad_hidden[...], tile)
+
+            with_tile(first)
+            with_tile(second)
+        fetch(6, side).wait()
+        fetch(4, side).wait()
+
+        def up(tile):
+            bottle = low(BRANCH_SCALE * dot_rows(grad_low[...], tile) * wide(bottles[side, 1]))
+            grad_hidden[:, pl.ds(0, 512)] = bottle
+
+        with_tile(up)
+        down_copy(side).wait()
+        grad_sum[...] += dot_rows(grad_hidden[:, pl.ds(0, 512)], down_tile[...])
+        if side:
+            down_copy(0).start()
+        part = 2 * side
+        grads[part + 1][...] = (BRANCH_SCALE * dot_columns(bottles[side, 0], grad_low[...])).reshape(
+            grads[part + 1].shape
+        )
+        grads[part][...] = dot_columns(feed_in[side], grad_hidden[:, pl.ds(0, 512)]).reshape(grads[part].shape)
+
+    def attend_back(layer, between=None):
+        def first(tile):
+            grad_att[...] = low(dot_rows(grad_low[...], tile))
+
+        with_tile(first)
+        fetch(0, layer).wait()
+        fetch(1, layer).wait()
+
+        def body(number, _):
+            seq, pair = number // 8, number % 8
+            masks = lane_masks()
+            rows = pl.ds(pl.multiple_of(seq * LEN, LEN), LEN)
+
+            def columns(part):
+                return pl.ds(pl.multiple_of(part * 1024 + pair * 128, 128), 128)
+
+            queries, keys, values = (qkv_all[layer, rows, columns(part)] for part in range(3))
+            grad_out = stack_heads(grad_att[rows, columns(0)], masks)
+            chance_low = probs_all[layer, seq, pair]
+            chance = wide(chance_low)
+            weighed = chance * dot_rows(grad_out, values)
+            grad_scores = low(weighed - chance * jnp.sum(weighed, -1, keepdims=True))
+            side = jnp.concatenate([grad_scores[:LEN], grad_scores[LEN:]], 1)
+            packed[rows, columns(0)] = low(dot(side, stack_heads(keys, masks)) * 0.125)
+            packed[rows, columns(1)] = low(dot_columns(grad_scores, stack_heads(queries, masks)) * 0.125)
+            packed[rows, columns(2)] = low(dot_columns(chance_low, grad_out))
+            return 0
+
+        lax.fori_loop(0, 8 * MICRO, body, 0, unroll=2)
+        if between is not None:
+            between()
+        for left in range(0, 3072, block):
+
+            def second(tile, left=left):
+                value = dot_rows(packed[:, pl.ds(left, block)], tile)
+                if layer == 2 and left == block:
+                    grad_memory[...] = value
+                elif layer == 2 and left > block:
+                    grad_memory[...] += value
+                else:
+                    grad_sum[...] += value
+
+            with_tile(second)
+
+    small[...] = extra[...]
+    fetch(3, slice(None)).wait()
+    norm_back(grad_in[...], 6)
+    feed_back(1)
+    phase_core((2, 3))
+    norm_back(grad_sum[...], 5)
+    attend_back(2)
+    phase_wide((2, 3))
+    norm_back(grad_sum[...], 4)
+    attend_back(1)
+    phase_mid((2, 3))
+    norm_back(grad_sum[...], 3)
+    norm_back(grad_memory[...], 2)
+    feed_back(0)
+    phase_core((0, 1))
+    phase_last((2, 3))
+    norm_back(grad_sum[...], 1)
+    attend_back(0, lambda: phase_wide((0, 1)))
+    square = phase_end((2, 3))
+    phase_mid((0, 1))
+    norm_back(grad_sum[...], 0)
+    copies = share(small_slots[0], small[...], "c")
+    phase_last((0, 1))
+    copies = share(small_slots[1], total(small_slots[0], "c", copies), "x")
+    copies = share(small_slots[2], total(small_slots[1], "x", copies), "y")
+    copies = share(small_slots[3], total(small_slots[2], "y", copies), "z")
+    square = jnp.broadcast_to(square + phase_end((0, 1)), (8, 128))
+    for place, axis in enumerate("cxyz"):
+        parts = share(square_slots[place], square, axis)
+        if place == 0:
+            whole = total(small_slots[3], "z", copies)
+            small_out[...] = whole
+            norm_square = jnp.sum(whole[:14] * whole[:14], keepdims=True)
+        square = total(square_slots[place], axis, parts)
+    square_out[...] = square + norm_square
+    for copy in started:
+        copy.wait_send()
+
+
+def run_backward(grad_decoded, norms, extra, held, saved, dp, vocab):
+    sizes = grid_of(dp, vocab)
+    z, y, x, c = (sizes[axis] for axis in "zyxc")
+    names = ("attn_in", "attn_out", "widen", "narrow", "down", "up")
+    down, up = held["down"].shape[5:], held["up"].shape[5:]
+    tails = (down, up, down, up)
+    f32, b16 = jnp.float32, jnp.bfloat16
+    anywhere, vmem = pl.BlockSpec(memory_space=pl.ANY), pl.BlockSpec(memory_space=pltpu.VMEM)
+    dma = pltpu.SemaphoreType.DMA
+    scratch = [pltpu.VMEM(value.shape, value.dtype) for value in saved]
+    scratch[2] = pltpu.VMEM((3, ROWS, 1024), f32)
+    scratch += [dma((16,)), dma((3,)), pltpu.VMEM((5, 1024, 1024), b16), dma((5,))]
+    scratch += [pltpu.VMEM((1024, 512), b16), dma((1,))]
+    scratch += [pltpu.VMEM((z, y, x, c) + tail, f32) for tail in tails]
+    scratch += [pltpu.VMEM((z, y, x) + tail, f32) for tail in tails]
+    for _ in range(2):
+        scratch += [pltpu.VMEM((z, y, x) + tail, b16) for tail in tails]
+    for lead in (((x - 1, z, y), (y - 1, z, x)), ((y - 1, z), (x - 1, z)), ((z - 1,), (z - 1,))):
+        for _ in range(2):
+            scratch += [pltpu.VMEM(lead[place % 2] + tail, b16) for place, tail in enumerate(tails)]
+    scratch.append(pltpu.VMEM((16, 1024), f32))
+    scratch += [pltpu.VMEM((sizes[axis], 16, 1024), f32) for axis in "cxyz"]
+    scratch += [pltpu.VMEM((sizes[axis], 8, 128), f32) for axis in "cxyz"]
+    scratch += [
+        pltpu.VMEM((ROWS, 1024), b16),
+        pltpu.VMEM((ROWS, 1024), f32),
+        pltpu.VMEM((ROWS, 1024), f32),
+        pltpu.VMEM((ROWS, 1024), b16),
+        pltpu.VMEM((ROWS, 1024), b16),
+        pltpu.VMEM((ROWS, 3072), b16),
+    ]
+    links = 6 * (x + y + z + c)
+    scratch += [dma((links,)), dma((links,))]
+    return pl.pallas_call(
+        functools.partial(backward_kernel, sizes),
+        out_shape=[jax.ShapeDtypeStruct(tail, f32) for tail in tails]
+        + [jax.ShapeDtypeStruct((16, 1024), f32), jax.ShapeDtypeStruct((8, 128), f32)],
+        in_specs=[vmem] * 3 + [anywhere] * 13,
+        out_specs=[vmem] * 6,
+        scratch_shapes=scratch,
+        compiler_params=pltpu.CompilerParams(
+            collective_id=2, has_side_effects=True, vmem_limit_bytes=62 * 2**20
+        ),
+    )(grad_decoded, norms, extra, *[held[name] for name in names], *saved)
 
 
 def attend_back(grad_low, queries, key_rows, values, probs, scale):
@@ -954,15 +1560,21 @@
         jnp.zeros((), jnp.bfloat16),
     ).reshape(groups // 2, 2, 2, ROWS, width)
     task_hot = (task_ids[:, None] == jnp.arange(TASKS)[None, :]).astype(jnp.float32)
-    task_counts = lax.psum(jnp.sum(task_hot * target_length[:, None].astype(jnp.float32), 0), "dp")
-    seq_scale = jnp.sum(task_hot * (1.0 / (TASKS * task_counts))[None, :], 1)
+    group_counts = jnp.sum(task_hot * target_length[:, None].astype(jnp.float32), 0)
     own = vocab_rank * MICRO
     source_count = lax.dynamic_slice_in_dim(source_length, own, MICRO)
     key_keep = jnp.broadcast_to(
         (jnp.arange(LEN)[None, None, :] < source_count[:, None, None]).astype(jnp.float32), (MICRO, 8, LEN)
     )
     parts = {
-        "norms": jnp.pad(norm_params.T, ((0, 0), (0, 114)))[None],
+        "norms": jnp.concatenate(
+            [
+                norm_params.T,
+                jnp.pad(group_counts, (0, norm_params.shape[1] - TASKS))[:, None],
+                jnp.zeros((norm_params.shape[1], 113), jnp.float32),
+            ],
+            1,
+        )[None],
         "attn_in": attention_in,
         "attn_out": attention_out,
         "widen": widen_weight,
@@ -971,17 +1583,34 @@
         "up": low(adapt_up),
     }
     held, saved = run_forward(parts, picked, positions, key_keep, dp, groups)
-    norms = held["norms"][0, :, :14].T
-    decoded = saved[7]
-    grad_decoded, own_loss = head(decoded, vocab_table, target_ids, target_length, seq_scale, groups, vocab_rank)
+    slab = held.pop("norms").reshape(dp, groups, -1, 128)
+    task_counts = jnp.sum(slab[:, 0, :TASKS, 14], 0)
+    seq_scale = jnp.sum(task_hot * (1.0 / (TASKS * task_counts))[None, :], 1)
+    norms = slab.reshape(width, 128)[:, :16].T
+    if groups <= 4 and rows_local % TILE == 0:
+        own_length = lax.dynamic_slice_in_dim(target_length, own, MICRO)
+        own_mask = (jnp.arange(LEN)[None, :] < own_length[:, None]).astype(jnp.float32)
+        own_weight = own_mask * lax.dynamic_slice_in_dim(seq_scale, own, MICRO)[:, None]
+        grad_decoded, row_loss = run_head(saved[7], target_ids, own_weight, vocab_table, dp, groups)
+        own_loss = jnp.sum(row_loss[0].reshape(MICRO, LEN) * own_mask, 1)
+    else:
+        grad_decoded, own_loss = head(
+            saved[7], vocab_table, target_ids, target_length, seq_scale, groups, vocab_rank
+        )
     task_local = jnp.sum(lax.dynamic_slice_in_dim(task_hot, own, MICRO) * own_loss[:, None], 0)
-    down_enc, up_enc, down_dec, up_dec, norm_grads = backward(grad_decoded, held, norms, saved[:7])
-    small = jnp.concatenate(
-        [norm_grads, jnp.pad(task_local[None], ((0, 1), (0, width - TASKS)))], 0
-    )
-    down_enc, up_enc, down_dec, up_dec, small, square = reduce_gradients(
-        down_enc, up_enc, down_dec, up_dec, small, dp, groups
-    )
+    task_row = jnp.pad(task_local[None], ((0, 1), (0, width - TASKS)))
+    if groups <= 4:
+        extra = jnp.pad(task_row, ((14, 0), (0, 0)))
+        down_enc, up_enc, down_dec, up_dec, small, square = run_backward(
+            grad_decoded, norms, extra, held, saved[:7], dp, groups
+        )
+    else:
+        held = {name: value.reshape(value.shape[0], -1, value.shape[-1]) for name, value in held.items()}
+        down_enc, up_enc, down_dec, up_dec, norm_grads = backward(grad_decoded, held, norms, saved[:7])
+        small = jnp.concatenate([norm_grads, task_row], 0)
+        down_enc, up_enc, down_dec, up_dec, small, square = reduce_gradients(
+            down_enc, up_enc, down_dec, up_dec, small, dp, groups
+        )
     shard_down = jnp.stack([down_enc, down_dec])
     shard_up = jnp.stack([up_enc, up_dec])
     full_norm, task_sums = small[:14], small[14, :TASKS]

time: 685 us -> 486 us (0.71)
  matrix products: 120 us -> 0 us
  local copies, waits for them, and re-layouts: 136 us -> 25.6 us
  Pallas kernels: 345 us -> 436 us
  blocking collectives: 31.5 us -> 0 us
  between operations: 17.3 us -> 3.11 us
  other arithmetic: 26 us -> 13.9 us
    dot_general x31 -> x0, matrix products: 120 us -> none  [the longest x14 78.8 us: dot_rows(): lax.dot_general(left, right, (((1,), (1,)), ((), ())), preferred_element_...]
    pallas_call x1 -> x2, Pallas kernels: 50.8 us -> 141 us  [the longest x1 88.2 us: run_backward(): pl.pallas_call(functools.partial(backward_kernel, sizes), out_shape=[jax....]
    slice x11 -> x1, local copies, waits for them, and re-layouts: 55.5 us -> 0.7 us  [local(): own_loss = jnp.sum(row_loss[0].reshape(MICRO, LEN) * own_mask, 1)]
    reshape x15 -> x0, local copies, waits for them, and re-layouts: 34.7 us -> none  [split_heads(): return value.reshape(MICRO, LEN, HEADS, value.shape[1] // HEADS)]
    psum x2 -> x0, blocking collectives: 25.8 us -> none  [the longest x1 19.1 us: local(): lax.psum(jnp.sum(task_hot * target_length[:, None].astype(jnp.float32), 0...]
    reduce_sum x3 -> x2, other arithmetic: 12.2 us -> 1.13 us  [the longest x1 0.95 us: local(): task_counts = jnp.sum(slab[:, 0, :TASKS, 14], 0)]
  transfers between devices with their start and end apart: 2 -> 0, of which waited for: 0 -> 0; matrix products, arithmetic and copies ran while one was open for 13% -> 0% of each run, Pallas kernels for 0% -> 0%
where the time goes in v4:
time: 486 us; the launch traced here: 478 us
  Pallas kernels  436 us (90%)
  local copies, waits for them, and re-layouts  25.6 us (5%)
  other arithmetic  13.9 us (3%)
    pallas_call x1, Pallas kernels, run_forward(): pl.pallas_call(functools.partial(forward_kernel, sizes, units, names), ou...  294 us
    pallas_call x1, Pallas kernels, run_backward(): pl.pallas_call(functools.partial(backward_kernel, sizes), out_shape=[jax....  88.2 us
    pallas_call x1, Pallas kernels, run_head(): pl.pallas_call(functools.partial(head_kernel, sizes), out_shape=[jax.Shap...  53.2 us
    gather x1, local copies, waits for them, and re-layouts, local(): jnp.take(vocab_table, jnp.clip(joined_ids, 0, rows_local - 1), axis=0)  17.4 us

profile of v4, /device:TPU:0, one launch (start us, length us, event | category | flops | bytes accessed | tf_op | source)
XLA Modules:
  0.0 478.2 jit_solution(4427066099730503659)
XLA Ops:
  0.6 0.7 dynamic_slice.15
  1.4 0.1 compare_convert_fusion
  1.5 0.6 broadcast_in_dim.69.refs_9_
  2.1 0.7 compare_and_fusion.1
  2.8 0.7 fusion.3
  3.6 17.4 %gather_fusion = bf16[2048,1024]{1,0:T(8,128)(2,1)} fusion(bf16[6400,1024]{1,0:T(8,128)(2,1)} %refs_3_.3, s32[2048]{0:T(1024)S(1)} %broadcast_clamp_fusion), kind=kCustom, calls=%fused_computation | custom fusion | bytes 8396800 | tf_op jit(solution)/shard_map/jit(_take)/gather | solution.py:1559
  20.9 0.0 copy-start.7
  21.0 4.0 select_select_fusion.refs_7_
  24.9 0.0 copy-done.2
  24.9 0.6 convert_element_type.29.refs_5_
  25.6 0.0 copy-done.1
  25.6 0.6 convert_element_type.30.refs_6_
  26.2 0.0 copy-done.13
  26.2 0.0 copy-done.11
  26.2 0.1 select_reduce_fusion.1
  26.3 0.1 copy.47
  26.4 0.0 copy-done.7
  26.4 0.1 copy.45
  26.5 0.1 pad.25.clone
  26.6 0.7 maximum_bitcast_fusion.refs_0_
  27.3 294.2 %shard_map.292 = (f32[1,4,2,2,2,32,128]{6,5,4,3,2,1,0:T(8,128)}, bf16[3,4,2,2,2,32,3072]{6,5,4,3,2,1,0:T(8,128)(2,1)}, bf16[3,4,2,2,2,32,1024]{6,5,4,3,2,1,0:T(8...) custom-call(f32[1,32,128]{2,1,0:T(8,128)} %maximum_bitcast_fusion.re, ...), custom_call_target="tpu_custom_call" | custom-call | tf_op jit(solution)/shard_map/pallas_call | solution.py:773
  321.4 0.9 slice_reduce_fusion
  322.4 0.2 select_reduce_fusion
  322.6 0.1 dynamic_slice.17
  322.7 0.1 dynamic_slice.16
  322.7 0.1 select_bitcast_fusion
  322.8 0.8 broadcast_in_dim.72.refs_2_
  323.6 0.0 copy-done.10
  323.6 1.2 broadcast_in_dim.71.refs_1_
  324.8 53.2 %shard_map.293 = (f32[256,1024]{1,0:T(8,128)}, f32[8,256]{1,0:T(8,128)}) custom-call(bf16[256,1024]{1,0:T(8,128)(2,1)} %get-tuple-element.35.refs_0_, s32[4,256,128]{2,1,0:T(8,128)} %broadcast_in_dim.71.refs_1_, f32[256,128]{1,0:T(8,128)} %broadcast_in_dim.72.refs_2_, bf16[6400,1024]{1,0:T(8,128)(2,1)} %refs_3_.3), custom_call_target="tpu_custom_call" | custom-call | tf_op jit(solution)/shard_map/pallas_call | solution.py:1009
  377.9 0.0 copy-done.12
  377.9 0.7 slice.20
  378.6 0.2 select_reduce_fusion.2
  378.8 0.1 fusion.4
  378.9 0.1 multiply_reduce_fusion
  379.0 0.6 pad.27.refs_2_
  379.6 0.0 copy-done
  379.6 0.8 copy.57
  380.4 0.0 copy-start.5
  380.5 0.0 copy-start.6
  380.5 88.2 %shard_map.294 = (f32[32,512]{1,0:T(8,128)}, f32[16,1024]{1,0:T(8,128)}, f32[32,512]{1,0:T(8,128)}, f32[16,1024]{1,0:T(8,128)}, f32[16,1024]{1,0:T(8,128)}, /*index=5*/f32[8,128]{1,0:T(8,128)}) custom-call(f32[256,1024]{1,0:T(8,128)} %get-tuple-element.37.refs_0_, f32[16,1024]{1,0:T(8,128)} %bitcast.30, f32[16,1024]{1,0:T(8,128)} %pad.27.refs_2_, ...), custom_call_target="tpu_custom_call" | custom-call | tf_op jit(solution)/shard_map/pallas_call | solution.py:1403
  468.7 1.2 slice.21
  470.7 1.4 multiply_subtract_fusion.2
  472.1 0.0 copy-done.4
  472.1 1.7 multiply_subtract_fusion
  473.8 0.0 copy-done.6
  473.8 1.7 multiply_subtract_fusion.1
  475.4 1.2 slice_bitcast_fusion
  (23 shorter events, 0.1 us)
Async XLA Ops:
  20.9 4.0 copy-start.2
  20.9 4.6 copy-start.1
  20.9 5.3 %copy-start.13 = (s32[8]{0:T(128)S(1)}, s32[8]{0:T(128)}, u32[]{:S(2)}) copy-start(s32[8]{0:T(128)} %param.25) | copy-start | bytes 100
  20.9 5.3 %copy-start.11 = (s32[8]{0:T(128)S(1)}, s32[8]{0:T(128)}, u32[]{:S(2)}) copy-start(s32[8]{0:T(128)} %param.26) | copy-start | bytes 100
  20.9 5.5 %copy-start.7 = (f32[14,32]{1,0:T(8,128)S(1)}, f32[14,32]{1,0:T(8,128)}, u32[]{:S(2)}) copy-start(f32[14,32]{1,0:T(8,128)} %param.35) | copy-start | bytes 5380
  24.9 298.6 %copy-start.10 = (s32[8,128]{1,0:T(8,128)S(1)}, s32[8,128]{1,0:T(8,128)}, u32[]{:S(2)}) copy-start(s32[8,128]{1,0:T(8,128)} %param.23) | copy-start | bytes 12292
  322.4 55.6 %copy-start.12 = (f32[4]{0:T(128)}, f32[4]{0:T(128)S(1)}, u32[]{:S(2)}) copy-start(f32[4]{0:T(128)S(1)} %slice_reduce_fusion) | copy-start | bytes 52
  324.8 54.9 %copy-start = (f32[1,4,2,2,2,32,128]{6,5,4,3,2,1,0:T(8,128)S(1)}, f32[1,4,2,2,2,32,128]{6,5,4,3,2,1,0:T(8,128)}, u32[]{:S(2)}) copy-start(f32[1,4,2,2,2,32,128]{6,5,4,3,2,1,0:T(8,128)} %get-tuple-element.36) | copy-start | bytes 1572868
  380.4 90.2 %copy-start.8 = (f32[14,32]{1,0:T(8,128)S(1)}, f32[14,32]{1,0:T(8,128)}, u32[]{:S(2)}) copy-start(f32[14,32]{1,0:T(8,128)} %param.41) | copy-start | bytes 5380
  380.4 90.2 %copy-start.9 = (f32[14,32]{1,0:T(8,128)S(1)}, f32[14,32]{1,0:T(8,128)}, u32[]{:S(2)}) copy-start(f32[14,32]{1,0:T(8,128)} %param.40) | copy-start | bytes 5380
  380.4 91.6 %copy-start.3 = (f32[2,16,1024]{2,1,0:T(8,128)S(1)}, f32[2,16,1024]{2,1,0:T(8,128)}, u32[]{:S(2)}) copy-start(f32[2,16,1024]{2,1,0:T(8,128)} %param.39) | copy-start | bytes 393220
  380.4 91.6 %copy-start.4 = (f32[2,16,1024]{2,1,0:T(8,128)S(1)}, f32[2,16,1024]{2,1,0:T(8,128)}, u32[]{:S(2)}) copy-start(f32[2,16,1024]{2,1,0:T(8,128)} %param.38) | copy-start | bytes 393220
  380.4 93.3 %copy-start.5 = (f32[2,32,512]{2,1,0:T(8,128)S(1)}, f32[2,32,512]{2,1,0:T(8,128)}, u32[]{:S(2)}) copy-start(f32[2,32,512]{2,1,0:T(8,128)} %param.37) | copy-start | bytes 393220
  380.5 93.3 %copy-start.6 = (f32[2,32,512]{2,1,0:T(8,128)S(1)}, f32[2,32,512]{2,1,0:T(8,128)}, u32[]{:S(2)}) copy-start(f32[2,32,512]{2,1,0:T(8,128)} %param.36) | copy-start | bytes 393220

commit v5 on v4

--- a/solution.py
+++ b/solution.py
@@ -221,15 +221,19 @@
     )(*grads, small)
 
 
-ORDERS = ("xzy", "yzx", "zyx", "xzy", "yzx", "zxy")
+ORDERS = ("xzy", "yzx", "zyx", "zxy")
 SEQUENCE = (
     ("norms", 0), ("attn_in", 0), ("attn_out", 0), ("down", 0), ("widen", 0), ("up", 0), ("narrow", 0),
     ("attn_in", 1), ("attn_out", 1), ("attn_in", 2), ("attn_out", 2), ("down", 1), ("widen", 1), ("up", 1),
     ("narrow", 1),
 )
 COLUMNS = {"norms": 128, "attn_in": 512, "attn_out": 512, "down": 512, "widen": 512, "up": 512, "narrow": 256}
-LAG = 3.0
-PACE = 0.7
+PARTS = {("narrow", 0): 2, ("narrow", 1): 4}
+LAG_Z = (2.5, 2.5, 2.5)
+LAG_LINE = (8.0, 3.5, 5.5)
+LAG_CORE = 2.75
+PACE = 0.5
+SETTLE = 0.8
 HEADS = 16
 LEN = 128
 MICRO = 2
@@ -243,17 +247,45 @@
     return [(axis, hop) for axis in order for hop in range(1, sizes[axis])]
 
 
-def plan_units(shapes, names, devices):
+def plan_units(shapes, names, sizes):
+    devices = sizes["z"] * sizes["y"] * sizes["x"] * sizes["c"]
     units, clock = [], 0.0
+    load = {"x": 0.85, "y": 0.0, "z": 0.0}
     for name, layer in SEQUENCE:
         if name not in names:
             continue
         rows, columns = shapes[name]
         step = min(COLUMNS[name], columns)
+        parts = PARTS.get((name, layer), 1)
+        if rows % (16 * parts):
+            parts = 1
+        height = rows // parts
         for left in range(0, columns, step):
-            units.append((name, layer, left, step, clock))
-            clock += rows * devices * step / 2**19
+            for top in range(0, rows, height):
+                size = height * devices * step / 2**19
+                best = None
+                for order in ORDERS:
+                    after, held = dict(load), 1
+                    for axis in order:
+                        after[axis] += size * held * (sizes[axis] - 1) * sizes["c"] / devices
+                        held *= sizes[axis]
+                    score = sum(value**4 for value in after.values())
+                    if best is None or score < best[0]:
+                        best = (score, order, after)
+                load = best[2]
+                units.append((name, layer, left, step, top, height, clock, best[1]))
+                clock += size
     return units
+
+
+def stage_clocks(unit, sizes):
+    order = unit[7]
+    found = [0.0]
+    for axis, _ in hops_of(order, sizes):
+        found.append(found[-1] + (LAG_Z if axis == "z" else LAG_LINE)[order.index(axis)])
+    found.append(found[-1] + LAG_CORE)
+    scale = min(1.0, 0.8 + unit[6] / 20.0)
+    return [unit[6] + scale * value for value in found]
 
 
 def dot(left, right):
@@ -364,12 +396,12 @@
     everything = slice(None)
 
     def own_source(unit):
-        name, layer, left, width, _ = unit
-        return ins[name].at[layer, :, pl.ds(left, width)]
+        name, layer, left, width, top, height = unit[:6]
+        return ins[name].at[layer, pl.ds(top, height), pl.ds(left, width)]
 
     def piece(unit, index):
-        name, layer, left, width, _ = unit
-        return outs[name].at[(layer,) + index + (everything, pl.ds(left, width))]
+        name, layer, left, width, top, height = unit[:6]
+        return outs[name].at[(layer,) + index + (pl.ds(top, height), pl.ds(left, width))]
 
     def view(unit, order, axis, coordinate):
         place = order.index(axis)
@@ -378,7 +410,7 @@
         return piece(unit, (at["z"], at["y"], at["x"], here["c"]))
 
     def sends(number, stage):
-        unit, order = units[number], ORDERS[number % len(ORDERS)]
+        unit, order = units[number], units[number][7]
         axis, hop = hops_of(order, sizes)[stage]
         size, mine = sizes[axis], here[axis]
         first = order.index(axis) == 0
@@ -431,7 +463,7 @@
                 def _(build=build):
                     build(True).wait_recv()
 
-        if stage == sizes[ORDERS[number % len(ORDERS)][0]] - 1:
+        if stage == sizes[units[number][7][0]] - 1:
             local_copy(number).wait()
         if stage < depth:
             for ok, _, build in sends(number, stage):
@@ -605,9 +637,9 @@
         return lax.broadcasted_iota(jnp.int32, (2 * LEN, LEN), 1) <= query
 
     steps = []
-    unit_of = {}
+    members = {}
     for number, unit in enumerate(units):
-        unit_of[unit[:3]] = number
+        members.setdefault(unit[:3], []).append(number)
 
     def add(run, cost, unit=None, clock=0.0):
         steps.append((unit, cost, clock, run))
@@ -615,28 +647,28 @@
     def attention_steps(which, norm, side, keep):
         for left in range(0, 3072, 512):
             from_memory = which == 2 and left >= 1024
-            add(project(which, left, side, from_memory), 0.6, unit_of["attn_in", which, left])
+            add(project(which, left, side, from_memory), 0.6, ("attn_in", which, left))
         for start in range(0, 16, 4):
             add(attention(which, start, keep), 2.0)
         for left in range(0, 1024, 512):
-            add(project_out(left), 0.6, unit_of["attn_out", which, left])
+            add(project_out(left), 0.6, ("attn_out", which, left))
         add(finish_attention(which, norm, side), 1.0)
 
     def feed_steps(norm, side):
-        add(narrow_down(side), 1.3, unit_of["down", side, 0])
+        add(narrow_down(side), 1.3, ("down", side, 0))
         for left in range(0, 4096, 512):
-            add(widen(left, side), 1.3, unit_of["widen", side, left])
+            add(widen(left, side), 1.3, ("widen", side, left))
         for left in range(0, 1024, 512):
             if "up" in names:
-                add(raise_up(left, side), 0.4, unit_of["up", side, left])
+                add(raise_up(left, side), 0.4, ("up", side, left))
             else:
                 part = functools.partial(lambda left, side: extra_up[side, :, pl.ds(left, 512)], left, side)
                 add(functools.partial(raise_up(left, side), part), 0.4)
         for left in range(0, 1024, 256):
-            add(narrow(left, side), 1.0, unit_of["narrow", side, left])
+            add(narrow(left, side), 1.0, ("narrow", side, left))
         add(finish_feed(norm, side), 1.0)
 
-    add(begin(0), 2.0, unit_of["norms", 0, 0], 8.0)
+    add(begin(0), 2.0, ("norms", 0, 0), 8.0)
     attention_steps(0, 1, 0, source_keep)
     feed_steps(2, 0)
     add(begin(1), 1.5, None, 20.0)
@@ -644,10 +676,10 @@
     attention_steps(2, 5, 1, source_keep)
     feed_steps(6, 1)
 
-    loads = [step[0] for step in steps if isinstance(step[0], int) and units[step[0]][0] != "norms"]
+    loads = [step[0] for step in steps if step[0] is not None and step[0][0] != "norms"]
     slot_of, rings = {}, {"tall": [], "flat": []}
     for unit in loads:
-        kind = "tall" if units[unit][0] == "narrow" else "flat"
+        kind = "tall" if unit[0] == "narrow" else "flat"
         ring = rings[kind]
         size = (tall_tiles if kind == "tall" else tiles).shape[0]
         slot_of[unit] = (kind, len(ring) % size, ring[len(ring) - size] if len(ring) >= size else None)
@@ -655,7 +687,8 @@
 
     def tile_parts(unit):
         kind, slot, _ = slot_of[unit]
-        name, layer, left, width, _ = units[unit]
+        name, layer, left = unit
+        width = units[members[unit][0]][3]
         source = outs[name].at[layer, :, :, :, :, :, pl.ds(left, width)]
         buffer = (tall_tiles if kind == "tall" else tiles).at[slot]
         sem = (tall_sem if kind == "tall" else tile_sem).at[slot]
@@ -664,7 +697,7 @@
         shape = tuple(sizes[axis] for axis in "zyxc") + (ins[name].shape[1], width)
         return pltpu.make_async_copy(source, target.reshape(shape), sem), target
 
-    complete, loaded, done = set(), set(), set()
+    complete, loaded, done, moment = set(), {}, set(), [0.0]
     waiting = list(loads)
 
     def try_loads():
@@ -674,14 +707,14 @@
             if unit not in complete or (before is not None and before not in done):
                 return
             tile_parts(unit)[0].start()
-            loaded.add(unit)
+            loaded[unit] = moment[0]
             waiting.pop(0)
 
     queue = list(steps)
 
     def run_step():
         unit, cost, _, run = queue.pop(0)
-        if unit is None or units[unit][0] == "norms":
+        if unit is None or unit[0] == "norms":
             run()
         else:
             copy, target = tile_parts(unit)
@@ -699,26 +732,33 @@
             return False
         if unit is None:
             return True
-        return unit in complete if units[unit][0] == "norms" else unit in loaded
+        if unit[0] == "norms":
+            return unit in complete
+        return unit in loaded and clock - loaded[unit] >= SETTLE
 
     for group in range(2):
         embed_first(group).start()
         embed_local(group).start()
     events = sorted(
-        (unit[4] + LAG * stage, -stage, number) for number, unit in enumerate(units) for stage in range(depth + 2)
+        (clock, -stage, number)
+        for number, unit in enumerate(units)
+        for stage, clock in enumerate(stage_clocks(unit, sizes))
     )
-    embed_done, credit, last = [], 0.0, 0.0
+    embed_done, credit, last, arrived = [], 0.0, 0.0, set()
     for clock, minus, number in events:
-        stage = -minus
+        stage, moment[0] = -minus, clock
         comm_step(number, stage)
         for group in range(2):
             if group not in embed_done and clock >= 1.5 + 1.5 * group:
                 embed_done.append(group)
                 embed_pass(group)
         if stage == depth + 1:
-            complete.add(number)
-            try_loads()
-        credit = min(credit + 3.7 * PACE * (clock - last) , 4.0)
+            arrived.add(number)
+            block = units[number][:3]
+            if all(part in arrived for part in members[block]):
+                complete.add(block)
+                try_loads()
+        credit = min(credit + 3.7 * PACE * (clock - last), 4.0)
         last = clock
         while ready(clock) and credit > 0.0:
             credit -= run_step()
@@ -742,7 +782,6 @@
 
 def run_forward(arrays, picked, places, key_keep, dp, vocab):
     sizes = grid_of(dp, vocab)
-    devices = dp * vocab
     grid = tuple(sizes[axis] for axis in "zyxc")
     extra = []
     arrays = dict(arrays)
@@ -750,7 +789,7 @@
         extra = [lax.all_gather(arrays.pop("up"), ("dp", "vocab"), axis=1, tiled=True)]
     names = list(arrays)
     shapes = {name: arrays[name].shape[1:] for name in names}
-    units = plan_units(shapes, names, devices)
+    units = plan_units(shapes, names, sizes)
     depth = sum(sizes[axis] - 1 for axis in "zyx")
     anywhere, vmem = pl.BlockSpec(memory_space=pl.ANY), pl.BlockSpec(memory_space=pltpu.VMEM)
     f32, b16 = jnp.float32, jnp.bfloat16
@@ -790,10 +829,10 @@
             pltpu.VMEM((ROWS, 1024), b16),
             pltpu.VMEM((ROWS, 1024), f32),
             pltpu.VMEM((ROWS, 4096), b16),
-            pltpu.VMEM((4, 1024, 512), b16),
-            pltpu.VMEM((2, 4096, 256), b16),
-            dma((5,)),
-            dma((2,)),
+            pltpu.VMEM((6, 1024, 512), b16),
+            pltpu.VMEM((3, 4096, 256), b16),
+            dma((7,)),
+            dma((3,)),
             dma((32,)),
         ],
         compiler_params=pltpu.CompilerParams(
@@ -1059,7 +1098,7 @@
     grads = take(4)
     sums, core_send, core_recv = take(4), take(4), take(4)
     wide_send, wide_recv, mid_send, mid_recv, last_send, last_recv = (take(4) for _ in range(6))
-    small, small_slots, square_slots = take(1)[0], take(4), take(4)
+    small, small_slots, (late, owner_slots, group_slots) = take(1)[0], take(4), take(3)
     grad_low, grad_sum, grad_memory, grad_hidden, grad_att, packed = take(6)
     send_sem, recv_sem = take(2)
     here = position(sizes)
@@ -1137,7 +1176,22 @@
     down_copy(1).start()
     for place, index in ((6, 1), (4, 1), (0, 2), (1, 2), (0, 1), (1, 1), (5, 0), (6, 0), (4, 0), (0, 0), (1, 0)):
         fetch(place, index)
-    lines_barrier(here, sizes)
+    barrier = pltpu.get_barrier_semaphore()
+    owners, groups = sizes["x"] * sizes["c"], sizes["z"] * sizes["y"]
+    owner, group = here["x"] * sizes["c"] + here["c"], here["z"] * sizes["y"] + here["y"]
+
+    def owner_at(step):
+        other = (owner + step) % owners
+        return {"x": other // sizes["c"], "c": other % sizes["c"]}
+
+    def group_at(step):
+        other = (group + step) % groups
+        return {"z": other // sizes["y"], "y": other % sizes["y"]}
+
+    peers = [owner_at(step) for step in range(1, owners)] + [group_at(step) for step in range(1, groups)]
+    for peer in peers:
+        pl.semaphore_signal(barrier, inc=1, device_id=device_at(here, sizes, **peer), device_id_type=MESH_ID)
+    pl.semaphore_wait(barrier, len(peers))
 
     used, started = [0], []
 
@@ -1312,9 +1366,12 @@
             packed[rows, columns(2)] = low(dot_columns(chance_low, grad_out))
             return 0
 
-        lax.fori_loop(0, 8 * MICRO, body, 0, unroll=2)
-        if between is not None:
-            between()
+        if between is None:
+            lax.fori_loop(0, 8 * MICRO, body, 0, unroll=4)
+        else:
+            for seq, extra_work in enumerate(between):
+                lax.fori_loop(8 * seq, 8 * seq + 8, body, 0, unroll=4)
+                extra_work()
         for left in range(0, 3072, block):
 
             def second(tile, left=left):
@@ -1345,24 +1402,51 @@
     phase_core((0, 1))
     phase_last((2, 3))
     norm_back(grad_sum[...], 1)
-    attend_back(0, lambda: phase_wide((0, 1)))
+    chain = [share(small_slots[0], small[...], "c")]
+
+    def halfway():
+        phase_wide((0, 1))
+        chain.append(share(small_slots[1], total(small_slots[0], "c", chain[0]), "x"))
+
+    def after():
+        chain.append(share(small_slots[2], total(small_slots[1], "x", chain[1]), "y"))
+
+    attend_back(0, (halfway, after))
+    chain.append(share(small_slots[3], total(small_slots[2], "y", chain[2]), "z"))
+    phase_mid((0, 1))
     square = phase_end((2, 3))
-    phase_mid((0, 1))
     norm_back(grad_sum[...], 0)
-    copies = share(small_slots[0], small[...], "c")
     phase_last((0, 1))
-    copies = share(small_slots[1], total(small_slots[0], "c", copies), "x")
-    copies = share(small_slots[2], total(small_slots[1], "x", copies), "y")
-    copies = share(small_slots[3], total(small_slots[2], "y", copies), "z")
-    square = jnp.broadcast_to(square + phase_end((0, 1)), (8, 128))
-    for place, axis in enumerate("cxyz"):
-        parts = share(square_slots[place], square, axis)
-        if place == 0:
-            whole = total(small_slots[3], "z", copies)
-            small_out[...] = whole
-            norm_square = jnp.sum(whole[:14] * whole[:14], keepdims=True)
-        square = total(square_slots[place], axis, parts)
-    square_out[...] = square + norm_square
+    for row in range(2):
+        for place in range(8):
+            late[8 * row + place : 8 * row + place + 1, :] = small[
+                7 * row : 7 * row + 1, 128 * place : 128 * place + 128
+            ]
+    whole = total(small_slots[3], "z", chain[3])
+    small_out[...] = whole
+    norm_square = jnp.sum(whole[:14] * whole[:14], keepdims=True)
+    square = square + phase_end((0, 1))
+    late[16:24, :] = jnp.broadcast_to(square, (8, 128))
+
+    def gather_late(slots, mine_at, count, at, value):
+        slots[mine_at] = value
+        copies = [copy_to(slots.at[mine_at], slots.at[mine_at], **at(step)) for step in range(1, count)]
+        for copy in copies:
+            copy.wait_recv()
+        value = slots[0]
+        for index in range(1, count):
+            value = value + slots[index]
+        return value
+
+    value = gather_late(owner_slots, owner, owners, owner_at, late[...])
+    value = gather_late(group_slots, group, groups, group_at, value)
+    for row in range(2):
+        for place in range(8):
+            small_out[7 * row : 7 * row + 1, 128 * place : 128 * place + 128] = value[
+                8 * row + place : 8 * row + place + 1, :
+            ]
+    norm_square = norm_square + jnp.sum(value[:16] * value[:16], keepdims=True)
+    square_out[...] = value[16:24] + norm_square
     for copy in started:
         copy.wait_send()
 
@@ -1389,7 +1473,7 @@
             scratch += [pltpu.VMEM(lead[place % 2] + tail, b16) for place, tail in enumerate(tails)]
     scratch.append(pltpu.VMEM((16, 1024), f32))
     scratch += [pltpu.VMEM((sizes[axis], 16, 1024), f32) for axis in "cxyz"]
-    scratch += [pltpu.VMEM((sizes[axis], 8, 128), f32) for axis in "cxyz"]
+    scratch += [pltpu.VMEM(shape, f32) for shape in ((24, 128), (vocab, 24, 128), (dp, 24, 128))]
     scratch += [
         pltpu.VMEM((ROWS, 1024), b16),
         pltpu.VMEM((ROWS, 1024), f32),
@@ -1398,7 +1482,7 @@
         pltpu.VMEM((ROWS, 1024), b16),
         pltpu.VMEM((ROWS, 3072), b16),
     ]
-    links = 6 * (x + y + z + c)
+    links = 6 * (x + y + z + c) + dp + vocab
     scratch += [dma((links,)), dma((links,))]
     return pl.pallas_call(
         functools.partial(backward_kernel, sizes),

time: 486 us -> 458 us (0.942)
  Pallas kernels: 436 us -> 408 us
    pallas_call x1, Pallas kernels: 294 us -> 276 us  [run_forward(): pl.pallas_call(functools.partial(forward_kernel, sizes, units, names), ou...]
    pallas_call x1, Pallas kernels: 88.2 us -> 80.2 us  [run_backward(): pl.pallas_call(functools.partial(backward_kernel, sizes), out_shape=[jax....]
where the time goes in v5:
time: 458 us; the launch traced here: 450 us
  Pallas kernels  408 us (89%)
  local copies, waits for them, and re-layouts  25.5 us (6%)
  other arithmetic  13.9 us (3%)
    pallas_call x1, Pallas kernels, run_forward(): pl.pallas_call(functools.partial(forward_kernel, sizes, units, names), ou...  276 us
    pallas_call x1, Pallas kernels, run_backward(): pl.pallas_call(functools.partial(backward_kernel, sizes), out_shape=[jax....  80.2 us
    pallas_call x1, Pallas kernels, run_head(): pl.pallas_call(functools.partial(head_kernel, sizes), out_shape=[jax.Shap...  52.2 us
    gather x1, local copies, waits for them, and re-layouts, local(): jnp.take(vocab_table, jnp.clip(joined_ids, 0, rows_local - 1), axis=0)  17.4 us

profile of v5, /device:TPU:0, one launch (start us, length us, event | category | flops | bytes accessed | tf_op | source)
XLA Modules:
  0.0 450.4 jit_solution(11216670859020309270)
XLA Ops:
  0.6 0.7 dynamic_slice.15
  1.4 0.1 compare_convert_fusion
  1.5 0.6 broadcast_in_dim.69.refs_9_
  2.1 0.7 compare_and_fusion.1
  2.8 0.7 fusion.3
  3.6 17.4 %gather_fusion = bf16[2048,1024]{1,0:T(8,128)(2,1)} fusion(bf16[6400,1024]{1,0:T(8,128)(2,1)} %refs_3_.3, s32[2048]{0:T(1024)S(1)} %broadcast_clamp_fusion), kind=kCustom, calls=%fused_computation | custom fusion | bytes 8396800 | tf_op jit(solution)/shard_map/jit(_take)/gather | solution.py:1643
  20.9 0.0 copy-start.7
  21.0 4.0 select_select_fusion.refs_7_
  24.9 0.0 copy-done.2
  24.9 0.6 convert_element_type.29.refs_5_
  25.6 0.0 copy-done.1
  25.6 0.6 convert_element_type.30.refs_6_
  26.2 0.0 copy-done.13
  26.2 0.0 copy-done.11
  26.2 0.1 select_reduce_fusion.1
  26.3 0.1 copy.47
  26.4 0.0 copy-done.7
  26.4 0.1 copy.45
  26.5 0.1 pad.25.clone
  26.6 0.7 maximum_bitcast_fusion.refs_0_
  27.3 275.7 %shard_map.292 = (f32[1,4,2,2,2,32,128]{6,5,4,3,2,1,0:T(8,128)}, bf16[3,4,2,2,2,32,3072]{6,5,4,3,2,1,0:T(8,128)(2,1)}, bf16[3,4,2,2,2,32,1024]{6,5,4,3,2,1,0:T(8...) custom-call(f32[1,32,128]{2,1,0:T(8,128)} %maximum_bitcast_fusion.re, ...), custom_call_target="tpu_custom_call" | custom-call | tf_op jit(solution)/shard_map/pallas_call | solution.py:812
  303.0 0.9 slice_reduce_fusion
  304.0 0.2 select_reduce_fusion
  304.2 0.1 dynamic_slice.17
  304.2 0.1 dynamic_slice.16
  304.3 0.1 select_bitcast_fusion
  304.4 0.8 broadcast_in_dim.72.refs_2_
  305.1 0.0 copy-done.10
  305.2 1.0 broadcast_in_dim.71.refs_1_
  306.2 52.2 %shard_map.293 = (f32[256,1024]{1,0:T(8,128)}, f32[8,256]{1,0:T(8,128)}) custom-call(bf16[256,1024]{1,0:T(8,128)(2,1)} %get-tuple-element.35.refs_0_, s32[4,256,128]{2,1,0:T(8,128)} %broadcast_in_dim.71.refs_1_, f32[256,128]{1,0:T(8,128)} %broadcast_in_dim.72.refs_2_, bf16[6400,1024]{1,0:T(8,128)(2,1)} %refs_3_.3), custom_call_target="tpu_custom_call" | custom-call | tf_op jit(solution)/shard_map/pallas_call | solution.py:1048
  358.4 0.0 copy-done.12
  358.4 0.7 slice.20
  359.1 0.2 select_reduce_fusion.2
  359.3 0.1 fusion.4
  359.4 0.1 multiply_reduce_fusion
  359.5 0.6 pad.27.refs_2_
  360.1 0.0 copy-done
  360.1 0.8 copy.57
  360.9 0.0 copy-start.5
  360.9 0.0 copy-start.6
  360.9 80.2 %shard_map.294 = (f32[32,512]{1,0:T(8,128)}, f32[16,1024]{1,0:T(8,128)}, f32[32,512]{1,0:T(8,128)}, f32[16,1024]{1,0:T(8,128)}, f32[16,1024]{1,0:T(8,128)}, /*index=5*/f32[8,128]{1,0:T(8,128)}) custom-call(f32[256,1024]{1,0:T(8,128)} %get-tuple-element.37.refs_0_, f32[16,1024]{1,0:T(8,128)} %bitcast.30, f32[16,1024]{1,0:T(8,128)} %pad.27.refs_2_, ...), custom_call_target="tpu_custom_call" | custom-call | tf_op jit(solution)/shard_map/pallas_call | solution.py:1487
  441.2 1.2 slice.21
  443.1 0.0 copy-done.8
  443.1 0.0 copy-done.9
  443.1 1.4 multiply_subtract_fusion.2
  444.5 1.7 multiply_subtract_fusion
  446.2 1.7 multiply_subtract_fusion.1
  447.9 1.2 slice_bitcast_fusion
  (23 shorter events, 0.1 us)
Async XLA Ops:
  20.9 4.0 copy-start.2
  20.9 4.6 %copy-start.1 = (f32[2,16,1024]{2,1,0:T(8,128)S(1)}, f32[2,16,1024]{2,1,0:T(8,128)}, u32[]{:S(2)}) copy-start(f32[2,16,1024]{2,1,0:T(8,128)} %param.34) | copy-start | bytes 393220
  20.9 5.3 %copy-start.13 = (s32[8]{0:T(128)S(1)}, s32[8]{0:T(128)}, u32[]{:S(2)}) copy-start(s32[8]{0:T(128)} %param.25) | copy-start | bytes 100
  20.9 5.3 %copy-start.11 = (s32[8]{0:T(128)S(1)}, s32[8]{0:T(128)}, u32[]{:S(2)}) copy-start(s32[8]{0:T(128)} %param.26) | copy-start | bytes 100
  20.9 5.5 %copy-start.7 = (f32[14,32]{1,0:T(8,128)S(1)}, f32[14,32]{1,0:T(8,128)}, u32[]{:S(2)}) copy-start(f32[14,32]{1,0:T(8,128)} %param.35) | copy-start | bytes 5380
  24.9 280.2 %copy-start.10 = (s32[8,128]{1,0:T(8,128)S(1)}, s32[8,128]{1,0:T(8,128)}, u32[]{:S(2)}) copy-start(s32[8,128]{1,0:T(8,128)} %param.23) | copy-start | bytes 12292
  304.0 54.5 %copy-start.12 = (f32[4]{0:T(128)}, f32[4]{0:T(128)S(1)}, u32[]{:S(2)}) copy-start(f32[4]{0:T(128)S(1)} %slice_reduce_fusion) | copy-start | bytes 52
  306.2 53.9 %copy-start = (f32[1,4,2,2,2,32,128]{6,5,4,3,2,1,0:T(8,128)S(1)}, f32[1,4,2,2,2,32,128]{6,5,4,3,2,1,0:T(8,128)}, u32[]{:S(2)}) copy-start(f32[1,4,2,2,2,32,128]{6,5,4,3,2,1,0:T(8,128)} %get-tuple-element.36) | copy-start | bytes 1572868
  360.9 82.2 %copy-start.8 = (f32[14,32]{1,0:T(8,128)S(1)}, f32[14,32]{1,0:T(8,128)}, u32[]{:S(2)}) copy-start(f32[14,32]{1,0:T(8,128)} %param.41) | copy-start | bytes 5380
  360.9 82.2 %copy-start.9 = (f32[14,32]{1,0:T(8,128)S(1)}, f32[14,32]{1,0:T(8,128)}, u32[]{:S(2)}) copy-start(f32[14,32]{1,0:T(8,128)} %param.40) | copy-start | bytes 5380
  360.9 83.6 %copy-start.3 = (f32[2,16,1024]{2,1,0:T(8,128)S(1)}, f32[2,16,1024]{2,1,0:T(8,128)}, u32[]{:S(2)}) copy-start(f32[2,16,1024]{2,1,0:T(8,128)} %param.39) | copy-start | bytes 393220
  360.9 83.6 %copy-start.4 = (f32[2,16,1024]{2,1,0:T(8,128)S(1)}, f32[2,16,1024]{2,1,0:T(8,128)}, u32[]{:S(2)}) copy-start(f32[2,16,1024]{2,1,0:T(8,128)} %param.38) | copy-start | bytes 393220
  360.9 85.3 %copy-start.5 = (f32[2,32,512]{2,1,0:T(8,128)S(1)}, f32[2,32,512]{2,1,0:T(8,128)}, u32[]{:S(2)}) copy-start(f32[2,32,512]{2,1,0:T(8,128)} %param.37) | copy-start | bytes 393220
  360.9 85.3 %copy-start.6 = (f32[2,32,512]{2,1,0:T(8,128)S(1)}, f32[2,32,512]{2,1,0:T(8,128)}, u32[]{:S(2)}) copy-start(f32[2,32,512]{2,1,0:T(8,128)} %param.36) | copy-start | bytes 393220

commit v6 on v5

--- a/solution.py
+++ b/solution.py
@@ -228,11 +228,11 @@
     ("narrow", 1),
 )
 COLUMNS = {"norms": 128, "attn_in": 512, "attn_out": 512, "down": 512, "widen": 512, "up": 512, "narrow": 256}
-PARTS = {("narrow", 0): 2, ("narrow", 1): 4}
-LAG_Z = (2.5, 2.5, 2.5)
-LAG_LINE = (8.0, 3.5, 5.5)
-LAG_CORE = 2.75
-PACE = 0.5
+PARTS = {("narrow", 1): 2}
+LAG_Z = (3.0, 3.0, 3.0)
+LAG_LINE = (8.0, 5.0, 5.5)
+LAG_CORE = 3.0
+PACE = 0.7
 SETTLE = 0.8
 HEADS = 16
 LEN = 128
@@ -284,7 +284,7 @@
     for axis, _ in hops_of(order, sizes):
         found.append(found[-1] + (LAG_Z if axis == "z" else LAG_LINE)[order.index(axis)])
     found.append(found[-1] + LAG_CORE)
-    scale = min(1.0, 0.8 + unit[6] / 20.0)
+    scale = min(1.0, 0.6 + unit[6] / 20.0)
     return [unit[6] + scale * value for value in found]
 
 
@@ -357,7 +357,7 @@
 
     count = len(names)
     ins = dict(zip(names, take(count)))
-    picked, places, key_keep = take(3)
+    picked, places, key_keep, owned = take(4)
     extra_up = None if "up" in names else take(1)[0]
     outs = dict(zip(names, take(count)))
     saved_out = take(8)
@@ -506,7 +506,8 @@
     def embed_pass(group):
         embed_first(group).wait_recv()
         embed_local(group).wait()
-        embed_here[group] = embed_here[group] + embed_core[group]
+        here_keep, core_keep = (jnp.concatenate([owned[core, group]] * 8, -1) for core in range(2))
+        embed_here[group] = embed_here[group] * here_keep + embed_core[group] * core_keep
         for step in range(1, sizes["x"]):
             embed_second(group, step).start()
 
@@ -780,7 +781,7 @@
                     build(False).wait_send()
 
 
-def run_forward(arrays, picked, places, key_keep, dp, vocab):
+def run_forward(arrays, picked, places, key_keep, owned, dp, vocab):
     sizes = grid_of(dp, vocab)
     grid = tuple(sizes[axis] for axis in "zyxc")
     extra = []
@@ -812,7 +813,7 @@
     out = pl.pallas_call(
         functools.partial(forward_kernel, sizes, units, names),
         out_shape=out_shape,
-        in_specs=[anywhere] * (len(names) + 1) + [vmem] * (2 + len(extra)),
+        in_specs=[anywhere] * (len(names) + 1) + [vmem] * (3 + len(extra)),
         out_specs=[anywhere] * len(out_shape),
         scratch_shapes=[dma((n, 2 * depth)), dma((n, 2 * depth)), dma((n,)), dma((n,)), dma((n,))]
         + [pltpu.VMEM(shape, kind) for shape, kind in saved]
@@ -838,7 +839,7 @@
         compiler_params=pltpu.CompilerParams(
             collective_id=0, has_side_effects=True, vmem_limit_bytes=61 * 2**20
         ),
-    )(*[arrays[name] for name in names], picked, places, key_keep, *extra)
+    )(*[arrays[name] for name in names], picked, places, key_keep, owned, *extra)
     held = dict(zip(names, out[: len(names)]))
     if extra:
         held["up"] = extra[0]
@@ -1633,16 +1634,16 @@
     dp, groups = lax.axis_size("dp"), lax.axis_size("vocab")
     vocab_rank = lax.axis_index("vocab")
     rows_local, width = vocab_table.shape
-    joined_ids = (
-        jnp.stack([source_ids.reshape(groups, -1), target_in.reshape(groups, -1)], 1).reshape(-1)
-        - vocab_rank * rows_local
-    )
-    inside = (joined_ids >= 0) & (joined_ids < rows_local)
-    picked = jnp.where(
-        inside[:, None],
-        jnp.take(vocab_table, jnp.clip(joined_ids, 0, rows_local - 1), axis=0),
-        jnp.zeros((), jnp.bfloat16),
-    ).reshape(groups // 2, 2, 2, ROWS, width)
+    joined_ids = jnp.stack([source_ids.reshape(groups, -1), target_in.reshape(groups, -1)], 1)
+    local_ids = jnp.clip(joined_ids.reshape(-1) - vocab_rank * rows_local, 0, rows_local - 1)
+    picked = jnp.take(vocab_table, local_ids, axis=0, mode="clip").reshape(groups // 2, 2, 2, ROWS, width)
+    core = vocab_rank % 2
+    owner = lax.dynamic_index_in_dim(
+        joined_ids.reshape(groups // 2, 2, 2, ROWS) // rows_local, core, 1, keepdims=False
+    ).transpose(1, 0, 2)
+    twins = jnp.stack([vocab_rank, vocab_rank + 1 - 2 * core])
+    owned = (owner[None] == twins[:, None, None, None]).astype(jnp.bfloat16)
+    owned = jnp.broadcast_to(owned[..., None], owned.shape + (128,))
     task_hot = (task_ids[:, None] == jnp.arange(TASKS)[None, :]).astype(jnp.float32)
     group_counts = jnp.sum(task_hot * target_length[:, None].astype(jnp.float32), 0)
     own = vocab_rank * MICRO
@@ -1666,7 +1667,7 @@
         "down": low(adapt_down),
         "up": low(adapt_up),
     }
-    held, saved = run_forward(parts, picked, positions, key_keep, dp, groups)
+    held, saved = run_forward(parts, picked, positions, key_keep, owned, dp, groups)
     slab = held.pop("norms").reshape(dp, groups, -1, 128)
     task_counts = jnp.sum(slab[:, 0, :TASKS, 14], 0)
     seq_scale = jnp.sum(task_hot * (1.0 / (TASKS * task_counts))[None, :], 1)

time: 458 us -> 454 us (level)
  no operation moved by 1% of the time
where the time goes in v6:
time: 454 us; the launch traced here: 447 us
  Pallas kernels  406 us (89%)
  local copies, waits for them, and re-layouts  28.2 us (6%)
  other arithmetic  9.48 us (2%)
    pallas_call x1, Pallas kernels, run_forward(): pl.pallas_call(functools.partial(forward_kernel, sizes, units, names), ou...  275 us
    pallas_call x1, Pallas kernels, run_backward(): pl.pallas_call(functools.partial(backward_kernel, sizes), out_shape=[jax....  80.5 us
    pallas_call x1, Pallas kernels, run_head(): pl.pallas_call(functools.partial(head_kernel, sizes), out_shape=[jax.Shap...  51 us
    gather x1, local copies, waits for them, and re-layouts, local(): jnp.take(vocab_table, local_ids, axis=0, mode='clip')  17.5 us

profile of v6, /device:TPU:0, one launch (start us, length us, event | category | flops | bytes accessed | tf_op | source)
XLA Modules:
  0.0 446.7 jit_solution(3731456431317196530)
XLA Ops:
  0.7 0.7 stack.37
  1.4 0.7 stack.38
  2.1 0.1 pad_add_fusion
  2.2 0.1 compare_convert_fusion
  2.3 1.2 broadcast_in_dim.24.refs_10_
  3.4 0.7 dynamic_slice.19
  4.2 0.1 compare_convert_fusion.1
  4.2 0.6 broadcast_in_dim.23.refs_9_
  4.8 0.7 fusion.4
  5.6 0.0 copy-start.2
  5.6 0.0 copy-start.1
  5.6 0.0 copy-start.13
  5.6 0.0 copy-start.11
  5.6 0.0 copy-start.7
  5.6 17.5 %gather_fusion = bf16[2048,1024]{1,0:T(8,128)(2,1)} fusion(bf16[6400,1024]{1,0:T(8,128)(2,1)} %refs_3_.3, s32[2048]{0:T(1024)S(1)} %broadcast_clamp_fusion), kind=kCustom, calls=%fused_computation | custom fusion | bytes 8396800 | tf_op jit(solution)/shard_map/jit(_take)/gather | solution.py:1639
  23.1 0.0 copy-done.2
  23.1 0.6 convert_element_type.36.refs_5_
  23.8 0.6 convert_element_type.37.refs_6_
  24.4 0.0 copy-done.11
  24.4 0.1 select_reduce_fusion.1
  24.5 0.1 copy.43
  24.6 0.1 copy.41
  24.7 0.1 pad.25.clone
  24.8 0.7 maximum_bitcast_fusion.refs_0_
  25.5 274.6 %shard_map.292 = (f32[1,4,2,2,2,32,128]{6,5,4,3,2,1,0:T(8,128)}, bf16[3,4,2,2,2,32,3072]{6,5,4,3,2,1,0:T(8,128)(2,1)}, bf16[3,4,2,2,2,32,1024]{6,5,4,3,2,1,0:T(8...) custom-call(f32[1,32,128]{2,1,0:T(8,128)} %maximum_bitcast_fusion.re, ...), custom_call_target="tpu_custom_call" | custom-call | tf_op jit(solution)/shard_map/pallas_call | solution.py:813
  300.1 1.1 slice_reduce_fusion
  301.2 0.2 select_reduce_fusion
  301.4 0.1 dynamic_slice.22
  301.5 0.1 dynamic_slice.21
  301.6 0.1 select_bitcast_fusion
  301.7 0.8 broadcast_in_dim.27.refs_2_
  302.4 1.0 broadcast_in_dim.26.refs_1_
  303.4 51.0 %shard_map.293 = (f32[256,1024]{1,0:T(8,128)}, f32[8,256]{1,0:T(8,128)}) custom-call(bf16[256,1024]{1,0:T(8,128)(2,1)} %get-tuple-element.35.refs_0_, s32[4,256,128]{2,1,0:T(8,128)} %broadcast_in_dim.26.refs_1_, f32[256,128]{1,0:T(8,128)} %broadcast_in_dim.27.refs_2_, bf16[6400,1024]{1,0:T(8,128)(2,1)} %refs_3_.3), custom_call_target="tpu_custom_call" | custom-call | tf_op jit(solution)/shard_map/pallas_call | solution.py:1049
  354.5 0.0 copy-done.12
  354.5 0.7 slice.20
  355.2 0.2 select_reduce_fusion.2
  355.4 0.1 fusion.5
  355.5 0.1 multiply_reduce_fusion
  355.6 0.6 pad.27.refs_2_
  356.2 0.8 copy.52
  357.0 0.0 copy-start.5
  357.0 0.0 copy-start.6
  357.0 80.5 %shard_map.294 = (f32[32,512]{1,0:T(8,128)}, f32[16,1024]{1,0:T(8,128)}, f32[32,512]{1,0:T(8,128)}, f32[16,1024]{1,0:T(8,128)}, f32[16,1024]{1,0:T(8,128)}, /*index=5*/f32[8,128]{1,0:T(8,128)}) custom-call(f32[256,1024]{1,0:T(8,128)} %get-tuple-element.37.refs_0_, f32[16,1024]{1,0:T(8,128)} %bitcast.37, f32[16,1024]{1,0:T(8,128)} %pad.27.refs_2_, ...), custom_call_target="tpu_custom_call" | custom-call | tf_op jit(solution)/shard_map/pallas_call | solution.py:1488
  437.5 1.2 slice.21
  439.5 1.4 multiply_subtract_fusion.2
  440.9 1.7 multiply_subtract_fusion
  442.5 1.7 multiply_subtract_fusion.1
  444.2 1.2 slice_bitcast_fusion
  (29 shorter events, 0.1 us)
Async XLA Ops:
  5.6 17.6 %copy-start.2 = (f32[2,32,512]{2,1,0:T(8,128)S(1)}, f32[2,32,512]{2,1,0:T(8,128)}, u32[]{:S(2)}) copy-start(f32[2,32,512]{2,1,0:T(8,128)} %param.33) | copy-start | bytes 393220
  5.6 18.2 %copy-start.1 = (f32[2,16,1024]{2,1,0:T(8,128)S(1)}, f32[2,16,1024]{2,1,0:T(8,128)}, u32[]{:S(2)}) copy-start(f32[2,16,1024]{2,1,0:T(8,128)} %param.34) | copy-start | bytes 393220
  5.6 18.8 %copy-start.13 = (s32[8]{0:T(128)S(1)}, s32[8]{0:T(128)}, u32[]{:S(2)}) copy-start(s32[8]{0:T(128)} %param.25) | copy-start | bytes 100
  5.6 18.8 %copy-start.11 = (s32[8]{0:T(128)S(1)}, s32[8]{0:T(128)}, u32[]{:S(2)}) copy-start(s32[8]{0:T(128)} %param.26) | copy-start | bytes 100
  5.6 19.0 %copy-start.7 = (f32[14,32]{1,0:T(8,128)S(1)}, f32[14,32]{1,0:T(8,128)}, u32[]{:S(2)}) copy-start(f32[14,32]{1,0:T(8,128)} %param.35) | copy-start | bytes 5380
  23.1 279.3 %copy-start.10 = (s32[8,128]{1,0:T(8,128)S(1)}, s32[8,128]{1,0:T(8,128)}, u32[]{:S(2)}) copy-start(s32[8,128]{1,0:T(8,128)} %param.23) | copy-start | bytes 12292
  301.2 53.3 %copy-start.12 = (f32[4]{0:T(128)}, f32[4]{0:T(128)S(1)}, u32[]{:S(2)}) copy-start(f32[4]{0:T(128)S(1)} %slice_reduce_fusion) | copy-start | bytes 52
  303.4 52.8 %copy-start = (f32[1,4,2,2,2,32,128]{6,5,4,3,2,1,0:T(8,128)S(1)}, f32[1,4,2,2,2,32,128]{6,5,4,3,2,1,0:T(8,128)}, u32[]{:S(2)}) copy-start(f32[1,4,2,2,2,32,128]{6,5,4,3,2,1,0:T(8,128)} %get-tuple-element.36) | copy-start | bytes 1572868
  357.0 82.4 %copy-start.8 = (f32[14,32]{1,0:T(8,128)S(1)}, f32[14,32]{1,0:T(8,128)}, u32[]{:S(2)}) copy-start(f32[14,32]{1,0:T(8,128)} %param.41) | copy-start | bytes 5380
  357.0 82.4 %copy-start.9 = (f32[14,32]{1,0:T(8,128)S(1)}, f32[14,32]{1,0:T(8,128)}, u32[]{:S(2)}) copy-start(f32[14,32]{1,0:T(8,128)} %param.40) | copy-start | bytes 5380
  357.0 83.9 %copy-start.3 = (f32[2,16,1024]{2,1,0:T(8,128)S(1)}, f32[2,16,1024]{2,1,0:T(8,128)}, u32[]{:S(2)}) copy-start(f32[2,16,1024]{2,1,0:T(8,128)} %param.39) | copy-start | bytes 393220
  357.0 83.9 %copy-start.4 = (f32[2,16,1024]{2,1,0:T(8,128)S(1)}, f32[2,16,1024]{2,1,0:T(8,128)}, u32[]{:S(2)}) copy-start(f32[2,16,1024]{2,1,0:T(8,128)} %param.38) | copy-start | bytes 393220
  357.0 85.5 %copy-start.5 = (f32[2,32,512]{2,1,0:T(8,128)S(1)}, f32[2,32,512]{2,1,0:T(8,128)}, u32[]{:S(2)}) copy-start(f32[2,32,512]{2,1,0:T(8,128)} %param.37) | copy-start | bytes 393220
  357.0 85.5 %copy-start.6 = (f32[2,32,512]{2,1,0:T(8,128)S(1)}, f32[2,32,512]{2,1,0:T(8,128)}, u32[]{:S(2)}) copy-start(f32[2,32,512]{2,1,0:T(8,128)} %param.36) | copy-start | bytes 393220
